TPU v7x, 256 devices: a whole 4x4x8 slice. The times are simulated.
256 devices in a mesh: span: 32 (over z, x), gx: 2 (over core), gy: 4 (over y).
Axes of the slice: x: 4, y: 4, z: 8, core: 2. Of those that a mesh axis runs over, the one named last changes fastest.
Arguments:
- flow_state: float32 [8, 8, 256, 320], P('gx', 'gy', 'span'), may hold values from -6 to 6
- source_term: float32 [8, 8, 256, 320], P('gx', 'gy', 'span'), may hold values from -6 to 6
- pseudo_time: float32 [8, 8, 256, 320], P('gx', 'gy', 'span'), may hold values from 1 to 4
- volume_jacobian: float32 [8, 8, 256, 3, 5, 5], P('gx', 'gy', 'span'), may hold values from -1.8 to 1.8
- side_jacobian: float32 [8, 8, 256, 4, 5, 5], P('gx', 'gy', 'span'), may hold values from -1.2 to 1.2
- span_jacobian: float32 [8, 8, 256, 2, 5, 5], P('gx', 'gy', 'span'), may hold values from -0.06 to 0.17
- line_inverse: float32 [8, 8, 320, 320], P('gx', 'gy'), may hold values from -0.02 to 1.02
- mirror_face: int32 [8, 8, 256, 4], P('gx', 'gy', 'span'), may hold values from 0 to 1
- edge_flip: int32 [8, 8, 256, 4], P('gx', 'gy', 'span'), may hold values from 0 to 1
Outputs:
- updated_state: float32 [8, 8, 256, 320], P('gx', 'gy', 'span')
- residual: float32 [8, 8, 256, 320], P('gx', 'gy', 'span')
All inputs are finite; a program needn't handle non-finite values.
Results may differ from a plain program's by a relative error of at most 0.0003.
Values sent between devices are 32-bit elements; how exact they have to be, the bound alone decides.
No kernel may reach another device: no remote copies, remote signals or barrier semaphores. Data moves between devices by JAX's collectives and lax.ppermute only.
A program may use at most 128 MiB of HBM per device.

v0:
```python
import jax
import jax.numpy as jnp
import numpy as np
from jax import lax
from jax.sharding import PartitionSpec as P

LIFT = 6.0
HIGHEST = lax.Precision.HIGHEST


def shifted(block, axis, distance):
    devices = range(lax.axis_size(axis))
    route = [(i - distance, i) for i in devices if i - distance in devices]
    return lax.ppermute(block, axis, route)


def padded_2(cells, sides, width):
    for axis, dim in sides:
        count = lax.axis_size(axis)
        ends = count - 1
        head = lax.slice_in_dim(cells, 0, width, axis=dim)
        tail = lax.slice_in_dim(cells, cells.shape[dim] - width, cells.shape[dim], axis=dim)
        cells = jnp.concatenate(
            [
                lax.ppermute(tail, axis, [(i, (i + 1) % count) for i in range(ends)]),
                cells,
                lax.ppermute(head, axis, [((i + 1) % count, i) for i in range(ends)]),
            ],
            axis=dim,
        )
    return cells


def from_behind(value, axis, steps):
    count = lax.axis_size(axis)
    pairs = [(source, (source + steps) % count) for source in range(count)]
    return lax.ppermute(value, axis, pairs)


def gll_derivative():
    points = np.array([-1.0, -1.0 / np.sqrt(5.0), 1.0 / np.sqrt(5.0), 1.0])
    matrix = np.zeros((4, 4))
    for target in range(4):
        for source in range(4):
            if target != source:
                numerator = 1.0
                for other_node in range(4):
                    if other_node != source and other_node != target:
                        numerator = numerator * (points[target] - points[other_node])
                denominator = 1.0
                for other_node in range(4):
                    if other_node != source:
                        denominator = denominator * (points[source] - points[other_node])
                matrix[target, source] = numerator / denominator
    for target in range(4):
        matrix[target, target] = -np.sum(matrix[target])
    return jnp.asarray(matrix, dtype=jnp.float32)


def split_nodes(field):
    return field.reshape(field.shape[:3] + (4, 4, 4, 5))


def side_traces(nodes):
    return jnp.stack(
        [nodes[:, :, :, 0], nodes[:, :, :, 3], nodes[:, :, :, :, 0], nodes[:, :, :, :, 3]], axis=3
    )


def volume_term(nodes, volume_jacobian):
    derivative = gll_derivative()
    fluxes = jnp.einsum("xyzdwv,xyzabcv->xyzdabcw", volume_jacobian, nodes, precision=HIGHEST)
    along_first = jnp.einsum(
        "pa,xyzabcw->xyzpbcw", derivative, fluxes[:, :, :, 0], precision=HIGHEST
    )
    along_second = jnp.einsum(
        "pb,xyzabcw->xyzapcw", derivative, fluxes[:, :, :, 1], precision=HIGHEST
    )
    along_span = jnp.einsum(
        "pc,xyzabcw->xyzabpw", derivative, fluxes[:, :, :, 2], precision=HIGHEST
    )
    return along_first + along_second + along_span


def face_coupling(own_sides, pairs, mirror_face, edge_flip, side_jacobian):
    lifted_faces = []
    for face_index in range(4):
        candidates = pairs[face_index]
        chosen = jnp.where(
            mirror_face[:, :, :, face_index, None, None, None] == 1,
            candidates[:, :, :, 1],
            candidates[:, :, :, 0],
        )
        mirrored_edge = jnp.flip(chosen, axis=3)
        chosen = jnp.where(
            edge_flip[:, :, :, face_index, None, None, None] == 1, mirrored_edge, chosen
        )
        jump = chosen - own_sides[:, :, :, face_index]
        lifted_faces.append(
            LIFT
            * jnp.einsum(
                "xyzwv,xyzecv->xyzecw", side_jacobian[:, :, :, face_index], jump, precision=HIGHEST
            )
        )
    return lifted_faces


def apply_residual(
    nodes,
    source_term,
    pseudo_time,
    volume_jacobian,
    side_jacobian,
    span_jacobian,
    mirror_face,
    edge_flip,
    pairs,
    lower_top,
    upper_bottom,
):
    lifted_faces = face_coupling(side_traces(nodes), pairs, mirror_face, edge_flip, side_jacobian)
    bottom_layer = nodes[:, :, :, :, :, 0]
    top_layer = nodes[:, :, :, :, :, 3]
    lower_term = LIFT * jnp.einsum(
        "xyzwv,xyzabv->xyzabw",
        span_jacobian[:, :, :, 0],
        lower_top - bottom_layer,
        precision=HIGHEST,
    )
    upper_term = LIFT * jnp.einsum(
        "xyzwv,xyzabv->xyzabw",
        span_jacobian[:, :, :, 1],
        upper_bottom - top_layer,
        precision=HIGHEST,
    )
    lifted = jnp.zeros_like(nodes)
    lifted = lifted.at[:, :, :, 0].add(lifted_faces[0])
    lifted = lifted.at[:, :, :, 3].add(lifted_faces[1])
    lifted = lifted.at[:, :, :, :, 0].add(lifted_faces[2])
    lifted = lifted.at[:, :, :, :, 3].add(lifted_faces[3])
    lifted = lifted.at[:, :, :, :, :, 0].add(lower_term)
    lifted = lifted.at[:, :, :, :, :, 3].add(upper_term)
    operator_value = volume_term(nodes, volume_jacobian) - lifted
    field = nodes.reshape(source_term.shape)
    return source_term - (pseudo_time * field + operator_value.reshape(source_term.shape))


def couple(jacobian, trace_value):
    line_count = trace_value.shape[0]
    return LIFT * jnp.einsum(
        "lwv,lpv->lpw", jacobian, trace_value.reshape(line_count, 16, 5), precision=HIGHEST
    ).reshape(line_count, 80)


def layer_traces(stacked, height):
    span_count, line_count = stacked.shape[:2]
    return stacked.reshape(span_count, line_count, 4, 4, 4, 5)[:, :, :, :, height].reshape(
        span_count, line_count, 80
    )


def trace_chain(initial_trace, direct_traces, coupling_block, jacobians, backward):

    def advance(running, inputs):
        direct_now, jacobian = inputs
        coupled = couple(jacobian, running)
        return (
            direct_now + jnp.einsum("lij,lj->li", coupling_block, coupled, precision=HIGHEST),
            coupled,
        )

    return lax.scan(advance, initial_trace, (direct_traces, jacobians), reverse=backward)


def compose(coupling_block, jacobians, backward):
    line_count = coupling_block.shape[0]

    def extend(running, jacobian):
        coupled = LIFT * jnp.einsum(
            "lwv,lpvq->lpwq", jacobian, running.reshape(line_count, 16, 5, 80), precision=HIGHEST
        )
        return (
            jnp.einsum(
                "lij,ljq->liq",
                coupling_block,
                coupled.reshape(line_count, 80, 80),
                precision=HIGHEST,
            ),
            None,
        )

    initial = jnp.broadcast_to(jnp.eye(80, dtype=jnp.float32), (line_count, 80, 80))
    return lax.scan(extend, initial, jacobians, reverse=backward)[0]


def hand_off(line_map, local_start, backward):
    line_count = local_start.shape[0]
    zero_trace = jnp.zeros((line_count, 80), jnp.float32)
    if backward:

        def backward_turn(turn_index, incoming):
            outgoing = jnp.einsum("lij,lj->li", line_map, incoming, precision=HIGHEST) + local_start
            return shifted(outgoing, "span", -1)

        return lax.fori_loop(0, lax.axis_size("span") - 1, backward_turn, zero_trace)

    def forward_turn(turn_index, incoming):
        outgoing = jnp.einsum("lij,lj->li", line_map, incoming, precision=HIGHEST) + local_start
        return shifted(outgoing, "span", 1)

    return lax.fori_loop(0, lax.axis_size("span") - 1, forward_turn, zero_trace)


def on_device(
    flow_state,
    source_term,
    pseudo_time,
    volume_jacobian,
    side_jacobian,
    span_jacobian,
    line_inverse,
    mirror_face,
    edge_flip,
):
    first_count, second_count, span_count = flow_state.shape[:3]
    nodes = split_nodes(flow_state)
    padded = padded_2(flow_state, (("gx", 0), ("gy", 1)), 1)
    beside_all = side_traces(split_nodes(padded))
    pairs = [
        beside_all[0:first_count, 1 : second_count + 1, :, 0:2],
        beside_all[2 : first_count + 2, 1 : second_count + 1, :, 0:2],
        beside_all[1 : first_count + 1, 0:second_count, :, 2:4],
        beside_all[1 : first_count + 1, 2 : second_count + 2, :, 2:4],
    ]
    top_layer = nodes[:, :, :, :, :, 3]
    bottom_layer = nodes[:, :, :, :, :, 0]
    below_top = from_behind(top_layer[:, :, span_count - 1], "span", 1)
    above_bottom = from_behind(bottom_layer[:, :, 0], "span", -1)
    lower_top = jnp.concatenate([below_top[:, :, None], top_layer[:, :, : span_count - 1]], axis=2)
    upper_bottom = jnp.concatenate([bottom_layer[:, :, 1:], above_bottom[:, :, None]], axis=2)
    residual = apply_residual(
        nodes,
        source_term,
        pseudo_time,
        volume_jacobian,
        side_jacobian,
        span_jacobian,
        mirror_face,
        edge_flip,
        pairs,
        lower_top,
        upper_bottom,
    )
    line_count = first_count * second_count
    inverse = line_inverse.reshape(line_count, 320, 320)
    lines = residual.reshape(line_count, span_count, 320)
    lower_jac = (
        span_jacobian[:, :, :, 0].reshape(line_count, span_count, 5, 5).transpose(1, 0, 2, 3)
    )
    upper_jac = (
        span_jacobian[:, :, :, 1].reshape(line_count, span_count, 5, 5).transpose(1, 0, 2, 3)
    )
    row_layers = inverse.reshape(line_count, 4, 4, 4, 5, 320)
    top_rows = row_layers[:, :, :, 3].reshape(line_count, 80, 4, 4, 4, 5)
    bottom_rows = row_layers[:, :, :, 0].reshape(line_count, 80, 4, 4, 4, 5)
    top_from_bottom = top_rows[:, :, :, :, 0].reshape(line_count, 80, 80)
    bottom_from_top = bottom_rows[:, :, :, :, 3].reshape(line_count, 80, 80)
    column_layers = inverse.reshape(line_count, 320, 4, 4, 4, 5)
    bottom_columns = column_layers[:, :, :, :, 0].reshape(line_count, 320, 80)
    top_columns = column_layers[:, :, :, :, 3].reshape(line_count, 320, 80)
    zero_trace = jnp.zeros((line_count, 80), jnp.float32)
    direct = jnp.einsum("lij,lsj->sli", inverse, lines, precision=HIGHEST)
    direct_top = layer_traces(direct, 3)
    forward_map = compose(top_from_bottom, lower_jac, False)
    forward_start = trace_chain(zero_trace, direct_top, top_from_bottom, lower_jac, False)[0]
    incoming_below = hand_off(forward_map, forward_start, False)
    coupled_below = trace_chain(incoming_below, direct_top, top_from_bottom, lower_jac, False)[1]
    solved = direct + jnp.einsum("lin,sln->sli", bottom_columns, coupled_below, precision=HIGHEST)
    solved_bottom = layer_traces(solved, 0)
    backward_map = compose(bottom_from_top, upper_jac, True)
    backward_start = trace_chain(zero_trace, solved_bottom, bottom_from_top, upper_jac, True)[0]
    incoming_above = hand_off(backward_map, backward_start, True)
    coupled_above = trace_chain(incoming_above, solved_bottom, bottom_from_top, upper_jac, True)[1]
    correction = solved + jnp.einsum("lin,sln->sli", top_columns, coupled_above, precision=HIGHEST)
    updated_state = flow_state + correction.transpose(1, 0, 2).reshape(flow_state.shape)
    return (updated_state, residual)


def solution(mesh):
    placed = (
        P("gx", "gy", "span", None),
        P("gx", "gy", "span", None),
        P("gx", "gy", "span", None),
        P("gx", "gy", "span", None, None, None),
        P("gx", "gy", "span", None, None, None),
        P("gx", "gy", "span", None, None, None),
        P("gx", "gy", None, None),
        P("gx", "gy", "span", None),
        P("gx", "gy", "span", None),
    )
    return jax.shard_map(
        on_device,
        mesh=mesh,
        in_specs=placed,
        out_specs=(P("gx", "gy", "span", None), P("gx", "gy", "span", None)),
        check_vma=False,
    )
```

profile of v0, /device:TPU:118, one launch (start us, length us, event | category | flops | bytes accessed | tf_op | source)
XLA Modules:
  0.0 992.7 jit_solution(1989075879828023747)
XLA Ops:
  25.9 7.9 copy.253
  40.6 22.1 %convolution_bitcast_fusion.2 = f32[4,2,8,3,4,4,4,5]{7,6,3,5,4,2,1,0:T(4,128)S(1)} fusion(f32[4,2,8,3,5,5,1,1]{5,4,3,7,6,2,1,0:T(8,128)} %copy.284, f32[4,2,8,4,4,4,5,1]{6,5,4,3,2,1,0,7:T(4,128)S(1)} %copy-done.3), kind=kOutput, calls=%fused_computation.42 | convolution fusion | flops 3686400 | bytes 346880 | tf_op jit(solution)/shard_map/xyzdwv,xyzabcv->xyzdabcw/dot_general | solution.py:72
  89.3 28.5 %reshape_squeeze.31 = f32[8,80,4,4,4,5]{5,4,3,2,0,1:T(4,128)} reshape(f32[8,4,4,1,5,320]{5,0,4,3,2,1:T(8,128)S(1)} %get-tuple-element.720) | data formatting | bytes 1638400 | tf_op jit(solution)/shard_map/reshape;squeeze | solution.py:264
  117.8 10.5 %slice.511 = f32[8,80,4,4,1,5]{5,4,3,2,0,1:T(1,128)} slice(f32[8,80,4,4,4,5]{5,4,3,2,0,1:T(4,128)} %reshape_squeeze.31), slice={[0:8], [0:80], [0:4], [0:4], [0:1], [0:5]} | slice | bytes 409600 | tf_op jit(solution)/shard_map/slice | solution.py:266
  128.3 9.3 copy.247
  137.9 13.8 %while.104 = (s32[]{:T(128)}, f32[8,80,80]{1,2,0:T(8,128)S(1)}, f32[8,8,5,5]{3,2,1,0:T(8,128)S(1)}, f32[8,80,80]{2,1,0:T(8,128)S(1)}, s32[]{:T(128)}) while((s32[]{:T(128)}, f32[8,80,80]{1,2,0:T(8,128)S(1)}, f32[8,8,5,5]{3,2,1,0:T(8,128)S(1)}, f32[8,80,80]{2,1,0:T(8,128)S(1)}, s32[]{:T(128)}) %tuple.269), condition=%wide.region_1.2_spmd, body=%wide.region_0.1_spmd.sunk | while | flops 52275200 | bytes 1998913 | solution.py:193
  161.1 29.4 %reshape_squeeze.36 = f32[8,80,4,4,4,5]{5,4,3,2,0,1:T(4,128)} reshape(f32[8,4,4,1,5,320]{5,0,4,3,2,1:T(8,128)} %get-tuple-element.721) | data formatting | bytes 1638400 | tf_op jit(solution)/shard_map/reshape;squeeze | solution.py:265
  190.5 11.1 %slice.515 = f32[8,80,4,4,1,5]{5,4,3,2,0,1:T(1,128)} slice(f32[8,80,4,4,4,5]{5,4,3,2,0,1:T(4,128)} %reshape_squeeze.36), slice={[0:8], [0:80], [0:4], [0:4], [3:4], [0:5]} | slice | bytes 409600 | tf_op jit(solution)/shard_map/slice | solution.py:267
  201.6 9.3 copy.257
  211.2 13.8 %while.107 = (s32[]{:T(128)}, f32[8,80,80]{1,2,0:T(8,128)S(1)}, f32[8,8,5,5]{3,2,1,0:T(8,128)S(1)}, f32[8,80,80]{2,1,0:T(8,128)S(1)}, s32[]{:T(128)}, /*index=5*/s32[]{:T(128)}) while((s32[]{:T(128)}, f32[8,80,80]{1,2,0:T(8,128)S(1)}, f32[8,8,5,5]{3,2,1,0:T(8,128)S(1)}, f32[8,80,80]{2,1,0:T(8,128)S(1)}, s32[]{:T(128)}, ...), condition=%wide.region_9.10_spmd, body=%wide.region_8.9_spmd.sunk | while | flops 52275200 | bytes 1998933 | solution.py:193
  261.4 9.7 reshape.502
  331.7 15.5 %while.110 = (s32[]{:T(128)}, f32[8,80]{1,0:T(8,128)S(1)}, f32[8,8,80]{2,1,0:T(8,128)S(1)}, f32[8,8,5,5]{3,2,1,0:T(8,128)}, f32[8,80,80]{2,1,0:T(8,128)S(1)}, /*index=5*/s32[]{:T(128)}, s32[]{:T(128)}) while((s32[]{:T(128)}, f32[8,80]{1,0:T(8,128)S(1)}, f32[8,8,80]{2,1,0:T(8,128)S(1)}, f32[8,8,5,5]{3,2,1,0:T(8,128)}, ...), condition=%wide.region_3.4_spmd.clone, body=%wide.region_2.3_spmd.clone.sunk | while | flops 654723 | bytes 276571 | solution.py:172
  347.3 292.6 %while.105 = (s32[]{:T(128)}, f32[8,80]{1,0:T(8,128)S(1)}, f32[8,80,80]{2,1,0:T(8,128)S(1)}, f32[8,80]{1,0:T(8,128)S(1)}, s32[]{:T(128)}) while((s32[]{:T(128)}, f32[8,80]{1,0:T(8,128)S(1)}, f32[8,80,80]{2,1,0:T(8,128)S(1)}, f32[8,80]{1,0:T(8,128)S(1)}, s32[]{:T(128)}) %tuple.247), condition=%wide.region_5.6_spmd, body=%wide.region_4.5_spmd.sunk | while | flops 615042 | bytes 227941 | solution.py:211
  347.9 7.3 collective-permute-start
  357.1 7.5 collective-permute-start
  366.6 7.5 collective-permute-start
  376.0 7.5 collective-permute-start
  385.4 7.5 collective-permute-start
  394.9 7.5 collective-permute-start
  404.3 7.5 collective-permute-start
  413.8 7.5 collective-permute-start
  423.2 7.5 collective-permute-start
  432.7 7.5 collective-permute-start
  442.1 7.5 collective-permute-start
  451.6 7.5 collective-permute-start
  461.0 7.5 collective-permute-start
  470.5 7.5 collective-permute-start
  479.9 7.5 collective-permute-start
  489.4 7.5 collective-permute-start
  498.8 7.5 collective-permute-start
  508.3 7.5 collective-permute-start
  517.7 7.5 collective-permute-start
  527.2 7.5 collective-permute-start
  536.6 7.5 collective-permute-start
  546.0 7.5 collective-permute-start
  555.5 7.5 collective-permute-start
  564.9 7.5 collective-permute-start
  574.4 7.5 collective-permute-start
  583.8 7.5 collective-permute-start
  593.3 7.5 collective-permute-start
  602.7 7.5 collective-permute-start
  612.2 7.5 collective-permute-start
  621.6 7.5 collective-permute-start
  631.1 7.5 collective-permute-start
  639.9 16.9 %while.106 = (s32[]{:T(128)}, f32[8,80]{1,0:T(8,128)S(1)}, f32[8,8,80]{2,0,1:T(8,128)S(1)}, f32[8,8,80]{2,1,0:T(8,128)S(1)}, f32[8,8,5,5]{3,2,1,0:T(8,128)}, /*index=5*/f32[8,80,80]{2,1,0:T(8,128)S(1)}, s32[]{:T(128)}, s32[]{:T(128)}) while((s32[]{:T(128)}, f32[8,80]{1,0:T(8,128)S(1)}, f32[8,8,80]{2,0,1:T(8,128)S(1)}, ...), condition=%wide.region_7.8_spmd, body=%wide.region_6.7_spmd.sunk | while | flops 654082 | bytes 281693 | solution.py:172
  665.4 15.6 %while.111 = (s32[]{:T(128)}, f32[8,80]{1,0:T(8,128)S(1)}, f32[8,8,80]{2,1,0:T(8,128)S(1)}, f32[8,8,5,5]{3,2,1,0:T(8,128)}, f32[8,80,80]{2,1,0:T(8,128)S(1)}, /*index=5*/s32[]{:T(128)}, s32[]{:T(128)}, s32[]{:T(128)}) while((s32[]{:T(128)}, f32[8,80]{1,0:T(8,128)S(1)}, f32[8,8,80]{2,1,0:T(8,128)S(1)}, ...), condition=%wide.region_11.12_spmd.clone, body=%wide.region_10.11_spmd.clone.sunk | while | flops 654724 | bytes 276083 | solution.py:172
  681.0 293.2 %while.108 = (s32[]{:T(128)}, f32[8,80]{1,0:T(8,128)S(1)}, f32[8,80,80]{2,1,0:T(8,128)S(1)}, f32[8,80]{1,0:T(8,128)S(1)}, s32[]{:T(128)}) while((s32[]{:T(128)}, f32[8,80]{1,0:T(8,128)S(1)}, f32[8,80,80]{2,1,0:T(8,128)S(1)}, f32[8,80]{1,0:T(8,128)S(1)}, s32[]{:T(128)}) %tuple.256), condition=%wide.region_13.14_spmd, body=%wide.region_12.13_spmd.sunk | while | flops 615042 | bytes 227941 | solution.py:205
  974.1 16.7 %while.109 = (s32[]{:T(128)}, f32[8,80]{1,0:T(8,128)S(1)}, f32[8,8,80]{2,0,1:T(8,128)S(1)}, f32[8,8,80]{2,1,0:T(8,128)S(1)}, f32[8,8,5,5]{3,2,1,0:T(8,128)}, /*i...) while((s32[]{:T(128)}, f32[8,80]{1,0:T(8,128)S(1)}, f32[8,8,80]{2,0,1:T(8,128)S(1)}, ...), condition=%wide.region_15.16_spmd, body=%wide.region_14.15_spmd.sunk | while | flops 654083 | bytes 281205 | solution.py:172
  (724 shorter events, 617.5 us)
Async XLA Ops:
  2.0 247.0 %collective-permute-start.2 = (f32[1,2,8,320]{3,2,1,0:T(8,128)}, f32[1,2,8,320]{3,2,1,0:T(8,128)}, u32[]{:S(2)}, u32[]{:S(2)}) collective-permute-start(f32[1,2,8,320]{3,2,1,0:T(8,128)} %get-tuple-element.739), channel_id=1, source_target_pairs={{0,4},{1,5},{2,6},{3,7},{8,12},{9,13},{10,14},{11,15},{16,20},{17,... | collective-permute-start | bytes 61448 | tf_op jit(solution)/shard_map/ppermute | solution.py:25
  4.3 245.4 %collective-permute-start.3 = (f32[1,2,8,320]{3,2,1,0:T(8,128)}, f32[1,2,8,320]{3,2,1,0:T(8,128)S(1)}, u32[]{:S(2)}, u32[]{:S(2)}) collective-permute-start(f32[1,2,8,320]{3,2,1,0:T(8,128)} %get-tuple-element.738), channel_id=1, source_target_pairs={{4,0},{5,1},{6,2},{7,3},{12,8},{13,9},{14,10},{15,11},{20,16},{21,... | collective-permute-start | bytes 61448 | tf_op jit(solution)/shard_map/ppermute | solution.py:27
  11.0 235.5 %collective-permute-start.6 = (f32[4,2,4,4,5]{4,3,2,1,0:T(4,128)}, f32[4,2,4,4,5]{4,3,2,1,0:T(4,128)}, u32[]{:S(2)}, u32[]{:S(2)}) collective-permute-start(f32[4,2,4,4,5]{4,3,2,1,0:T(4,128)} %slice_bitcast_fusion.20), channel_id=1, source_target_pairs={{0,8},{8,16},{16,24},{24,32},{32,40},{40,48},{48,56},{56,64},{64,7... | collective-permute-start | bytes 7688 | tf_op jit(solution)/shard_map/ppermute | solution.py:37
  14.7 241.0 %collective-permute-start.7 = (f32[4,2,4,4,5]{4,3,2,1,0:T(4,128)}, f32[4,2,4,4,5]{4,3,2,1,0:T(4,128)}, u32[]{:S(2)}, u32[]{:S(2)}) collective-permute-start(f32[4,2,4,4,5]{4,3,2,1,0:T(4,128)} %slice_bitcast_fusion.19), channel_id=1, source_target_pairs={{0,248},{8,0},{16,8},{24,16},{32,24},{40,32},{48,40},{56,48},{64,5... | collective-permute-start | bytes 7688 | tf_op jit(solution)/shard_map/ppermute | solution.py:37
  249.8 11.6 %collective-permute-start.4 = (f32[6,1,8,320]{3,2,1,0:T(8,128)S(1)}, f32[6,1,8,320]{3,2,1,0:T(8,128)S(1)}, u32[]{:S(2)}, u32[]{:S(2)}) collective-permute-start(f32[6,1,8,320]{3,2,1,0:T(8,128)S(1)} %get-tuple-element.736), channel_id=1, source_target_pairs={{0,1},{1,2},{2,3},{4,5},{5,6},{6,7},{8,9},{9,10},{10,11},{12,13},{... | collective-permute-start | bytes 184328 | tf_op jit(solution)/shard_map/ppermute | solution.py:25
  357.1 8.8 collective-permute-start
  366.6 8.8 collective-permute-start
  376.0 8.8 collective-permute-start
  385.4 8.8 collective-permute-start
  394.9 8.8 collective-permute-start
  404.3 8.8 collective-permute-start
  413.8 8.8 collective-permute-start
  423.2 8.8 collective-permute-start
  432.7 8.8 collective-permute-start
  442.1 8.8 collective-permute-start
  451.6 8.8 collective-permute-start
  461.0 8.8 collective-permute-start
  470.5 8.8 collective-permute-start
  479.9 8.8 collective-permute-start
  489.4 8.8 collective-permute-start
  498.8 8.8 collective-permute-start
  508.3 8.8 collective-permute-start
  517.7 8.8 collective-permute-start
  527.2 8.8 collective-permute-start
  536.6 8.8 collective-permute-start
  546.0 8.8 collective-permute-start
  555.5 8.8 collective-permute-start
  564.9 8.8 collective-permute-start
  574.4 8.8 collective-permute-start
  583.8 8.8 collective-permute-start
  593.3 8.8 collective-permute-start
  602.7 8.8 collective-permute-start
  612.2 8.8 collective-permute-start
  621.6 8.8 collective-permute-start
  631.1 8.8 collective-permute-start
  681.6 9.1 collective-permute-start.1
  700.8 8.8 collective-permute-start.1
  710.2 8.8 collective-permute-start.1
  719.7 8.8 collective-permute-start.1
  729.1 8.8 collective-permute-start.1
  738.6 8.8 collective-permute-start.1
  748.0 8.8 collective-permute-start.1
  757.5 8.8 collective-permute-start.1
  766.9 8.8 collective-permute-start.1
  776.4 8.8 collective-permute-start.1
  804.7 8.8 collective-permute-start.1
  814.2 8.8 collective-permute-start.1
  823.6 8.8 collective-permute-start.1
  (63 other events, 1104.8 us)
where the time goes:
time: 1000 us; the launch traced here: 993 us
  starting transfers between devices  305 us (30%)
  local copies, waits for them, and re-layouts  256 us (26%)
  waiting for transfers between devices  254 us (25%)
  matrix products  165 us (16%)
    ppermute x62, starting transfers between devices, shifted(): return lax.ppermute(block, axis, route)  292 us
    ppermute x62, waiting for transfers between devices, shifted(): return lax.ppermute(block, axis, route)  254 us
    dot_general x32, matrix products, couple(): jnp.einsum('lwv,lpv->lpw', jacobian, trace_value.reshape(line_count, 16,...  31.2 us
    another operation x1, local copies, waits for them, and re-layouts, on_device(): bottom_rows = row_layers[:, :, :, 0].reshape(line_count, 80, 4, 4, 4, 5)  29.4 us
    another operation x1, local copies, waits for them, and re-layouts, on_device(): top_rows = row_layers[:, :, :, 3].reshape(line_count, 80, 4, 4, 4, 5)  28.5 us
    unnamed x97, local copies, waits for them, and re-layouts  27.6 us
    dot_general x1, matrix products, volume_term(): jnp.einsum('xyzdwv,xyzabcv->xyzdabcw', volume_jacobian, nodes, precision=...  22.1 us
    slice x2, local copies, waits for them, and re-layouts, on_device(): bottom_from_top = bottom_rows[:, :, :, :, 3].reshape(line_count, 80, 80)  20.4 us
  transfers between devices with their start and end apart: 68, of which 62 were waited for; matrix products, arithmetic and copies ran while one was open for 25% of the time, Pallas kernels for 0%

commit v1 on v0

v1 whole, which is shorter than its diff:
```python
import functools

import jax
import jax.numpy as jnp
import numpy as np
from jax import lax
from jax.experimental import pallas as pl
from jax.experimental.pallas import tpu as pltpu
from jax.sharding import PartitionSpec as P

LIFT = 6.0
F32 = jnp.float32
BF16 = jnp.bfloat16
VMEM_LIMIT = 56 * 1024 * 1024
LINES = 8
SEG = 8


def derivative_matrix():
    points = np.array([-1.0, -1.0 / np.sqrt(5.0), 1.0 / np.sqrt(5.0), 1.0])
    matrix = np.zeros((4, 4))
    for target in range(4):
        for source in range(4):
            if target != source:
                numerator = 1.0
                denominator = 1.0
                for other in range(4):
                    if other != source and other != target:
                        numerator *= points[target] - points[other]
                    if other != source:
                        denominator *= points[source] - points[other]
                matrix[target, source] = numerator / denominator
    for target in range(4):
        matrix[target, target] = -np.sum(matrix[target])
    return matrix


def entry(a, b, c, v):
    return ((4 * a + b) * 4 + c) * 5 + v


@functools.cache
def constants():
    select = np.zeros((1120, 320), np.float32)
    place = np.zeros((320, 800), np.float32)
    layers = np.zeros((160, 320), np.float32)
    for v in range(5):
        for a in range(4):
            for b in range(4):
                for c in range(4):
                    row = v * 64 + a * 16 + b * 4 + c
                    select[row, entry(a, b, c, v)] = 1
                    place[entry(a, b, c, v), row] = 1
        for e in range(4):
            for c in range(4):
                row = v * 16 + e * 4 + c
                for side, plane in enumerate((0, 3)):
                    for flip in range(2):
                        along = 3 - e if flip else e
                        block = (side * 2 + flip) * 80
                        select[320 + block + row, entry(plane, along, c, v)] = 1
                        select[640 + block + row, entry(along, plane, c, v)] = 1
                    place[entry(plane, e, c, v), 320 + 80 * side + row] = -1
                    place[entry(e, plane, c, v), 480 + 80 * side + row] = -1
        for a in range(4):
            for b in range(4):
                row = v * 16 + a * 4 + b
                select[960 + row, entry(a, b, 3, v)] = 1
                select[1040 + row, entry(a, b, 0, v)] = 1
                place[entry(a, b, 0, v), 640 + row] = -1
                place[entry(a, b, 3, v), 720 + row] = -1
                layers[row, entry(a, b, 3, v)] = 1
                layers[80 + row, entry(a, b, 0, v)] = 1
    top, bottom = layers[:80].T, layers[80:].T
    columns_high = np.zeros((320, 512), np.float32)
    columns_low = np.zeros((320, 512), np.float32)
    for base, chosen in ((0, bottom), (256, top)):
        columns_high[:, base : base + 80] = chosen
        columns_high[:, base + 80 : base + 160] = chosen
        columns_low[:, base + 160 : base + 240] = chosen
    spread = np.concatenate([bottom, top], axis=1)
    eye, d = np.eye(4), derivative_matrix()
    along = np.concatenate(
        [
            np.kron(np.kron(d, eye), eye),
            np.kron(np.kron(eye, d), eye),
            np.kron(np.kron(eye, eye), d),
        ],
        axis=1,
    )
    high = along.astype(jnp.bfloat16).astype(np.float64)
    along = np.concatenate([high, high, along - high], axis=1)
    twice = np.concatenate([np.eye(64), np.eye(64)], axis=1)
    as_bf16 = lambda x: np.asarray(x, np.float32).astype(jnp.bfloat16)
    return {
        "select": as_bf16(select),
        "place": as_bf16(place),
        "layers": as_bf16(layers),
        "columns_high": as_bf16(columns_high),
        "columns_low": as_bf16(columns_low),
        "spread": as_bf16(spread),
        "along": as_bf16(along),
        "twice": as_bf16(twice),
        "eye": as_bf16(np.eye(320)),
    }


def dot(a, b):
    return lax.dot_general(a, b, (((1,), (0,)), ((), ())), preferred_element_type=F32)


def dot_nt(a, b):
    return lax.dot_general(a, b, (((1,), (1,)), ((), ())), preferred_element_type=F32)


def split(x):
    high = x.astype(BF16)
    return high, (x - high.astype(F32)).astype(BF16)


def split_3(x):
    high = x.astype(BF16)
    rest = x - high.astype(F32)
    middle = rest.astype(BF16)
    return high, middle, (rest - middle.astype(F32)).astype(BF16)


def lanes(shape):
    return lax.broadcasted_iota(jnp.int32, shape, len(shape) - 1)


def rows(shape):
    return lax.broadcasted_iota(jnp.int32, shape, len(shape) - 2)


def roll(x, amount):
    return pltpu.roll(x, amount % 128, 1)


def pair_lanes(x):
    high = x.astype(BF16).astype(F32)
    return jnp.where(lanes(x.shape) < 64, high, roll(x - high, 64)).astype(BF16)


def left_cat(x):
    high, low = split(x)
    return jnp.concatenate([high, high, low], axis=1)


def right_cat(x):
    high, low = split(x)
    return jnp.concatenate([high, low, high], axis=0)


def prepare_kernel(inverse, columns_high, columns_low, layers, high_out, low_out, fwd_out, bwd_out):
    for line in range(LINES):
        high, low = split(inverse[line])
        high_out[line] = high
        low_out[line] = low
        columns = dot(high, columns_high[...]) + dot(low, columns_low[...])
        chosen = dot(layers[...], columns.astype(BF16)).astype(BF16)
        fwd_out[line] = chosen[:, :256]
        bwd_out[line] = chosen[80:, 256:]


def mix(coefficient, slabs):
    out = []
    for w in range(5):
        total = coefficient(w, 0) * slabs[0]
        for v in range(1, 5):
            total = total + coefficient(w, v) * slabs[v]
        out.append(total)
    return out


def slabs_of(x, size):
    return [x[v * size : (v + 1) * size] for v in range(5)]


def sweep_kernel(
    flags,
    span_scalars,
    flow,
    gx_low,
    gx_high,
    gy_low,
    gy_high,
    below,
    above,
    source,
    pseudo,
    tables,
    inverse_high,
    inverse_low,
    fwd,
    bwd,
    select,
    place,
    layers,
    along,
    twice,
    eye,
    residual_out,
    turned_out,
    maps_out,
    z_high,
    z_low,
    v_high,
    v_low,
    extended,
    flux,
    started,
    t_state,
    w_state,
    bottoms,
):
    first_lo, first_hi = flags[0].astype(F32), flags[1].astype(F32)
    second_lo, second_hi = flags[2].astype(F32), flags[3].astype(F32)
    u = flow[...]
    extended[0:64] = u
    extended[64:80] = gx_high[...] * first_hi
    extended[80:112] = jnp.zeros((32, 320), F32)
    extended[112:128] = gx_low[...] * first_lo
    for i in range(4):
        extended[128 + 16 * i : 136 + 16 * i] = gy_low[8 * i : 8 * i + 8] * second_lo
        extended[136 + 16 * i : 144 + 16 * i] = gy_high[8 * i : 8 * i + 8] * second_hi
    position = rows((8, 320))
    for line in range(LINES):
        extended[192 + 8 * line : 200 + 8 * line] = jnp.where(
            position == 0,
            below[line : line + 1],
            jnp.where(position == 7, above[line : line + 1], 0.0),
        )
    parts = split_3(extended[...])
    chosen = sum(dot_nt(select[...], part) for part in parts)
    near, far = chosen[:, :128], chosen[:, 128:]
    lane = lanes((1, 128))
    table = lambda r: tables[r : r + 1, :]

    by_variable = slabs_of(near[0:320], 64)
    for d in range(3):
        mixed = mix(lambda w, v: table(d * 25 + w * 5 + v), by_variable)
        for w in range(5):
            flux[d * 64 : d * 64 + 64, w * 128 : w * 128 + 128] = mixed[w]
    volume = dot(along[...], right_cat(flux[...]))
    pieces = [volume[:, w * 128 : w * 128 + 128] for w in range(5)]

    for f in range(4):
        base = 320 + 320 * (f // 2)
        candidates = [near[base + 80 * n : base + 80 * n + 80] for n in range(4)]
        outer = [far[base + 80 * n : base + 80 * n + 80] for n in range(4)]
        own = candidates[2 * (f % 2)]
        if f == 0:
            shifted = [roll(x, 16) for x in candidates]
        elif f == 1:
            shifted = [roll(x, -16) for x in candidates]
        elif f == 2:
            shifted = [
                jnp.where((lane // 8) % 2 == 1, roll(x, 8), y) for x, y in zip(candidates, outer)
            ]
        else:
            shifted = [
                jnp.where((lane // 8) % 2 == 0, roll(x, -8), y) for x, y in zip(candidates, outer)
            ]
        mirrored = table(225 + f) > 0.5
        flipped = table(229 + f) > 0.5
        neighbour = jnp.where(
            flipped,
            jnp.where(mirrored, shifted[3], shifted[1]),
            jnp.where(mirrored, shifted[2], shifted[0]),
        )
        jump = LIFT * (neighbour - own)
        pieces += mix(lambda w, v: table(75 + f * 25 + w * 5 + v), slabs_of(jump, 16))

    top, bottom = near[960:1040], near[1040:1120]
    outer_top, outer_bottom = roll(far[960:1040], 64), roll(far[1040:1120], 64)
    lower_jump = LIFT * (jnp.where(lane % 8 == 0, outer_top, roll(top, 1)) - bottom)
    upper_jump = LIFT * (jnp.where(lane % 8 == 7, outer_bottom, roll(bottom, -1)) - top)
    pieces += mix(lambda w, v: table(175 + w * 5 + v), slabs_of(lower_jump, 16))
    pieces += mix(lambda w, v: table(200 + w * 5 + v), slabs_of(upper_jump, 16))
    stacked = jnp.concatenate(pieces, axis=0)
    operator = dot(place[...], pair_lanes(stacked))
    operator_high, operator_low = split(operator)
    operator_rows = dot_nt(twice[...], operator_high) + dot_nt(twice[...], operator_low)
    residual = source[...] - (pseudo[...] * u + operator_rows)
    residual_out[...] = residual

    high, low = split(residual)
    turned = dot_nt(eye[...], jnp.concatenate([high, low], axis=0))
    turned_out[...] = turned + roll(turned, 64)
    turned = turned.astype(BF16)
    wide_lane = lanes((320, 128)) % 64
    direct = jnp.zeros((320, 128), F32)
    for line in range(LINES):
        applied = dot(inverse_high[line], turned) + dot(inverse_low[line], turned)
        direct = jnp.where(wide_lane // 8 == line, applied, direct)
    direct = direct + roll(direct, 64)
    traces = dot(layers[...], pair_lanes(direct))
    traces = traces + roll(traces, 64)

    trace_lane = lanes((160, 128))
    small_lane, small_row = lanes((80, 128)), rows((80, 128))
    for line in range(LINES):
        moved = roll(traces, 80 - 8 * line)
        started[line] = jnp.where((trace_lane >= 80) & (trace_lane < 88), moved, 0.0)
        t_state[line] = jnp.where(small_lane == small_row, 1.0, 0.0)
        w_state[line] = jnp.where(lanes((80, 256)) == rows((80, 256)) + 88, 1.0, 0.0)

    def forward(k, carry):
        mine = small_lane == 80 + k
        for line in range(LINES):
            at = (line * SEG + k) * 50
            z = jnp.concatenate(
                mix(lambda w, v: span_scalars[at + w * 5 + v], slabs_of(t_state[line], 16)),
                axis=0,
            )
            z_hi, z_lo = split(z)
            z_high[line, k] = z_hi
            z_low[line, k] = z_lo
            y = dot(fwd[line, :, 0:240], jnp.concatenate([z_hi, z_lo, z_hi], axis=0))
            t_state[line] = y[:80] + jnp.where(mine, started[line, 0:80], 0.0)
            bottoms[line, k] = y[80:] + jnp.where(mine, started[line, 80:160], 0.0)
        return carry

    lax.fori_loop(0, SEG, forward, 0)

    def backward(step, carry):
        k = SEG - 1 - step
        for line in range(LINES):
            at = (line * SEG + k) * 50 + 25
            z = jnp.concatenate(
                mix(lambda w, v: span_scalars[at + w * 5 + v], slabs_of(w_state[line], 16)),
                axis=0,
            )
            z_hi, z_lo = split(z)
            v_high[line, k] = z_hi
            v_low[line, k] = z_lo
            y = dot(bwd[line, :, 0:240], jnp.concatenate([z_hi, z_lo, z_hi], axis=0))
            w_state[line, :, 0:128] = y[:, :128] + bottoms[line, k]
            w_state[line, :, 128:256] = y[:, 128:]
        return carry

    lax.fori_loop(0, SEG, backward, 0)
    for line in range(LINES):
        maps_out[line, :, 0:128] = w_state[line, :, 0:128]
        maps_out[line, :, 128:256] = w_state[line, :, 128:256] + roll(t_state[line], 40)


def compose_kernel(maps, t_out, w_out, whole_out):
    lane = lanes((80, 128))
    tall_lane, tall_row = lanes((128, 128)), rows((128, 128))
    zero = jnp.zeros((48, 128), F32)
    fixed = jnp.where((tall_row < 80) & (tall_lane == tall_row), 1.0, 0.0)
    ones = jnp.where((tall_row >= 80) & (tall_row < 88) & (tall_lane == 80), 1.0, 0.0)
    state = fixed + ones
    coupled = []
    for e in range(SEG):
        t_out[e] = state
        left, right = maps[e, :, 0:128], maps[e, :, 128:256]
        state_cat = right_cat(state)
        both = jnp.concatenate([jnp.where(lane < 88, roll(right, 88), 0.0), jnp.where(lane < 88, left, 0.0)], axis=0)
        y = dot(left_cat(both), state_cat)
        coupled.append(y[80:])
        state = jnp.concatenate([y[:80], ones[80:]], axis=0)
    last = state[:80]
    w0 = jnp.where(tall_lane == tall_row + 81, 1.0, 0.0)
    w1 = jnp.where((tall_lane == tall_row - 47) & (tall_row < 80), 1.0, 0.0)
    for e in range(SEG - 1, -1, -1):
        w_out[e, :, 0:128] = w0
        w_out[e, :, 128:256] = w1
        left, right = maps[e, :, 0:128], maps[e, :, 128:256]
        back = jnp.where(lane < 40, roll(left, 40), jnp.where(lane < 80, roll(right, 40), 0.0))
        back_cat = left_cat(back)
        y0 = dot(back_cat, right_cat(w0)) + coupled[e]
        y1 = dot(back_cat, right_cat(w1))
        w0 = jnp.concatenate([y0, zero], axis=0)
        w1 = jnp.concatenate([y1, zero], axis=0)
    second = w1[:80] + roll(last, 33)
    for copy in range(whole_out.shape[0]):
        whole_out[copy, :, 0:128] = w0[:80]
        whole_out[copy, :, 128:256] = second


def solve_kernel(flags, wholes, t_in, w_in, out):
    groups = wholes.shape[0]
    lane = lanes((80, 128))
    tall_row = rows((128, 128))
    one = jnp.where(tall_row == 80, 1.0, 0.0)
    zero = jnp.zeros((48, 128), F32)

    def pieces(group):
        left, right = wholes[group, :, 0:128], wholes[group, :, 128:256]
        forward = jnp.where(lane < 81, roll(right, -33), 0.0)
        cross = jnp.where(lane < 81, left, 0.0)
        back = jnp.where(lane < 47, roll(left, 47), jnp.where(lane < 80, roll(right, 47), 0.0))
        return forward, cross, back

    parts = [pieces(group) for group in range(groups)]
    traces = [one]
    for group in range(groups - 1):
        y = dot(left_cat(parts[group][0]), right_cat(traces[-1]))
        traces.append(jnp.concatenate([y, zero], axis=0) + one)
    backs = [jnp.zeros((128, 128), F32)]
    for group in range(groups - 1, 0, -1):
        y = dot(left_cat(parts[group][1]), right_cat(traces[group]))
        y = y + dot(left_cat(parts[group][2]), right_cat(backs[0]))
        backs.insert(0, jnp.concatenate([y, zero], axis=0))
    mine = flags[4]
    trace, back = traces[0], backs[0]
    for group in range(1, groups):
        trace = jnp.where(mine == group, traces[group], trace)
        back = jnp.where(mine == group, backs[group], back)
    trace_row = jnp.transpose(trace)[0:8]
    back_row = roll(jnp.transpose(back)[0:8], 81)
    line_lane = lanes((8, 128))
    y0 = jnp.where(line_lane < 81, trace_row, back_row)
    y1 = jnp.where(line_lane < 33, back_row, 0.0)
    trace_cat = left_cat(trace_row)
    y_cat = left_cat(jnp.concatenate([y0, y1], axis=1))
    for e in range(SEG):
        high, low = split(t_in[e])
        t_row = dot_nt(trace_cat, jnp.concatenate([high, low, high], axis=1))
        high, low = split(w_in[e])
        c_row = roll(dot_nt(y_cat, jnp.concatenate([high, low, high], axis=1)), 88)
        first = jnp.where(line_lane < 80, t_row, jnp.where(line_lane < 88, 1.0, c_row))
        second = jnp.where(line_lane < 40, c_row, 0.0)
        out[e : e + 1, 0:128] = first[0:1]
        out[e : e + 1, 128:256] = second[0:1]


def finish_kernel(
    incoming,
    z_high,
    z_low,
    v_high,
    v_low,
    turned,
    inverse_high,
    inverse_low,
    flow,
    spread,
    twice,
    out,
):
    y = incoming[...]
    y = jnp.broadcast_to(y[:, None, :], (8, 8, 256)).reshape(64, 256)
    high, low = split(y)
    y = jnp.concatenate([high, low], axis=0)
    small_lane = lanes((80, 128)) % 64
    lower = jnp.zeros((80, 128), F32)
    upper = jnp.zeros((80, 128), F32)
    for line in range(LINES):
        z_hi, z_lo = z_high[line].reshape(640, 128), z_low[line].reshape(640, 128)
        v_hi, v_lo = v_high[line].reshape(640, 256), v_low[line].reshape(640, 256)
        c = dot_nt(z_hi, y[:, :128]) + dot_nt(z_lo, y[:, :128])
        d = dot_nt(v_hi, y) + dot_nt(v_lo, y)
        for k in range(SEG):
            mine = small_lane == line * SEG + k
            lower = jnp.where(mine, c[80 * k : 80 * k + 80], lower)
            upper = jnp.where(mine, d[80 * k : 80 * k + 80], upper)
    both = jnp.concatenate([lower, upper], axis=0)
    both = both + roll(both, 64)
    added = dot(spread[...], pair_lanes(both))
    load = pair_lanes(turned[...] + added + roll(added, 64))
    wide_lane = lanes((320, 128)) % 64
    total = jnp.zeros((320, 128), F32)
    for line in range(LINES):
        applied = dot(inverse_high[line], load) + dot(inverse_low[line], load)
        total = jnp.where(wide_lane // 8 == line, applied, total)
    high, low = split(total)
    out[...] = flow[...] + dot_nt(twice[...], high) + dot_nt(twice[...], low)


def call(kernel, out_shape, in_specs, scratch=(), flops=0, moved=0, name=None):
    return pl.pallas_call(
        kernel,
        out_shape=out_shape,
        in_specs=in_specs,
        out_specs=jax.tree.map(lambda _: pl.BlockSpec(memory_space=pltpu.VMEM), out_shape),
        scratch_shapes=list(scratch),
        compiler_params=pltpu.CompilerParams(vmem_limit_bytes=VMEM_LIMIT),
        cost_estimate=pl.CostEstimate(flops=flops, bytes_accessed=moved, transcendentals=0),
        name=name,
    )


VM = pl.BlockSpec(memory_space=pltpu.VMEM)
SM = pl.BlockSpec(memory_space=pltpu.SMEM)


def shape(*dims, dtype=F32):
    return jax.ShapeDtypeStruct(dims, dtype)


def on_device(
    flow_state,
    source_term,
    pseudo_time,
    volume_jacobian,
    side_jacobian,
    span_jacobian,
    line_inverse,
    mirror_face,
    edge_flip,
):
    const = {name: jnp.asarray(value) for name, value in constants().items()}
    span_size, gx_size, gy_size = (lax.axis_size(a) for a in ("span", "gx", "gy"))
    groups = span_size // SEG
    span_at, gx_at, gy_at = (lax.axis_index(a) for a in ("span", "gx", "gy"))
    flags = jnp.stack(
        [
            (gx_at > 0).astype(jnp.int32),
            (gx_at < gx_size - 1).astype(jnp.int32),
            (gy_at > 0).astype(jnp.int32),
            (gy_at < gy_size - 1).astype(jnp.int32),
            (span_at // SEG).astype(jnp.int32),
        ]
    )

    def ring(value, axis, step):
        count = lax.axis_size(axis)
        return lax.ppermute(value, axis, [(i, (i + step) % count) for i in range(count)])

    with jax.named_scope("halo"):
        gx_high = ring(flow_state[0], "gx", -1).reshape(16, 320)
        gx_low = ring(flow_state[3], "gx", 1).reshape(16, 320)
        gy_low = ring(flow_state[:, 1], "gy", 1).reshape(32, 320)
        gy_high = ring(flow_state[:, 0], "gy", -1).reshape(32, 320)
        below = ring(flow_state[:, :, SEG - 1], "span", 1).reshape(8, 320)
        above = ring(flow_state[:, :, 0], "span", -1).reshape(8, 320)

    with jax.named_scope("tables"):
        turn = lambda x: jnp.moveaxis(x.reshape(64, -1), 0, 1).astype(F32)
        tables = jnp.concatenate(
            [
                turn(x)
                for x in (volume_jacobian, side_jacobian, span_jacobian, mirror_face, edge_flip)
            ],
            axis=0,
        )
        tables = jnp.pad(tables, ((0, 0), (0, 64)))
        span_scalars = (LIFT * span_jacobian).reshape(3200)

    flow = flow_state.reshape(64, 320)
    inverse = line_inverse.reshape(LINES, 320, 320)
    inverse_high, inverse_low, fwd, bwd = call(
        prepare_kernel,
        (
            shape(LINES, 320, 320, dtype=BF16),
            shape(LINES, 320, 320, dtype=BF16),
            shape(LINES, 160, 256, dtype=BF16),
            shape(LINES, 80, 256, dtype=BF16),
        ),
        [VM] * 4,
        flops=4_000_000_000,
        moved=8_000_000,
        name="prepare",
    )(inverse, const["columns_high"], const["columns_low"], const["layers"])

    residual, turned, maps, z_high, z_low, v_high, v_low = call(
        sweep_kernel,
        (
            shape(64, 320),
            shape(320, 128),
            shape(LINES, 80, 256),
            shape(LINES, SEG, 80, 128, dtype=BF16),
            shape(LINES, SEG, 80, 128, dtype=BF16),
            shape(LINES, SEG, 80, 256, dtype=BF16),
            shape(LINES, SEG, 80, 256, dtype=BF16),
        ),
        [SM, SM] + [VM] * 20,
        scratch=[
            pltpu.VMEM((256, 320), F32),
            pltpu.VMEM((192, 640), F32),
            pltpu.VMEM((LINES, 160, 128), F32),
            pltpu.VMEM((LINES, 80, 128), F32),
            pltpu.VMEM((LINES, 80, 256), F32),
            pltpu.VMEM((LINES, SEG, 80, 128), F32),
        ],
        flops=10_000_000_000,
        moved=20_000_000,
        name="sweep",
    )(
        flags,
        span_scalars,
        flow,
        gx_low,
        gx_high,
        gy_low,
        gy_high,
        below,
        above,
        source_term.reshape(64, 320),
        pseudo_time.reshape(64, 320),
        tables,
        inverse_high,
        inverse_low,
        fwd,
        bwd,
        const["select"],
        const["place"],
        const["layers"],
        const["along"],
        const["twice"],
        const["eye"],
    )

    within = [[SEG * g + m for m in range(SEG)] for g in range(groups)]
    across = [[SEG * g + m for g in range(groups)] for m in range(SEG)]

    def exchange(value, members):
        return lax.all_to_all(value, "span", 0, 0, axis_index_groups=members, tiled=True)

    maps = exchange(maps, within)
    t_maps, w_maps, whole = call(
        compose_kernel,
        (shape(SEG, 128, 128), shape(SEG, 128, 256), shape(groups, 80, 256)),
        [VM],
        name="compose",
    )(maps)
    wholes = exchange(whole, across)
    answers = call(solve_kernel, shape(SEG, 256), [SM] + [VM] * 3, name="solve")(
        flags, wholes, t_maps, w_maps
    )
    incoming = exchange(answers, within)
    updated = call(finish_kernel, shape(64, 320), [VM] * 11, name="finish")(
        incoming,
        z_high,
        z_low,
        v_high,
        v_low,
        turned,
        inverse_high,
        inverse_low,
        flow,
        const["spread"],
        const["twice"],
    )
    return updated.reshape(flow_state.shape), residual.reshape(flow_state.shape)


def solution(mesh):
    lines = P("gx", "gy", "span", None)
    blocks = P("gx", "gy", "span", None, None, None)
    return jax.shard_map(
        on_device,
        mesh=mesh,
        in_specs=(lines, lines, lines, blocks, blocks, blocks, P("gx", "gy", None, None), lines, lines),
        out_specs=(lines, lines),
        check_vma=False,
    )
```

time: 1000 us -> 111 us (0.11)
  the two profiles are of different devices: /device:TPU:118 before, /device:TPU:2 now
where the time goes in v1:
time: 111 us; the launch traced here: 110 us
  blocking collectives  47.1 us (42%)
  Pallas kernels  45.7 us (41%)
  local copies, waits for them, and re-layouts  10.6 us (10%)
  starting transfers between devices  5.95 us (5%)
    all_to_all x3, blocking collectives, exchange(): lax.all_to_all(value, 'span', 0, 0, axis_index_groups=members, tiled=True)  47.1 us
    pallas_call x1, Pallas kernels, on_device(): call(sweep_kernel, (shape(64, 320), shape(320, 128), shape(LINES, 80, 256...  18.9 us
    pallas_call x1, Pallas kernels, on_device(): call(finish_kernel, shape(64, 320), [VM] * 11, name='finish')  9.48 us
    pallas_call x1, Pallas kernels, on_device(): call(prepare_kernel, (shape(LINES, 320, 320, dtype=BF16), shape(LINES, 32...  8.57 us
    ppermute x6, starting transfers between devices, ring(): lax.ppermute(value, axis, [(i, (i + step) % count) for i in range(count)])  5.95 us
    pallas_call x1, Pallas kernels, on_device(): call(compose_kernel, (shape(SEG, 128, 128), shape(SEG, 128, 256), shape(g...  4.54 us
    pallas_call x1, Pallas kernels, on_device(): call(solve_kernel, shape(SEG, 256), [SM] + [VM] * 3, name='solve')  4.13 us
  transfers between devices with their start and end apart: 6, of which 0 were waited for; matrix products, arithmetic and copies ran while one was open for 7% of the time, Pallas kernels for 8%

profile of v1, /device:TPU:2, one launch (start us, length us, event | category | flops | bytes accessed | tf_op | source)
XLA Modules:
  0.0 110.3 jit_solution(3666612745306683255)
XLA Ops:
  0.6 1.0 fusion
  1.6 1.6 %collective-permute-start.4 = (f32[4,2,320]{2,1,0:T(2,128)S(1)}, f32[4,2,320]{2,1,0:T(2,128)S(1)}, u32[]{:S(2)}, u32[]{:S(2)}) collective-permute-start(f32[4,2,320]{2,1,0:T(2,128)S(1)} %bitcast.57), channel_id=1, source_target_pairs={{0,8},{8,16},{16,24},{24,32},{32,40},{40,48},{48,56},{56,64},{64,7... | collective-permute-start | bytes 30728 | tf_op jit(solution)/shard_map/halo/ppermute | solution.py:522
  3.2 0.9 collective-permute-start.5
  4.1 0.8 slice_bitcast_fusion.2
  4.8 0.0 collective-permute-start.1
  4.9 0.5 collective-permute-start
  5.4 0.8 slice_bitcast_fusion
  6.2 2.7 %collective-permute-start.3 = (f32[4,8,320]{2,1,0:T(8,128)S(1)}, f32[4,8,320]{2,1,0:T(8,128)S(1)}, u32[]{:S(2)}, u32[]{:S(2)}) collective-permute-start(f32[4,8,320]{2,1,0:T(8,128)S(1)} %get-tuple-element.32), channel_id=1, source_target_pairs={{0,3},{1,0},{2,1},{3,2},{4,7},{5,4},{6,5},{7,6},{8,11},{9,8},{10,9... | collective-permute-start | bytes 122888 | tf_op jit(solution)/shard_map/halo/ppermute | solution.py:522
  8.9 8.6 %prepare.1 = (bf16[8,320,320]{2,1,0:T(8,128)(2,1)}, bf16[8,320,320]{2,1,0:T(8,128)(2,1)}, bf16[8,160,256]{2,1,0:T(8,128)(2,1)}, bf16[8,80,256]{2,1,0:T(8,128)(2,1)}) custom-call(f32[8,320,320]{2,1,0:T(8,128)} %bitcast.60, bf16[320,512]{1,0:T(8,128)(2,1)} %constant.58.clone.columns_high, bf16[320,512]{1,0:T(8,128)(2,1)} %constant.59.clone.columns_low, ...), custom_call_target="tpu_custom_call" | custom-call | flops 4000000000 | bytes 8000000 | tf_op jit(solution)/shard_map/prepare/pallas_call | solution.py:546
  17.5 0.0 collective-permute-done.4
  17.5 0.3 collective-permute-start.2
  17.8 0.1 broadcast_multiply_fusion
  17.9 0.1 copy.34
  18.0 0.0 copy-done.3
  18.1 0.1 convert_element_type.25
  18.2 0.1 convert_element_type.28
  18.3 0.3 reshape.70
  18.5 0.1 copy.32
  18.7 0.4 reshape.68
  19.0 0.5 copy.31
  19.6 0.8 reshape.58.span_scalars
  20.4 0.2 copy.33
  20.6 0.5 reshape.69
  21.1 0.4 concatenate.3
  21.5 0.7 pad.4.tables
  22.2 0.7 stack.39.flags
  22.9 0.6 reshape.64.below
  23.5 0.0 collective-permute-done.5
  23.5 0.6 reshape.65.above
  24.1 0.0 collective-permute-done.1
  24.1 0.0 collective-permute-done
  24.1 0.0 copy-start.8
  24.1 0.0 collective-permute-done.3
  24.1 0.0 collective-permute-done.2
  24.1 0.0 copy-start.6
  24.1 0.5 copy-done.7
  24.7 0.0 copy-done.8
  24.7 0.0 copy-done.5
  24.7 0.0 copy-done.6
  24.8 18.9 %sweep.1 = (f32[64,320]{1,0:T(8,128)}, f32[320,128]{1,0:T(8,128)}, f32[8,80,256]{2,1,0:T(8,128)}, bf16[8,8,80,128]{3,2,1,0:T(8,128)(2,1)}, bf16[8,8,80,128]{3,2,...) custom-call(s32[5]{0:T(128)} %stack.39.flags, f32[3200]{0:T(1024)} %reshape.58.span_scalars, ...), custom_call_target="tpu_custom_call" | custom-call | flops 10000000000 | bytes 20000000 | tf_op jit(solution)/shard_map/sweep/pallas_call | solution.py:560
  43.7 21.1 %all_to_all.21.maps = f32[8,80,256]{2,1,0:T(8,128)} all-to-all(f32[8,80,256]{2,1,0:T(8,128)} %get-tuple-element.20), channel_id=1, replica_groups={{0,8,16,24,32,40,48,56},{64,72,80,88,96,104,112,120},{128,136,144,152,1..., dimensions={0} | all-to-all | bytes 1310720 | tf_op jit(solution)/shard_map/all_to_all | solution.py:612
  64.8 4.5 %compose.1 = (f32[8,128,128]{2,1,0:T(8,128)}, f32[8,128,256]{2,1,0:T(8,128)}, f32[4,80,256]{2,1,0:T(8,128)}) custom-call(f32[8,80,256]{2,1,0:T(8,128)} %all_to_all.21.maps), custom_call_target="tpu_custom_call" | custom-call | tf_op jit(solution)/shard_map/compose/pallas_call | solution.py:615
  69.3 17.6 %all_to_all.22.wholes = f32[4,80,256]{2,1,0:T(8,128)} all-to-all(f32[4,80,256]{2,1,0:T(8,128)} %get-tuple-element.21), channel_id=1, replica_groups={{0,64,128,192},{8,72,136,200},{16,80,144,208},{24,88,152,216},{32,96,16..., dimensions={0} | all-to-all | bytes 655360 | tf_op jit(solution)/shard_map/all_to_all | solution.py:612
  86.9 4.1 %solve.1 = f32[8,256]{1,0:T(8,128)} custom-call(s32[5]{0:T(128)} %stack.39.flags, f32[4,80,256]{2,1,0:T(8,128)} %all_to_all.22.wholes, f32[8,128,128]{2,1,0:T(8,128)} %get-tuple-element.22.t_in, f32[8,128,256]{2,1,0:T(8,128)} %get-tuple-element.23.w_in), custom_call_target="tpu_custom_call" | custom-call | tf_op jit(solution)/shard_map/solve/pallas_call | solution.py:622
  91.0 0.7 copy.37
  91.8 8.4 %all_to_all.23 = f32[8,1,256]{2,1,0:T(1,128)S(1)} all-to-all(f32[8,1,256]{2,1,0:T(1,128)S(1)} %copy.37), channel_id=1, replica_groups={{0,8,16,24,32,40,48,56},{64,72,80,88,96,104,112,120},{128,136,144,152,1..., dimensions={0} | all-to-all | bytes 16384 | tf_op jit(solution)/shard_map/all_to_all | solution.py:612
  100.2 0.6 copy.46
  100.8 9.5 %finish.1 = f32[64,320]{1,0:T(8,128)} custom-call(f32[8,256]{1,0:T(8,128)} %bitcast.55, bf16[8,8,80,128]{3,2,1,0:T(8,128)(2,1)} %get-tuple-element.24.z_high, bf16[8,8,80,128]{3,2,1,0:T(8,128)(2,1)} %get-tuple-element.25.z_low, bf16[8,8,80,256]{3,2,1,0:T(8,128)(2,1)} %get-tuple-element.26.v_high, bf16[8,8,80,256]{3,2,1,0:T(8,128)(2,1)} %get-tuple-element.27.v_low, ...), custom_call_target="tpu_custom_call" | custom-call | tf_op jit(solution)/shard_map/finish/pallas_call | solution.py:626
  (17 shorter events, 0.1 us)
Async XLA Ops:
  1.6 15.9 %collective-permute-start.4 = (f32[4,2,320]{2,1,0:T(2,128)S(1)}, f32[4,2,320]{2,1,0:T(2,128)S(1)}, u32[]{:S(2)}, u32[]{:S(2)}) collective-permute-start(f32[4,2,320]{2,1,0:T(2,128)S(1)} %bitcast.57), channel_id=1, source_target_pairs={{0,8},{8,16},{16,24},{24,32},{32,40},{40,48},{48,56},{56,64},{64,7... | collective-permute-start | bytes 30728 | tf_op jit(solution)/shard_map/halo/ppermute | solution.py:522
  3.2 20.3 %collective-permute-start.5 = (f32[4,2,320]{2,1,0:T(2,128)S(1)}, f32[4,2,320]{2,1,0:T(2,128)S(1)}, u32[]{:S(2)}, u32[]{:S(2)}) collective-permute-start(f32[4,2,320]{2,1,0:T(2,128)S(1)} %bitcast.56), channel_id=1, source_target_pairs={{0,248},{8,0},{16,8},{24,16},{32,24},{40,32},{48,40},{56,48},{64,5... | collective-permute-start | bytes 30728 | tf_op jit(solution)/shard_map/halo/ppermute | solution.py:522
  4.8 19.2 %collective-permute-start.1 = (f32[2,8,320]{2,1,0:T(8,128)S(1)}, f32[2,8,320]{2,1,0:T(8,128)S(1)}, u32[]{:S(2)}, u32[]{:S(2)}) collective-permute-start(f32[2,8,320]{2,1,0:T(8,128)S(1)} %get-tuple-element.34), channel_id=1, source_target_pairs={{0,4},{4,0},{1,5},{5,1},{2,6},{6,2},{3,7},{7,3},{8,12},{12,8},{9,1... | collective-permute-start | bytes 61448 | tf_op jit(solution)/shard_map/halo/ppermute | solution.py:522
  4.9 19.2 %collective-permute-start = (f32[2,8,320]{2,1,0:T(8,128)S(1)}, f32[2,8,320]{2,1,0:T(8,128)S(1)}, u32[]{:S(2)}, u32[]{:S(2)}) collective-permute-start(f32[2,8,320]{2,1,0:T(8,128)S(1)} %get-tuple-element.35), channel_id=1, source_target_pairs={{0,4},{4,0},{1,5},{5,1},{2,6},{6,2},{3,7},{7,3},{8,12},{12,8},{9,1... | collective-permute-start | bytes 61448 | tf_op jit(solution)/shard_map/halo/ppermute | solution.py:522
  6.2 17.9 %collective-permute-start.3 = (f32[4,8,320]{2,1,0:T(8,128)S(1)}, f32[4,8,320]{2,1,0:T(8,128)S(1)}, u32[]{:S(2)}, u32[]{:S(2)}) collective-permute-start(f32[4,8,320]{2,1,0:T(8,128)S(1)} %get-tuple-element.32), channel_id=1, source_target_pairs={{0,3},{1,0},{2,1},{3,2},{4,7},{5,4},{6,5},{7,6},{8,11},{9,8},{10,9... | collective-permute-start | bytes 122888 | tf_op jit(solution)/shard_map/halo/ppermute | solution.py:522
  8.9 8.9 %copy-start = (f32[4,2,8,2,5,5]{2,3,5,4,1,0:T(2,128)S(1)}, f32[4,2,8,2,5,5]{2,3,5,4,1,0:T(2,128)}, u32[]{:S(2)}) copy-start(f32[4,2,8,2,5,5]{2,3,5,4,1,0:T(2,128)} %param.23) | copy-start | bytes 38404
  8.9 9.1 %copy-start.3 = (s32[4,2,8,4]{2,3,1,0:T(4,128)S(1)}, s32[4,2,8,4]{2,3,1,0:T(4,128)}, u32[]{:S(2)}) copy-start(s32[4,2,8,4]{2,3,1,0:T(4,128)} %param.25) | copy-start | bytes 3076
  8.9 9.2 %copy-start.4 = (s32[4,2,8,4]{2,3,1,0:T(4,128)S(1)}, s32[4,2,8,4]{2,3,1,0:T(4,128)}, u32[]{:S(2)}) copy-start(s32[4,2,8,4]{2,3,1,0:T(4,128)} %param.26) | copy-start | bytes 3076
  8.9 9.6 %copy-start.2 = (f32[4,2,8,3,5,5]{2,1,5,4,3,0:T(2,128)S(1)}, f32[4,2,8,3,5,5]{2,1,5,4,3,0:T(2,128)}, u32[]{:S(2)}) copy-start(f32[4,2,8,3,5,5]{2,1,5,4,3,0:T(2,128)} %param.21) | copy-start | bytes 57604
  17.5 2.9 %copy-start.1 = (f32[4,2,8,4,5,5]{2,3,5,4,1,0:T(4,128)S(1)}, f32[4,2,8,4,5,5]{2,3,5,4,1,0:T(4,128)}, u32[]{:S(2)}) copy-start(f32[4,2,8,4,5,5]{2,3,5,4,1,0:T(4,128)} %param.22) | copy-start | bytes 76804
  17.5 6.6 %collective-permute-start.2 = (f32[4,8,320]{2,1,0:T(8,128)S(1)}, f32[4,8,320]{2,1,0:T(8,128)S(1)}, u32[]{:S(2)}, u32[]{:S(2)}) collective-permute-start(f32[4,8,320]{2,1,0:T(8,128)S(1)} %get-tuple-element.33), channel_id=1, source_target_pairs={{0,1},{1,2},{2,3},{3,0},{4,5},{5,6},{6,7},{7,4},{8,9},{9,10},{10,1... | collective-permute-start | bytes 122888 | tf_op jit(solution)/shard_map/halo/ppermute | solution.py:522
  24.1 0.6 copy-start.7
  24.1 0.6 copy-start.8
  24.1 0.6 copy-start.5
  24.1 0.6 copy-start.6

commit v2 on v1

--- a/solution.py
+++ b/solution.py
@@ -11,7 +11,6 @@
 LIFT = 6.0
 F32 = jnp.float32
 BF16 = jnp.bfloat16
-VMEM_LIMIT = 56 * 1024 * 1024
 LINES = 8
 SEG = 8
 
@@ -91,18 +90,32 @@
     high = along.astype(jnp.bfloat16).astype(np.float64)
     along = np.concatenate([high, high, along - high], axis=1)
     twice = np.concatenate([np.eye(64), np.eye(64)], axis=1)
-    as_bf16 = lambda x: np.asarray(x, np.float32).astype(jnp.bfloat16)
-    return {
-        "select": as_bf16(select),
-        "place": as_bf16(place),
-        "layers": as_bf16(layers),
-        "columns_high": as_bf16(columns_high),
-        "columns_low": as_bf16(columns_low),
-        "spread": as_bf16(spread),
-        "along": as_bf16(along),
-        "twice": as_bf16(twice),
-        "eye": as_bf16(np.eye(320)),
-    }
+    eye_320 = np.eye(320)
+    blocks = [
+        select,
+        place[:, :320],
+        place[:, 320:640],
+        place[:, 640:],
+        along[:, :192],
+        along[:, 384:],
+        twice,
+        eye_320,
+        spread,
+    ]
+    fixed = np.zeros((sum(len(block) for block in blocks), 320), np.float32)
+    at = 0
+    for block in blocks:
+        fixed[at : at + len(block), : block.shape[1]] = block
+        at += len(block)
+    early = np.zeros((800, 512), np.float32)
+    early[:320], early[320:640], early[640:, :320] = columns_high, columns_low, layers
+    return early.astype(jnp.bfloat16), fixed.astype(jnp.bfloat16)
+
+
+SELECT, PLACE_A, PLACE_B, PLACE_C = slice(0, 1120), slice(1120, 1440), slice(1440, 1760), slice(1760, 2080)
+ALONG_HIGH, ALONG_LOW, TWICE = slice(2080, 2144), slice(2144, 2208), slice(2208, 2272)
+EYE, SPREAD = slice(2272, 2592), slice(2592, 2912)
+SIDE, SPAN, MIRROR, FLIP = 80, 184, 240, 244
 
 
 def dot(a, b):
@@ -152,15 +165,65 @@
     return jnp.concatenate([high, low, high], axis=0)
 
 
-def prepare_kernel(inverse, columns_high, columns_low, layers, high_out, low_out, fwd_out, bwd_out):
-    for line in range(LINES):
-        high, low = split(inverse[line])
+def pack_kernel(flow, plane_out, up_out, down_out, last_out, first_out):
+    at = pl.multiple_of((1 - lax.axis_index("gx")) * 48, 16)
+    plane_out[...] = flow[pl.ds(at, 16)]
+    for i in range(4):
+        down_out[8 * i : 8 * i + 8] = flow[16 * i : 16 * i + 8]
+        up_out[8 * i : 8 * i + 8] = flow[16 * i + 8 : 16 * i + 16]
+    for line in range(LINES):
+        first_out[line : line + 1] = flow[8 * line : 8 * line + 1]
+        last_out[line : line + 1] = flow[8 * line + 7 : 8 * line + 8]
+
+
+def prepare_kernel(
+    inverse,
+    early,
+    volume_jacobian,
+    side_jacobian,
+    span_jacobian,
+    mirror_face,
+    edge_flip,
+    high_out,
+    low_out,
+    rows_high,
+    rows_low,
+    fwd_out,
+    bwd_out,
+    tables,
+    wide,
+    held,
+    arrived,
+):
+    copies = [
+        pltpu.make_async_copy(inverse.at[line], held.at[line], arrived.at[line])
+        for line in range(LINES)
+    ]
+    for copy in copies:
+        copy.start()
+    for line in range(LINES):
+        here = slice(8 * line, 8 * line + 8)
+        tables[0:75, here] = volume_jacobian[line // 2, :, line % 2, :]
+        tables[SIDE : SIDE + 100, here] = side_jacobian[line].reshape(100, 8)
+        span = LIFT * span_jacobian[line].reshape(50, 8)
+        tables[SPAN : SPAN + 50, here] = span
+        tables[MIRROR : MIRROR + 4, here] = mirror_face[line].astype(F32)
+        tables[FLIP : FLIP + 4, here] = edge_flip[line].astype(F32)
+        for k in range(SEG):
+            wide[line, k] = jnp.broadcast_to(span[:, k : k + 1], (50, 128))
+    for line in range(LINES):
+        copies[line].wait()
+        high, low = split(held[line])
         high_out[line] = high
         low_out[line] = low
-        columns = dot(high, columns_high[...]) + dot(low, columns_low[...])
-        chosen = dot(layers[...], columns.astype(BF16)).astype(BF16)
-        fwd_out[line] = chosen[:, :256]
-        bwd_out[line] = chosen[80:, 256:]
+        layers = early[640:800, 0:320]
+        chosen_high = dot(layers, high).astype(BF16)
+        chosen_low = dot(layers, low).astype(BF16)
+        rows_high[line] = chosen_high
+        rows_low[line] = chosen_low
+        both = (dot(chosen_high, early[0:320]) + dot(chosen_low, early[320:640])).astype(BF16)
+        fwd_out[line] = both[:, :256]
+        bwd_out[line] = both[80:, 256:]
 
 
 def mix(coefficient, slabs):
@@ -178,11 +241,8 @@
 
 
 def sweep_kernel(
-    flags,
-    span_scalars,
     flow,
-    gx_low,
-    gx_high,
+    plane,
     gy_low,
     gy_high,
     below,
@@ -190,16 +250,12 @@
     source,
     pseudo,
     tables,
-    inverse_high,
-    inverse_low,
+    wide,
+    rows_high,
+    rows_low,
     fwd,
     bwd,
-    select,
-    place,
-    layers,
-    along,
-    twice,
-    eye,
+    fixed,
     residual_out,
     turned_out,
     maps_out,
@@ -214,13 +270,15 @@
     w_state,
     bottoms,
 ):
-    first_lo, first_hi = flags[0].astype(F32), flags[1].astype(F32)
-    second_lo, second_hi = flags[2].astype(F32), flags[3].astype(F32)
+    gx_at, gy_at = lax.axis_index("gx"), lax.axis_index("gy")
+    first_lo = (gx_at > 0).astype(F32)
+    second_lo = (gy_at > 0).astype(F32)
+    second_hi = (gy_at < lax.axis_size("gy") - 1).astype(F32)
     u = flow[...]
     extended[0:64] = u
-    extended[64:80] = gx_high[...] * first_hi
+    extended[64:80] = plane[...] * (1.0 - first_lo)
     extended[80:112] = jnp.zeros((32, 320), F32)
-    extended[112:128] = gx_low[...] * first_lo
+    extended[112:128] = plane[...] * first_lo
     for i in range(4):
         extended[128 + 16 * i : 136 + 16 * i] = gy_low[8 * i : 8 * i + 8] * second_lo
         extended[136 + 16 * i : 144 + 16 * i] = gy_high[8 * i : 8 * i + 8] * second_hi
@@ -231,8 +289,7 @@
             below[line : line + 1],
             jnp.where(position == 7, above[line : line + 1], 0.0),
         )
-    parts = split_3(extended[...])
-    chosen = sum(dot_nt(select[...], part) for part in parts)
+    chosen = sum(dot_nt(fixed[SELECT], part) for part in split(extended[...]))
     near, far = chosen[:, :128], chosen[:, 128:]
     lane = lanes((1, 128))
     table = lambda r: tables[r : r + 1, :]
@@ -242,7 +299,9 @@
         mixed = mix(lambda w, v: table(d * 25 + w * 5 + v), by_variable)
         for w in range(5):
             flux[d * 64 : d * 64 + 64, w * 128 : w * 128 + 128] = mixed[w]
-    volume = dot(along[...], right_cat(flux[...]))
+    flux_high, flux_low = split(flux[...])
+    volume = dot(fixed[ALONG_HIGH, 0:192], flux_high) + dot(fixed[ALONG_HIGH, 0:192], flux_low)
+    volume = volume + dot(fixed[ALONG_LOW, 0:192], flux_high)
     pieces = [volume[:, w * 128 : w * 128 + 128] for w in range(5)]
 
     for f in range(4):
@@ -262,43 +321,44 @@
             shifted = [
                 jnp.where((lane // 8) % 2 == 0, roll(x, -8), y) for x, y in zip(candidates, outer)
             ]
-        mirrored = table(225 + f) > 0.5
-        flipped = table(229 + f) > 0.5
+        mirrored = table(MIRROR + f) > 0.5
+        flipped = table(FLIP + f) > 0.5
         neighbour = jnp.where(
             flipped,
             jnp.where(mirrored, shifted[3], shifted[1]),
             jnp.where(mirrored, shifted[2], shifted[0]),
         )
         jump = LIFT * (neighbour - own)
-        pieces += mix(lambda w, v: table(75 + f * 25 + w * 5 + v), slabs_of(jump, 16))
+        pieces += mix(lambda w, v: table(SIDE + (w * 5 + v) * 4 + f), slabs_of(jump, 16))
 
     top, bottom = near[960:1040], near[1040:1120]
     outer_top, outer_bottom = roll(far[960:1040], 64), roll(far[1040:1120], 64)
-    lower_jump = LIFT * (jnp.where(lane % 8 == 0, outer_top, roll(top, 1)) - bottom)
-    upper_jump = LIFT * (jnp.where(lane % 8 == 7, outer_bottom, roll(bottom, -1)) - top)
-    pieces += mix(lambda w, v: table(175 + w * 5 + v), slabs_of(lower_jump, 16))
-    pieces += mix(lambda w, v: table(200 + w * 5 + v), slabs_of(upper_jump, 16))
-    stacked = jnp.concatenate(pieces, axis=0)
-    operator = dot(place[...], pair_lanes(stacked))
+    lower_jump = jnp.where(lane % 8 == 0, outer_top, roll(top, 1)) - bottom
+    upper_jump = jnp.where(lane % 8 == 7, outer_bottom, roll(bottom, -1)) - top
+    pieces += mix(lambda w, v: table(SPAN + (w * 5 + v) * 2), slabs_of(lower_jump, 16))
+    pieces += mix(lambda w, v: table(SPAN + (w * 5 + v) * 2 + 1), slabs_of(upper_jump, 16))
+    pieces = [
+        pair_lanes(jnp.concatenate(group, axis=0)) for group in (pieces[:5], pieces[5:25], pieces[25:])
+    ]
+    operator = dot(fixed[PLACE_A], pieces[0]) + dot(fixed[PLACE_B], pieces[1])
+    operator = operator + dot(fixed[PLACE_C, 0:160], pieces[2])
     operator_high, operator_low = split(operator)
-    operator_rows = dot_nt(twice[...], operator_high) + dot_nt(twice[...], operator_low)
+    twice = fixed[TWICE, 0:128]
+    operator_rows = dot_nt(twice, operator_high) + dot_nt(twice, operator_low)
     residual = source[...] - (pseudo[...] * u + operator_rows)
     residual_out[...] = residual
 
     high, low = split(residual)
-    turned = dot_nt(eye[...], jnp.concatenate([high, low], axis=0))
+    turned = dot_nt(fixed[EYE], jnp.concatenate([high, low], axis=0))
     turned_out[...] = turned + roll(turned, 64)
     turned = turned.astype(BF16)
-    wide_lane = lanes((320, 128)) % 64
-    direct = jnp.zeros((320, 128), F32)
-    for line in range(LINES):
-        applied = dot(inverse_high[line], turned) + dot(inverse_low[line], turned)
-        direct = jnp.where(wide_lane // 8 == line, applied, direct)
-    direct = direct + roll(direct, 64)
-    traces = dot(layers[...], pair_lanes(direct))
+    trace_lane = lanes((160, 128))
+    traces = jnp.zeros((160, 128), F32)
+    for line in range(LINES):
+        applied = dot(rows_high[line], turned) + dot(rows_low[line], turned)
+        traces = jnp.where(trace_lane % 64 // 8 == line, applied, traces)
     traces = traces + roll(traces, 64)
 
-    trace_lane = lanes((160, 128))
     small_lane, small_row = lanes((80, 128)), rows((80, 128))
     for line in range(LINES):
         moved = roll(traces, 80 - 8 * line)
@@ -309,9 +369,8 @@
     def forward(k, carry):
         mine = small_lane == 80 + k
         for line in range(LINES):
-            at = (line * SEG + k) * 50
             z = jnp.concatenate(
-                mix(lambda w, v: span_scalars[at + w * 5 + v], slabs_of(t_state[line], 16)),
+                mix(lambda w, v: wide[line, k, pl.ds((w * 5 + v) * 2, 1)], slabs_of(t_state[line], 16)),
                 axis=0,
             )
             z_hi, z_lo = split(z)
@@ -327,10 +386,18 @@
     def backward(step, carry):
         k = SEG - 1 - step
         for line in range(LINES):
-            at = (line * SEG + k) * 50 + 25
             z = jnp.concatenate(
-                mix(lambda w, v: span_scalars[at + w * 5 + v], slabs_of(w_state[line], 16)),
-                axis=0,
+                [
+                    jnp.concatenate(
+                        mix(
+                            lambda w, v: wide[line, k, pl.ds((w * 5 + v) * 2 + 1, 1)],
+                            slabs_of(w_state[line, :, half], 16),
+                        ),
+                        axis=0,
+                    )
+                    for half in (slice(0, 128), slice(128, 256))
+                ],
+                axis=1,
             )
             z_hi, z_lo = split(z)
             v_high[line, k] = z_hi
@@ -376,13 +443,16 @@
         w0 = jnp.concatenate([y0, zero], axis=0)
         w1 = jnp.concatenate([y1, zero], axis=0)
     second = w1[:80] + roll(last, 33)
-    for copy in range(whole_out.shape[0]):
-        whole_out[copy, :, 0:128] = w0[:80]
-        whole_out[copy, :, 128:256] = second
-
-
-def solve_kernel(flags, wholes, t_in, w_in, out):
-    groups = wholes.shape[0]
+    whole_out[:, 0:128] = w0[:80]
+    whole_out[:, 128:256] = second
+
+
+def solve_kernel(*refs):
+    *parts, t_in, w_in, out, wholes = refs
+    groups = len(parts)
+    mine = lax.axis_index("span") // SEG
+    for distance, part in enumerate(parts):
+        wholes[lax.rem(mine - distance + groups, groups)] = part[...]
     lane = lanes((80, 128))
     tall_row = rows((128, 128))
     one = jnp.where(tall_row == 80, 1.0, 0.0)
@@ -405,7 +475,6 @@
         y = dot(left_cat(parts[group][1]), right_cat(traces[group]))
         y = y + dot(left_cat(parts[group][2]), right_cat(backs[0]))
         backs.insert(0, jnp.concatenate([y, zero], axis=0))
-    mine = flags[4]
     trace, back = traces[0], backs[0]
     for group in range(1, groups):
         trace = jnp.where(mine == group, traces[group], trace)
@@ -424,8 +493,8 @@
         c_row = roll(dot_nt(y_cat, jnp.concatenate([high, low, high], axis=1)), 88)
         first = jnp.where(line_lane < 80, t_row, jnp.where(line_lane < 88, 1.0, c_row))
         second = jnp.where(line_lane < 40, c_row, 0.0)
-        out[e : e + 1, 0:128] = first[0:1]
-        out[e : e + 1, 128:256] = second[0:1]
+        out[e, :, 0:128] = first
+        out[e, :, 128:256] = second
 
 
 def finish_kernel(
@@ -438,13 +507,10 @@
     inverse_high,
     inverse_low,
     flow,
-    spread,
-    twice,
+    fixed,
     out,
 ):
-    y = incoming[...]
-    y = jnp.broadcast_to(y[:, None, :], (8, 8, 256)).reshape(64, 256)
-    high, low = split(y)
+    high, low = split(incoming[...].reshape(64, 256))
     y = jnp.concatenate([high, low], axis=0)
     small_lane = lanes((80, 128)) % 64
     lower = jnp.zeros((80, 128), F32)
@@ -460,7 +526,7 @@
             upper = jnp.where(mine, d[80 * k : 80 * k + 80], upper)
     both = jnp.concatenate([lower, upper], axis=0)
     both = both + roll(both, 64)
-    added = dot(spread[...], pair_lanes(both))
+    added = dot(fixed[SPREAD, 0:160], pair_lanes(both))
     load = pair_lanes(turned[...] + added + roll(added, 64))
     wide_lane = lanes((320, 128)) % 64
     total = jnp.zeros((320, 128), F32)
@@ -468,24 +534,25 @@
         applied = dot(inverse_high[line], load) + dot(inverse_low[line], load)
         total = jnp.where(wide_lane // 8 == line, applied, total)
     high, low = split(total)
-    out[...] = flow[...] + dot_nt(twice[...], high) + dot_nt(twice[...], low)
-
-
-def call(kernel, out_shape, in_specs, scratch=(), flops=0, moved=0, name=None):
+    twice = fixed[TWICE, 0:128]
+    out[...] = flow[...] + dot_nt(twice, high) + dot_nt(twice, low)
+
+
+def call(kernel, out_shape, in_specs, scratch=(), limit=16, flops=0, moved=0, name=None):
     return pl.pallas_call(
         kernel,
         out_shape=out_shape,
         in_specs=in_specs,
         out_specs=jax.tree.map(lambda _: pl.BlockSpec(memory_space=pltpu.VMEM), out_shape),
         scratch_shapes=list(scratch),
-        compiler_params=pltpu.CompilerParams(vmem_limit_bytes=VMEM_LIMIT),
+        compiler_params=pltpu.CompilerParams(vmem_limit_bytes=limit * 1024 * 1024),
         cost_estimate=pl.CostEstimate(flops=flops, bytes_accessed=moved, transcendentals=0),
         name=name,
     )
 
 
 VM = pl.BlockSpec(memory_space=pltpu.VMEM)
-SM = pl.BlockSpec(memory_space=pltpu.SMEM)
+HBM = pl.BlockSpec(memory_space=pl.ANY)
 
 
 def shape(*dims, dtype=F32):
@@ -503,59 +570,54 @@
     mirror_face,
     edge_flip,
 ):
-    const = {name: jnp.asarray(value) for name, value in constants().items()}
-    span_size, gx_size, gy_size = (lax.axis_size(a) for a in ("span", "gx", "gy"))
-    groups = span_size // SEG
-    span_at, gx_at, gy_at = (lax.axis_index(a) for a in ("span", "gx", "gy"))
-    flags = jnp.stack(
-        [
-            (gx_at > 0).astype(jnp.int32),
-            (gx_at < gx_size - 1).astype(jnp.int32),
-            (gy_at > 0).astype(jnp.int32),
-            (gy_at < gy_size - 1).astype(jnp.int32),
-            (span_at // SEG).astype(jnp.int32),
-        ]
-    )
+    early, fixed = (jnp.asarray(value) for value in constants())
+    groups = lax.axis_size("span") // SEG
 
     def ring(value, axis, step):
         count = lax.axis_size(axis)
         return lax.ppermute(value, axis, [(i, (i + step) % count) for i in range(count)])
 
+    flow = flow_state.reshape(64, 320)
+    plane, up, down, last, first = call(
+        pack_kernel,
+        (shape(16, 320), shape(32, 320), shape(32, 320), shape(8, 320), shape(8, 320)),
+        [VM],
+        limit=4,
+        name="pack",
+    )(flow)
     with jax.named_scope("halo"):
-        gx_high = ring(flow_state[0], "gx", -1).reshape(16, 320)
-        gx_low = ring(flow_state[3], "gx", 1).reshape(16, 320)
-        gy_low = ring(flow_state[:, 1], "gy", 1).reshape(32, 320)
-        gy_high = ring(flow_state[:, 0], "gy", -1).reshape(32, 320)
-        below = ring(flow_state[:, :, SEG - 1], "span", 1).reshape(8, 320)
-        above = ring(flow_state[:, :, 0], "span", -1).reshape(8, 320)
-
-    with jax.named_scope("tables"):
-        turn = lambda x: jnp.moveaxis(x.reshape(64, -1), 0, 1).astype(F32)
-        tables = jnp.concatenate(
-            [
-                turn(x)
-                for x in (volume_jacobian, side_jacobian, span_jacobian, mirror_face, edge_flip)
-            ],
-            axis=0,
-        )
-        tables = jnp.pad(tables, ((0, 0), (0, 64)))
-        span_scalars = (LIFT * span_jacobian).reshape(3200)
-
-    flow = flow_state.reshape(64, 320)
+        below, above = ring(last, "span", 1), ring(first, "span", -1)
+        gy_low, gy_high = ring(up, "gy", 1), ring(down, "gy", -1)
+        plane = ring(plane, "gx", 1)
+
     inverse = line_inverse.reshape(LINES, 320, 320)
-    inverse_high, inverse_low, fwd, bwd = call(
+    inverse_high, inverse_low, rows_high, rows_low, fwd, bwd, tables, wide = call(
         prepare_kernel,
         (
             shape(LINES, 320, 320, dtype=BF16),
             shape(LINES, 320, 320, dtype=BF16),
+            shape(LINES, 160, 320, dtype=BF16),
+            shape(LINES, 160, 320, dtype=BF16),
             shape(LINES, 160, 256, dtype=BF16),
             shape(LINES, 80, 256, dtype=BF16),
+            shape(248, 128),
+            shape(LINES, SEG, 50, 128),
         ),
-        [VM] * 4,
+        [HBM] + [VM] * 6,
+        scratch=[pltpu.VMEM((LINES, 320, 320), F32), pltpu.SemaphoreType.DMA((LINES,))],
+        limit=24,
         flops=4_000_000_000,
         moved=8_000_000,
         name="prepare",
-    )(inverse, const["columns_high"], const["columns_low"], const["layers"])
+    )(
+        inverse,
+        early,
+        volume_jacobian.transpose(0, 3, 4, 5, 1, 2).reshape(4, 75, 2, SEG),
+        side_jacobian.transpose(0, 1, 4, 5, 3, 2).reshape(LINES, 25, 4, SEG),
+        span_jacobian.transpose(0, 1, 4, 5, 3, 2).reshape(LINES, 25, 2, SEG),
+        mirror_face.transpose(0, 1, 3, 2).reshape(LINES, 4, SEG),
+        edge_flip.transpose(0, 1, 3, 2).reshape(LINES, 4, SEG),
+    )
 
     residual, turned, maps, z_high, z_low, v_high, v_low = call(
         sweep_kernel,
@@ -568,7 +630,7 @@
             shape(LINES, SEG, 80, 256, dtype=BF16),
             shape(LINES, SEG, 80, 256, dtype=BF16),
         ),
-        [SM, SM] + [VM] * 20,
+        [VM] * 15,
         scratch=[
             pltpu.VMEM((256, 320), F32),
             pltpu.VMEM((192, 640), F32),
@@ -577,15 +639,13 @@
             pltpu.VMEM((LINES, 80, 256), F32),
             pltpu.VMEM((LINES, SEG, 80, 128), F32),
         ],
+        limit=28,
         flops=10_000_000_000,
         moved=20_000_000,
         name="sweep",
     )(
-        flags,
-        span_scalars,
         flow,
-        gx_low,
-        gx_high,
+        plane,
         gy_low,
         gy_high,
         below,
@@ -593,48 +653,39 @@
         source_term.reshape(64, 320),
         pseudo_time.reshape(64, 320),
         tables,
-        inverse_high,
-        inverse_low,
+        wide,
+        rows_high,
+        rows_low,
         fwd,
         bwd,
-        const["select"],
-        const["place"],
-        const["layers"],
-        const["along"],
-        const["twice"],
-        const["eye"],
+        fixed,
     )
 
     within = [[SEG * g + m for m in range(SEG)] for g in range(groups)]
-    across = [[SEG * g + m for g in range(groups)] for m in range(SEG)]
-
-    def exchange(value, members):
-        return lax.all_to_all(value, "span", 0, 0, axis_index_groups=members, tiled=True)
-
-    maps = exchange(maps, within)
+
+    def exchange(value):
+        return lax.all_to_all(value, "span", 0, 0, axis_index_groups=within, tiled=True)
+
+    maps = exchange(maps)
     t_maps, w_maps, whole = call(
         compose_kernel,
-        (shape(SEG, 128, 128), shape(SEG, 128, 256), shape(groups, 80, 256)),
+        (shape(SEG, 128, 128), shape(SEG, 128, 256), shape(80, 256)),
         [VM],
+        limit=8,
         name="compose",
     )(maps)
-    wholes = exchange(whole, across)
-    answers = call(solve_kernel, shape(SEG, 256), [SM] + [VM] * 3, name="solve")(
-        flags, wholes, t_maps, w_maps
-    )
-    incoming = exchange(answers, within)
-    updated = call(finish_kernel, shape(64, 320), [VM] * 11, name="finish")(
-        incoming,
-        z_high,
-        z_low,
-        v_high,
-        v_low,
-        turned,
-        inverse_high,
-        inverse_low,
-        flow,
-        const["spread"],
-        const["twice"],
+    wholes = [whole] + [ring(whole, "span", SEG * distance) for distance in range(1, groups)]
+    answers = call(
+        solve_kernel,
+        shape(SEG, 8, 256),
+        [VM] * (groups + 2),
+        scratch=[pltpu.VMEM((groups, 80, 256), F32)],
+        limit=8,
+        name="solve",
+    )(*wholes, t_maps, w_maps)
+    incoming = exchange(answers)
+    updated = call(finish_kernel, shape(64, 320), [VM] * 10, limit=20, name="finish")(
+        incoming, z_high, z_low, v_high, v_low, turned, inverse_high, inverse_low, flow, fixed
     )
     return updated.reshape(flow_state.shape), residual.reshape(flow_state.shape)
 

time: 111 us -> 88.4 us (0.80)
  blocking collectives: 47.1 us -> 29.7 us
  Pallas kernels: 45.7 us -> 30.4 us
  starting transfers between devices: 5.95 us -> 13.1 us
  waiting for transfers between devices: 0.02 us -> 5.15 us
  local copies, waits for them, and re-layouts: 10.6 us -> 8.49 us
    all_to_all x3 -> x2, blocking collectives: 47.1 us -> 29.7 us  [exchange(): lax.all_to_all(value, 'span', 0, 0, axis_index_groups=within, tiled=True)]
    pallas_call x3 -> x4, Pallas kernels: 18.1 us -> 9.51 us  [the longest x1 4.97 us: on_device(): call(finish_kernel, shape(64, 320), [VM] * 10, limit=20, name='finish')]
    pallas_call x1, Pallas kernels: 18.9 us -> 11.3 us  [on_device(): call(sweep_kernel, (shape(64, 320), shape(320, 128), shape(LINES, 80, 256...]
    ppermute x6 -> x8, starting transfers between devices: 5.95 us -> 13.1 us  [ring(): lax.ppermute(value, axis, [(i, (i + step) % count) for i in range(count)])]
    unnamed x24, local copies, waits for them, and re-layouts: 1.67 us -> 8.49 us
    ppermute x6 -> x8, waiting for transfers between devices: 0.02 us -> 5.15 us  [ring(): lax.ppermute(value, axis, [(i, (i + step) % count) for i in range(count)])]
    reshape x6 -> x0, local copies, waits for them, and re-layouts: 3.13 us -> none  [the longest x3 1.11 us: on_device(): turn = lambda x: jnp.moveaxis(x.reshape(64, -1), 0, 1).astype(F32)]
    squeeze x2 -> x0, local copies, waits for them, and re-layouts: 1.59 us -> none  [the longest x1 0.83 us: on_device(): gy_high = ring(flow_state[:, 0], 'gy', -1).reshape(32, 320)]
  transfers between devices with their start and end apart: 6 -> 8, of which waited for: 0 -> 2; matrix products, arithmetic and copies ran while one was open for 7% -> 0% of each run, Pallas kernels for 8% -> 11%
where the time goes in v2:
time: 88.4 us; the launch traced here: 87.6 us
  Pallas kernels  30.4 us (34%)
  blocking collectives  29.7 us (34%)
  starting transfers between devices  13.1 us (15%)
  local copies, waits for them, and re-layouts  8.49 us (10%)
  waiting for transfers between devices  5.15 us (6%)
    all_to_all x2, blocking collectives, exchange(): lax.all_to_all(value, 'span', 0, 0, axis_index_groups=within, tiled=True)  29.7 us
    ppermute x8, starting transfers between devices, ring(): lax.ppermute(value, axis, [(i, (i + step) % count) for i in range(count)])  13.1 us
    pallas_call x1, Pallas kernels, on_device(): call(sweep_kernel, (shape(64, 320), shape(320, 128), shape(LINES, 80, 256...  11.3 us
    pallas_call x1, Pallas kernels, on_device(): call(prepare_kernel, (shape(LINES, 320, 320, dtype=BF16), shape(LINES, 32...  9.63 us
    unnamed x24, local copies, waits for them, and re-layouts  8.49 us
    ppermute x8, waiting for transfers between devices, ring(): lax.ppermute(value, axis, [(i, (i + step) % count) for i in range(count)])  5.15 us
    pallas_call x1, Pallas kernels, on_device(): call(finish_kernel, shape(64, 320), [VM] * 10, limit=20, name='finish')  4.97 us
    pallas_call x1, Pallas kernels, on_device(): call(compose_kernel, (shape(SEG, 128, 128), shape(SEG, 128, 256), shape(8...  2.47 us
  transfers between devices with their start and end apart: 8, of which 2 were waited for; matrix products, arithmetic and copies ran while one was open for 0% of the time, Pallas kernels for 11%

profile of v2, /device:TPU:2, one launch (start us, length us, event | category | flops | bytes accessed | tf_op | source)
XLA Modules:
  0.0 87.6 jit_solution(7803888907454928942)
XLA Ops:
  0.6 0.0 copy-start.1
  0.6 0.9 %copy-done.1 = f32[4,2,8,320]{3,2,1,0:T(8,128)S(1)} copy-done((f32[4,2,8,320]{3,2,1,0:T(8,128)S(1)}, f32[4,2,8,320]{3,2,1,0:T(8,128)}, u32[]{:S(2)}) %copy-start.1) | copy-done | bytes 81944
  1.6 1.6 %collective-permute-start.3 = (f32[8,320]{1,0:T(8,128)S(1)}, f32[8,320]{1,0:T(8,128)S(1)}, u32[]{:S(2)}, u32[]{:S(2)}) collective-permute-start(f32[8,320]{1,0:T(8,128)S(1)} %get-tuple-element.28), channel_id=1, source_target_pairs={{0,8},{8,16},{16,24},{24,32},{32,40},{40,48},{48,56},{56,64},{64,7... | collective-permute-start | bytes 30728 | tf_op jit(solution)/shard_map/halo/ppermute | solution.py:578
  3.1 0.9 collective-permute-start.4
  4.0 0.0 collective-permute-start
  4.0 1.2 %collective-permute-start.1 = (f32[32,320]{1,0:T(8,128)S(1)}, f32[32,320]{1,0:T(8,128)S(1)}, u32[]{:S(2)}, u32[]{:S(2)}) collective-permute-start(f32[32,320]{1,0:T(8,128)S(1)} %get-tuple-element.26), channel_id=1, source_target_pairs={{0,1},{1,2},{2,3},{3,0},{4,5},{5,6},{6,7},{7,4},{8,9},{9,10},{10,1... | collective-permute-start | bytes 122888 | tf_op jit(solution)/shard_map/halo/ppermute | solution.py:578
  5.2 2.0 %collective-permute-start.2 = (f32[32,320]{1,0:T(8,128)S(1)}, f32[32,320]{1,0:T(8,128)S(1)}, u32[]{:S(2)}, u32[]{:S(2)}) collective-permute-start(f32[32,320]{1,0:T(8,128)S(1)} %get-tuple-element.27), channel_id=1, source_target_pairs={{0,3},{1,0},{2,1},{3,2},{4,7},{5,4},{6,5},{7,6},{8,11},{9,8},{10,9... | collective-permute-start | bytes 122888 | tf_op jit(solution)/shard_map/halo/ppermute | solution.py:578
  7.2 0.0 copy-start.3
  7.2 2.1 %copy-done.3 = f32[4,2,320,320]{3,2,1,0:T(8,128)S(1)} copy-done((f32[4,2,320,320]{3,2,1,0:T(8,128)S(1)}, f32[4,2,320,320]{3,2,1,0:T(8,128)}, u32[]{:S(2)}) %copy-start.3) | copy-done | bytes 3276824
  9.3 0.0 copy-start.4
  9.3 1.0 %copy-done.4 = f32[4,2,8,4,5,5]{2,3,5,4,1,0:T(4,128)S(1)} copy-done((f32[4,2,8,4,5,5]{2,3,5,4,1,0:T(4,128)S(1)}, f32[4,2,8,4,5,5]{2,3,5,4,1,0:T(4,128)}, u32[]{:S(2)}) %copy-start.4) | copy-done | bytes 25624
  10.3 0.0 copy-start.5
  10.3 1.0 %copy-done.5 = f32[4,2,8,3,5,5]{2,1,5,4,3,0:T(2,128)S(1)} copy-done((f32[4,2,8,3,5,5]{2,1,5,4,3,0:T(2,128)S(1)}, f32[4,2,8,3,5,5]{2,1,5,4,3,0:T(2,128)}, u32[]{:S(2)}) %copy-start.5) | copy-done | bytes 19224
  11.3 0.0 copy-start.6
  11.3 0.9 %copy-done.6 = f32[4,2,8,2,5,5]{2,3,5,4,1,0:T(2,128)S(1)} copy-done((f32[4,2,8,2,5,5]{2,3,5,4,1,0:T(2,128)S(1)}, f32[4,2,8,2,5,5]{2,3,5,4,1,0:T(2,128)}, u32[]{:S(2)}) %copy-start.6) | copy-done | bytes 12824
  12.2 0.0 copy-start.9
  12.2 0.7 copy-done.9
  13.0 0.0 copy-start.10
  13.0 0.7 copy-done.10
  13.7 0.0 copy-start.11
  13.7 1.1 %copy-done.11 = bf16[800,512]{1,0:T(8,128)(2,1)S(1)} copy-done((bf16[800,512]{1,0:T(8,128)(2,1)S(1)}, bf16[800,512]{1,0:T(8,128)(2,1)}, u32[]{:S(2)}) %copy-start.11) | copy-done | bytes 819224
  14.8 0.0 copy-start
  14.8 0.0 copy-start.2
  14.8 0.0 copy-start.7
  14.8 0.0 copy-start.8
  14.8 9.6 %prepare.1 = (bf16[8,320,320]{2,1,0:T(8,128)(2,1)S(1)}, bf16[8,320,320]{2,1,0:T(8,128)(2,1)S(1)}, bf16[8,160,320]{2,1,0:T(8,128)(2,1)S(1)}, bf16[8,160,320]{2,1,...) custom-call(f32[8,320,320]{2,1,0:T(8,128)S(1)} %bitcast.24, ...), custom_call_target="tpu_custom_call" | custom-call | flops 4000000000 | bytes 8000000 | tf_op jit(solution)/shard_map/prepare/pallas_call | solution.py:594
  24.5 0.0 collective-permute-done.3.below
  24.5 0.0 collective-permute-done.4.above
  24.5 0.0 collective-permute-done.plane
  24.5 0.0 collective-permute-done.1.gy_low
  24.5 0.0 collective-permute-done.2.gy_high
  24.5 0.0 copy-done
  24.5 0.0 copy-done.2
  24.5 0.0 copy-done.7
  24.6 0.0 copy-done.8
  24.6 11.3 %sweep.1 = (f32[64,320]{1,0:T(8,128)}, f32[320,128]{1,0:T(8,128)S(1)}, f32[8,80,256]{2,1,0:T(8,128)S(1)}, bf16[8,8,80,128]{3,2,1,0:T(8,128)(2,1)S(1)}, bf16[8,8,...) custom-call(f32[64,320]{1,0:T(8,128)S(1)} %bitcast.22, ...), custom_call_target="tpu_custom_call" | custom-call | flops 10000000000 | bytes 20000000 | tf_op jit(solution)/shard_map/sweep/pallas_call | solution.py:622
  35.8 19.1 %all_to_all.10.maps = f32[8,80,256]{2,1,0:T(8,128)S(1)} all-to-all(f32[8,80,256]{2,1,0:T(8,128)S(1)} %get-tuple-element.36), channel_id=1, replica_groups={{0,8,16,24,32,40,48,56},{64,72,80,88,96,104,112,120},{128,136,144,152,1..., dimensions={0} | all-to-all | bytes 1310720 | tf_op jit(solution)/shard_map/all_to_all | solution.py:667
  55.0 2.5 %compose.1 = (f32[8,128,128]{2,1,0:T(8,128)S(1)}, f32[8,128,256]{2,1,0:T(8,128)S(1)}, f32[80,256]{1,0:T(8,128)S(1)}) custom-call(f32[8,80,256]{2,1,0:T(8,128)S(1)} %all_to_all.10.maps), custom_call_target="tpu_custom_call" | custom-call | tf_op jit(solution)/shard_map/compose/pallas_call | solution.py:670
  57.4 2.4 %collective-permute-start.7 = (f32[80,256]{1,0:T(8,128)S(1)}, f32[80,256]{1,0:T(8,128)S(1)}, u32[]{:S(2)}, u32[]{:S(2)}) collective-permute-start(f32[80,256]{1,0:T(8,128)S(1)} %get-tuple-element.37.refs_0_), channel_id=1, source_target_pairs={{0,192},{8,200},{16,208},{24,216},{32,224},{40,232},{48,240},{56,2... | collective-permute-start | bytes 245768 | tf_op jit(solution)/shard_map/ppermute | solution.py:578
  59.8 2.2 %collective-permute-start.6 = (f32[80,256]{1,0:T(8,128)S(1)}, f32[80,256]{1,0:T(8,128)S(1)}, u32[]{:S(2)}, u32[]{:S(2)}) collective-permute-start(f32[80,256]{1,0:T(8,128)S(1)} %get-tuple-element.37.refs_0_), channel_id=1, source_target_pairs={{0,128},{8,136},{16,144},{24,152},{32,160},{40,168},{48,176},{56,1... | collective-permute-start | bytes 245768 | tf_op jit(solution)/shard_map/ppermute | solution.py:578
  62.0 2.8 %collective-permute-start.5 = (f32[80,256]{1,0:T(8,128)S(1)}, f32[80,256]{1,0:T(8,128)S(1)}, u32[]{:S(2)}, u32[]{:S(2)}) collective-permute-start(f32[80,256]{1,0:T(8,128)S(1)} %get-tuple-element.37.refs_0_), channel_id=1, source_target_pairs={{0,64},{8,72},{16,80},{24,88},{32,96},{40,104},{48,112},{56,120},{... | collective-permute-start | bytes 245768 | tf_op jit(solution)/shard_map/ppermute | solution.py:578
  64.8 0.0 collective-permute-done.7.refs_3_
  64.8 4.3 %collective-permute-done.6.refs_2_ = f32[80,256]{1,0:T(8,128)S(1)} collective-permute-done((f32[80,256]{1,0:T(8,128)S(1)}, f32[80,256]{1,0:T(8,128)S(1)}, u32[]{:S(2)}, u32[]{:S(2)}) %collective-permute-start.6) | collective-permute-done | bytes 81952 | tf_op jit(solution)/shard_map/ppermute | solution.py:578
  69.2 0.8 collective-permute-done.5.refs_1_
  70.0 2.0 %solve.1 = f32[8,8,256]{2,1,0:T(8,128)S(1)} custom-call(f32[80,256]{1,0:T(8,128)S(1)} %get-tuple-element.37.refs_0_, f32[80,256]{1,0:T(8,128)S(1)} %collective-permute-done.5.refs_1_, f32[80,256]{1,0:T(8,128)S(1)} %collective-permute-done.6.refs_2_, f32[80,256]{1,0:T(8,128)S(1)} %collective-permute-done.7.refs_3_, ...), custom_call_target="tpu_custom_call" | custom-call | tf_op jit(solution)/shard_map/solve/pallas_call | solution.py:678
  72.0 10.6 %all_to_all.11.incoming = f32[8,8,256]{2,1,0:T(8,128)S(1)} all-to-all(f32[8,8,256]{2,1,0:T(8,128)S(1)} %solve.1), channel_id=1, replica_groups={{0,8,16,24,32,40,48,56},{64,72,80,88,96,104,112,120},{128,136,144,152,1..., dimensions={0} | all-to-all | bytes 131072 | tf_op jit(solution)/shard_map/all_to_all | solution.py:667
  82.6 5.0 %finish.1 = f32[64,320]{1,0:T(8,128)} custom-call(f32[8,8,256]{2,1,0:T(8,128)S(1)} %all_to_all.11.incoming, bf16[8,8,80,128]{3,2,1,0:T(8,128)(2,1)S(1)} %get-tuple-element.40.z_high, bf16[8,8,80,128]{3,2,1,0:T(8,128)(2,1)S(1)} %get-tuple-element.41.z_low, bf16[8,8,80,256]{3,2,1,0:T(8,128)(2,1)S(1)} %get-tuple-element.42.v_high, ...), custom_call_target="tpu_custom_call" | custom-call | tf_op jit(solution)/shard_map/finish/pallas_call | solution.py:687
  (1 shorter events, 0.0 us)
Async XLA Ops:
  0.6 0.9 %copy-start.1 = (f32[4,2,8,320]{3,2,1,0:T(8,128)S(1)}, f32[4,2,8,320]{3,2,1,0:T(8,128)}, u32[]{:S(2)}) copy-start(f32[4,2,8,320]{3,2,1,0:T(8,128)} %param.11) | copy-start | bytes 245764
  1.6 22.9 %collective-permute-start.3 = (f32[8,320]{1,0:T(8,128)S(1)}, f32[8,320]{1,0:T(8,128)S(1)}, u32[]{:S(2)}, u32[]{:S(2)}) collective-permute-start(f32[8,320]{1,0:T(8,128)S(1)} %get-tuple-element.28), channel_id=1, source_target_pairs={{0,8},{8,16},{16,24},{24,32},{32,40},{40,48},{48,56},{56,64},{64,7... | collective-permute-start | bytes 30728 | tf_op jit(solution)/shard_map/halo/ppermute | solution.py:578
  3.1 21.4 %collective-permute-start.4 = (f32[8,320]{1,0:T(8,128)S(1)}, f32[8,320]{1,0:T(8,128)S(1)}, u32[]{:S(2)}, u32[]{:S(2)}) collective-permute-start(f32[8,320]{1,0:T(8,128)S(1)} %get-tuple-element.29), channel_id=1, source_target_pairs={{0,248},{8,0},{16,8},{24,16},{32,24},{40,32},{48,40},{56,48},{64,5... | collective-permute-start | bytes 30728 | tf_op jit(solution)/shard_map/halo/ppermute | solution.py:578
  4.0 20.5 %collective-permute-start = (f32[16,320]{1,0:T(8,128)S(1)}, f32[16,320]{1,0:T(8,128)S(1)}, u32[]{:S(2)}, u32[]{:S(2)}) collective-permute-start(f32[16,320]{1,0:T(8,128)S(1)} %get-tuple-element.25), channel_id=1, source_target_pairs={{0,4},{4,0},{1,5},{5,1},{2,6},{6,2},{3,7},{7,3},{8,12},{12,8},{9,1... | collective-permute-start | bytes 61448 | tf_op jit(solution)/shard_map/halo/ppermute | solution.py:578
  4.0 20.5 %collective-permute-start.1 = (f32[32,320]{1,0:T(8,128)S(1)}, f32[32,320]{1,0:T(8,128)S(1)}, u32[]{:S(2)}, u32[]{:S(2)}) collective-permute-start(f32[32,320]{1,0:T(8,128)S(1)} %get-tuple-element.26), channel_id=1, source_target_pairs={{0,1},{1,2},{2,3},{3,0},{4,5},{5,6},{6,7},{7,4},{8,9},{9,10},{10,1... | collective-permute-start | bytes 122888 | tf_op jit(solution)/shard_map/halo/ppermute | solution.py:578
  5.2 19.3 %collective-permute-start.2 = (f32[32,320]{1,0:T(8,128)S(1)}, f32[32,320]{1,0:T(8,128)S(1)}, u32[]{:S(2)}, u32[]{:S(2)}) collective-permute-start(f32[32,320]{1,0:T(8,128)S(1)} %get-tuple-element.27), channel_id=1, source_target_pairs={{0,3},{1,0},{2,1},{3,2},{4,7},{5,4},{6,5},{7,6},{8,11},{9,8},{10,9... | collective-permute-start | bytes 122888 | tf_op jit(solution)/shard_map/halo/ppermute | solution.py:578
  7.2 2.1 %copy-start.3 = (f32[4,2,320,320]{3,2,1,0:T(8,128)S(1)}, f32[4,2,320,320]{3,2,1,0:T(8,128)}, u32[]{:S(2)}) copy-start(f32[4,2,320,320]{3,2,1,0:T(8,128)} %param.17) | copy-start | bytes 9830404
  9.3 1.0 %copy-start.4 = (f32[4,2,8,4,5,5]{2,3,5,4,1,0:T(4,128)S(1)}, f32[4,2,8,4,5,5]{2,3,5,4,1,0:T(4,128)}, u32[]{:S(2)}) copy-start(f32[4,2,8,4,5,5]{2,3,5,4,1,0:T(4,128)} %param.15) | copy-start | bytes 76804
  10.3 1.0 %copy-start.5 = (f32[4,2,8,3,5,5]{2,1,5,4,3,0:T(2,128)S(1)}, f32[4,2,8,3,5,5]{2,1,5,4,3,0:T(2,128)}, u32[]{:S(2)}) copy-start(f32[4,2,8,3,5,5]{2,1,5,4,3,0:T(2,128)} %param.14) | copy-start | bytes 57604
  11.3 0.9 %copy-start.6 = (f32[4,2,8,2,5,5]{2,3,5,4,1,0:T(2,128)S(1)}, f32[4,2,8,2,5,5]{2,3,5,4,1,0:T(2,128)}, u32[]{:S(2)}) copy-start(f32[4,2,8,2,5,5]{2,3,5,4,1,0:T(2,128)} %param.16) | copy-start | bytes 38404
  12.2 0.7 copy-start.9
  13.0 0.7 copy-start.10
  13.7 1.1 %copy-start.11 = (bf16[800,512]{1,0:T(8,128)(2,1)S(1)}, bf16[800,512]{1,0:T(8,128)(2,1)}, u32[]{:S(2)}) copy-start(bf16[800,512]{1,0:T(8,128)(2,1)} %constant.4.clone.early) | copy-start | bytes 2457604
  14.8 9.7 %copy-start = (bf16[2912,320]{1,0:T(8,128)(2,1)S(1)}, bf16[2912,320]{1,0:T(8,128)(2,1)}, u32[]{:S(2)}) copy-start(bf16[2912,320]{1,0:T(8,128)(2,1)} %constant.5.clone.fixed) | copy-start | bytes 5591044
  14.8 9.7 %copy-start.2 = (f32[4,2,8,320]{3,2,1,0:T(8,128)S(1)}, f32[4,2,8,320]{3,2,1,0:T(8,128)}, u32[]{:S(2)}) copy-start(f32[4,2,8,320]{3,2,1,0:T(8,128)} %param.11) | copy-start | bytes 245764
  14.8 9.7 %copy-start.7 = (f32[4,2,8,320]{3,2,1,0:T(8,128)S(1)}, f32[4,2,8,320]{3,2,1,0:T(8,128)}, u32[]{:S(2)}) copy-start(f32[4,2,8,320]{3,2,1,0:T(8,128)} %param.12) | copy-start | bytes 245764
  14.8 9.7 %copy-start.8 = (f32[4,2,8,320]{3,2,1,0:T(8,128)S(1)}, f32[4,2,8,320]{3,2,1,0:T(8,128)}, u32[]{:S(2)}) copy-start(f32[4,2,8,320]{3,2,1,0:T(8,128)} %param.13) | copy-start | bytes 245764
  57.4 7.4 %collective-permute-start.7 = (f32[80,256]{1,0:T(8,128)S(1)}, f32[80,256]{1,0:T(8,128)S(1)}, u32[]{:S(2)}, u32[]{:S(2)}) collective-permute-start(f32[80,256]{1,0:T(8,128)S(1)} %get-tuple-element.37.refs_0_), channel_id=1, source_target_pairs={{0,192},{8,200},{16,208},{24,216},{32,224},{40,232},{48,240},{56,2... | collective-permute-start | bytes 245768 | tf_op jit(solution)/shard_map/ppermute | solution.py:578
  59.8 9.4 %collective-permute-start.6 = (f32[80,256]{1,0:T(8,128)S(1)}, f32[80,256]{1,0:T(8,128)S(1)}, u32[]{:S(2)}, u32[]{:S(2)}) collective-permute-start(f32[80,256]{1,0:T(8,128)S(1)} %get-tuple-element.37.refs_0_), channel_id=1, source_target_pairs={{0,128},{8,136},{16,144},{24,152},{32,160},{40,168},{48,176},{56,1... | collective-permute-start | bytes 245768 | tf_op jit(solution)/shard_map/ppermute | solution.py:578
  62.0 8.0 %collective-permute-start.5 = (f32[80,256]{1,0:T(8,128)S(1)}, f32[80,256]{1,0:T(8,128)S(1)}, u32[]{:S(2)}, u32[]{:S(2)}) collective-permute-start(f32[80,256]{1,0:T(8,128)S(1)} %get-tuple-element.37.refs_0_), channel_id=1, source_target_pairs={{0,64},{8,72},{16,80},{24,88},{32,96},{40,104},{48,112},{56,120},{... | collective-permute-start | bytes 245768 | tf_op jit(solution)/shard_map/ppermute | solution.py:578

commit v3 on v2

--- a/solution.py
+++ b/solution.py
@@ -178,12 +178,12 @@
 
 def prepare_kernel(
     inverse,
-    early,
-    volume_jacobian,
-    side_jacobian,
-    span_jacobian,
-    mirror_face,
-    edge_flip,
+    early_in,
+    volume_in,
+    side_in,
+    span_in,
+    mirror_in,
+    flip_in,
     high_out,
     low_out,
     rows_high,
@@ -191,39 +191,52 @@
     fwd_out,
     bwd_out,
     tables,
-    wide,
     held,
+    early,
+    volume_jacobian,
+    side_jacobian,
+    span_jacobian,
+    mirror_face,
+    edge_flip,
     arrived,
 ):
+    pairs = [
+        (volume_in, volume_jacobian),
+        (side_in, side_jacobian),
+        (span_in, span_jacobian),
+        (mirror_in, mirror_face),
+        (flip_in, edge_flip),
+        (early_in, early),
+    ]
+    pairs += [(inverse.at[line], held.at[line]) for line in range(LINES)]
     copies = [
-        pltpu.make_async_copy(inverse.at[line], held.at[line], arrived.at[line])
-        for line in range(LINES)
+        pltpu.make_async_copy(source, target, arrived.at[at])
+        for at, (source, target) in enumerate(pairs)
     ]
     for copy in copies:
         copy.start()
+    for copy in copies[:6]:
+        copy.wait()
     for line in range(LINES):
         here = slice(8 * line, 8 * line + 8)
         tables[0:75, here] = volume_jacobian[line // 2, :, line % 2, :]
         tables[SIDE : SIDE + 100, here] = side_jacobian[line].reshape(100, 8)
-        span = LIFT * span_jacobian[line].reshape(50, 8)
-        tables[SPAN : SPAN + 50, here] = span
+        tables[SPAN : SPAN + 50, here] = LIFT * span_jacobian[line].reshape(50, 8)
         tables[MIRROR : MIRROR + 4, here] = mirror_face[line].astype(F32)
         tables[FLIP : FLIP + 4, here] = edge_flip[line].astype(F32)
-        for k in range(SEG):
-            wide[line, k] = jnp.broadcast_to(span[:, k : k + 1], (50, 128))
     for line in range(LINES):
-        copies[line].wait()
+        copies[6 + line].wait()
         high, low = split(held[line])
         high_out[line] = high
         low_out[line] = low
         layers = early[640:800, 0:320]
-        chosen_high = dot(layers, high).astype(BF16)
-        chosen_low = dot(layers, low).astype(BF16)
-        rows_high[line] = chosen_high
-        rows_low[line] = chosen_low
-        both = (dot(chosen_high, early[0:320]) + dot(chosen_low, early[320:640])).astype(BF16)
-        fwd_out[line] = both[:, :256]
-        bwd_out[line] = both[80:, 256:]
+        rows_high[line] = dot(layers, high).astype(BF16)
+        rows_low[line] = dot(layers, low).astype(BF16)
+    mine = lax.rem(lax.axis_index("span"), LINES)
+    both = dot(rows_high[mine], early[0:320]) + dot(rows_low[mine], early[320:640])
+    both = both.astype(BF16)
+    fwd_out[...] = both[:, :256]
+    bwd_out[...] = both[80:, 256:]
 
 
 def mix(coefficient, slabs):
@@ -250,25 +263,14 @@
     source,
     pseudo,
     tables,
-    wide,
     rows_high,
     rows_low,
-    fwd,
-    bwd,
     fixed,
     residual_out,
     turned_out,
-    maps_out,
-    z_high,
-    z_low,
-    v_high,
-    v_low,
+    sent_out,
     extended,
     flux,
-    started,
-    t_state,
-    w_state,
-    bottoms,
 ):
     gx_at, gy_at = lax.axis_index("gx"), lax.axis_index("gy")
     first_lo = (gx_at > 0).astype(F32)
@@ -359,61 +361,82 @@
         traces = jnp.where(trace_lane % 64 // 8 == line, applied, traces)
     traces = traces + roll(traces, 64)
 
+    sent = jnp.concatenate([traces, tables[SPAN : SPAN + 56], jnp.zeros((40, 128), F32)], axis=0)
+    sent_out[...] = jnp.transpose(sent)[:64]
+
+
+def maps_kernel(
+    received,
+    fwd,
+    bwd,
+    z_high,
+    z_low,
+    v_high,
+    v_low,
+    t_out,
+    w_out,
+    whole_out,
+    wide,
+    started,
+    t_state,
+    w_state,
+    bottoms,
+    maps,
+):
+    turned = jnp.transpose(jnp.concatenate([received[...], jnp.zeros((64, 256), F32)], axis=0))
+    jacobians = turned[160:210]
+    trace_lane = lanes((160, 128))
     small_lane, small_row = lanes((80, 128)), rows((80, 128))
-    for line in range(LINES):
-        moved = roll(traces, 80 - 8 * line)
-        started[line] = jnp.where((trace_lane >= 80) & (trace_lane < 88), moved, 0.0)
-        t_state[line] = jnp.where(small_lane == small_row, 1.0, 0.0)
-        w_state[line] = jnp.where(lanes((80, 256)) == rows((80, 256)) + 88, 1.0, 0.0)
+    for e in range(SEG):
+        for k in range(SEG):
+            at = e * SEG + k
+            wide[e, k] = jnp.broadcast_to(jacobians[:, at : at + 1], (50, 128))
+        moved = roll(turned[0:160], 80 - 8 * e)
+        started[e] = jnp.where((trace_lane >= 80) & (trace_lane < 88), moved, 0.0)
+        t_state[e] = jnp.where(small_lane == small_row, 1.0, 0.0)
+        w_state[e] = jnp.where(lanes((80, 256)) == rows((80, 256)) + 88, 1.0, 0.0)
+
+    def coupled(e, k, side, state):
+        out = mix(lambda w, v: wide[e, k, pl.ds((w * 5 + v) * 2 + side, 1)], slabs_of(state, 16))
+        return jnp.concatenate(out, axis=0)
 
     def forward(k, carry):
         mine = small_lane == 80 + k
-        for line in range(LINES):
-            z = jnp.concatenate(
-                mix(lambda w, v: wide[line, k, pl.ds((w * 5 + v) * 2, 1)], slabs_of(t_state[line], 16)),
-                axis=0,
-            )
-            z_hi, z_lo = split(z)
-            z_high[line, k] = z_hi
-            z_low[line, k] = z_lo
-            y = dot(fwd[line, :, 0:240], jnp.concatenate([z_hi, z_lo, z_hi], axis=0))
-            t_state[line] = y[:80] + jnp.where(mine, started[line, 0:80], 0.0)
-            bottoms[line, k] = y[80:] + jnp.where(mine, started[line, 80:160], 0.0)
+        for pair in range(0, SEG, 2):
+            cats = []
+            for e in (pair, pair + 1):
+                z_hi, z_lo = split(coupled(e, k, 0, t_state[e]))
+                z_high[e, k] = z_hi
+                z_low[e, k] = z_lo
+                cats.append(jnp.concatenate([z_hi, z_lo, z_hi], axis=0))
+            both = dot(fwd[:, 0:240], jnp.concatenate(cats, axis=1))
+            for e, y in ((pair, both[:, :128]), (pair + 1, both[:, 128:])):
+                t_state[e] = y[:80] + jnp.where(mine, started[e, 0:80], 0.0)
+                bottoms[e, k] = y[80:] + jnp.where(mine, started[e, 80:160], 0.0)
         return carry
 
     lax.fori_loop(0, SEG, forward, 0)
 
     def backward(step, carry):
         k = SEG - 1 - step
-        for line in range(LINES):
-            z = jnp.concatenate(
-                [
-                    jnp.concatenate(
-                        mix(
-                            lambda w, v: wide[line, k, pl.ds((w * 5 + v) * 2 + 1, 1)],
-                            slabs_of(w_state[line, :, half], 16),
-                        ),
-                        axis=0,
-                    )
-                    for half in (slice(0, 128), slice(128, 256))
-                ],
-                axis=1,
-            )
-            z_hi, z_lo = split(z)
-            v_high[line, k] = z_hi
-            v_low[line, k] = z_lo
-            y = dot(bwd[line, :, 0:240], jnp.concatenate([z_hi, z_lo, z_hi], axis=0))
-            w_state[line, :, 0:128] = y[:, :128] + bottoms[line, k]
-            w_state[line, :, 128:256] = y[:, 128:]
+        for e in range(SEG):
+            z = [coupled(e, k, 1, w_state[e, :, half]) for half in (slice(0, 128), slice(128, 256))]
+            z_hi, z_lo = split(jnp.concatenate(z, axis=1))
+            v_high[e, k] = z_hi
+            v_low[e, k] = z_lo
+            y = dot(bwd[:, 0:240], jnp.concatenate([z_hi, z_lo, z_hi], axis=0))
+            w_state[e, :, 0:128] = y[:, :128] + bottoms[e, k]
+            w_state[e, :, 128:256] = y[:, 128:]
         return carry
 
     lax.fori_loop(0, SEG, backward, 0)
-    for line in range(LINES):
-        maps_out[line, :, 0:128] = w_state[line, :, 0:128]
-        maps_out[line, :, 128:256] = w_state[line, :, 128:256] + roll(t_state[line], 40)
-
-
-def compose_kernel(maps, t_out, w_out, whole_out):
+    for e in range(SEG):
+        maps[e, :, 0:128] = w_state[e, :, 0:128]
+        maps[e, :, 128:256] = w_state[e, :, 128:256] + roll(t_state[e], 40)
+    compose(maps, t_out, w_out, whole_out)
+
+
+def compose(maps, t_out, w_out, whole_out):
     lane = lanes((80, 128))
     tall_lane, tall_row = lanes((128, 128)), rows((128, 128))
     zero = jnp.zeros((48, 128), F32)
@@ -448,7 +471,7 @@
 
 
 def solve_kernel(*refs):
-    *parts, t_in, w_in, out, wholes = refs
+    *parts, t_in, w_in, z_high, z_low, v_high, v_low, out, wholes = refs
     groups = len(parts)
     mine = lax.axis_index("span") // SEG
     for distance, part in enumerate(parts):
@@ -486,6 +509,7 @@
     y1 = jnp.where(line_lane < 33, back_row, 0.0)
     trace_cat = left_cat(trace_row)
     y_cat = left_cat(jnp.concatenate([y0, y1], axis=1))
+    answers = []
     for e in range(SEG):
         high, low = split(t_in[e])
         t_row = dot_nt(trace_cat, jnp.concatenate([high, low, high], axis=1))
@@ -493,40 +517,28 @@
         c_row = roll(dot_nt(y_cat, jnp.concatenate([high, low, high], axis=1)), 88)
         first = jnp.where(line_lane < 80, t_row, jnp.where(line_lane < 88, 1.0, c_row))
         second = jnp.where(line_lane < 40, c_row, 0.0)
-        out[e, :, 0:128] = first
-        out[e, :, 128:256] = second
-
-
-def finish_kernel(
-    incoming,
-    z_high,
-    z_low,
-    v_high,
-    v_low,
-    turned,
-    inverse_high,
-    inverse_low,
-    flow,
-    fixed,
-    out,
-):
-    high, low = split(incoming[...].reshape(64, 256))
+        answers.append(jnp.concatenate([first, second], axis=1))
+    high, low = split(jnp.concatenate(answers, axis=0))
     y = jnp.concatenate([high, low], axis=0)
-    small_lane = lanes((80, 128)) % 64
+    small_lane = lane % 64
     lower = jnp.zeros((80, 128), F32)
     upper = jnp.zeros((80, 128), F32)
-    for line in range(LINES):
-        z_hi, z_lo = z_high[line].reshape(640, 128), z_low[line].reshape(640, 128)
-        v_hi, v_lo = v_high[line].reshape(640, 256), v_low[line].reshape(640, 256)
+    for e in range(SEG):
+        z_hi, z_lo = z_high[e].reshape(640, 128), z_low[e].reshape(640, 128)
+        v_hi, v_lo = v_high[e].reshape(640, 256), v_low[e].reshape(640, 256)
         c = dot_nt(z_hi, y[:, :128]) + dot_nt(z_lo, y[:, :128])
         d = dot_nt(v_hi, y) + dot_nt(v_lo, y)
         for k in range(SEG):
-            mine = small_lane == line * SEG + k
+            mine = small_lane == e * SEG + k
             lower = jnp.where(mine, c[80 * k : 80 * k + 80], lower)
             upper = jnp.where(mine, d[80 * k : 80 * k + 80], upper)
-    both = jnp.concatenate([lower, upper], axis=0)
-    both = both + roll(both, 64)
-    added = dot(fixed[SPREAD, 0:160], pair_lanes(both))
+    both = jnp.concatenate([lower, upper, jnp.zeros((96, 128), F32)], axis=0)
+    out[...] = jnp.transpose(both + roll(both, 64))[:64]
+
+
+def finish_kernel(incoming, turned, inverse_high, inverse_low, flow, fixed, out):
+    high, low = split(incoming[...])
+    added = dot_nt(fixed[SPREAD, 0:160], jnp.concatenate([high, low], axis=0)[:, 0:160])
     load = pair_lanes(turned[...] + added + roll(added, 64))
     wide_lane = lanes((320, 128)) % 64
     total = jnp.zeros((320, 128), F32)
@@ -552,7 +564,7 @@
 
 
 VM = pl.BlockSpec(memory_space=pltpu.VMEM)
-HBM = pl.BlockSpec(memory_space=pl.ANY)
+HBM = pl.BlockSpec(memory_space=pltpu.HBM)
 
 
 def shape(*dims, dtype=F32):
@@ -591,57 +603,42 @@
         plane = ring(plane, "gx", 1)
 
     inverse = line_inverse.reshape(LINES, 320, 320)
-    inverse_high, inverse_low, rows_high, rows_low, fwd, bwd, tables, wide = call(
+    natural = [
+        volume_jacobian.transpose(0, 3, 4, 5, 1, 2).reshape(4, 75, 2, SEG),
+        side_jacobian.transpose(0, 1, 4, 5, 3, 2).reshape(LINES, 25, 4, SEG),
+        span_jacobian.transpose(0, 1, 4, 5, 3, 2).reshape(LINES, 25, 2, SEG),
+        mirror_face.transpose(0, 1, 3, 2).reshape(LINES, 4, SEG),
+        edge_flip.transpose(0, 1, 3, 2).reshape(LINES, 4, SEG),
+    ]
+    inverse_high, inverse_low, rows_high, rows_low, fwd, bwd, tables = call(
         prepare_kernel,
         (
             shape(LINES, 320, 320, dtype=BF16),
             shape(LINES, 320, 320, dtype=BF16),
             shape(LINES, 160, 320, dtype=BF16),
             shape(LINES, 160, 320, dtype=BF16),
-            shape(LINES, 160, 256, dtype=BF16),
-            shape(LINES, 80, 256, dtype=BF16),
+            shape(160, 256, dtype=BF16),
+            shape(80, 256, dtype=BF16),
             shape(248, 128),
-            shape(LINES, SEG, 50, 128),
         ),
-        [HBM] + [VM] * 6,
-        scratch=[pltpu.VMEM((LINES, 320, 320), F32), pltpu.SemaphoreType.DMA((LINES,))],
+        [HBM] * 7,
+        scratch=[pltpu.VMEM((LINES, 320, 320), F32), pltpu.VMEM(early.shape, BF16)]
+        + [pltpu.VMEM(x.shape, x.dtype) for x in natural]
+        + [pltpu.SemaphoreType.DMA((LINES + 6,))],
         limit=24,
         flops=4_000_000_000,
         moved=8_000_000,
         name="prepare",
-    )(
-        inverse,
-        early,
-        volume_jacobian.transpose(0, 3, 4, 5, 1, 2).reshape(4, 75, 2, SEG),
-        side_jacobian.transpose(0, 1, 4, 5, 3, 2).reshape(LINES, 25, 4, SEG),
-        span_jacobian.transpose(0, 1, 4, 5, 3, 2).reshape(LINES, 25, 2, SEG),
-        mirror_face.transpose(0, 1, 3, 2).reshape(LINES, 4, SEG),
-        edge_flip.transpose(0, 1, 3, 2).reshape(LINES, 4, SEG),
-    )
-
-    residual, turned, maps, z_high, z_low, v_high, v_low = call(
+    )(*(pltpu.with_memory_space_constraint(x, pltpu.HBM) for x in (inverse, early, *natural)))
+
+    residual, turned, sent = call(
         sweep_kernel,
-        (
-            shape(64, 320),
-            shape(320, 128),
-            shape(LINES, 80, 256),
-            shape(LINES, SEG, 80, 128, dtype=BF16),
-            shape(LINES, SEG, 80, 128, dtype=BF16),
-            shape(LINES, SEG, 80, 256, dtype=BF16),
-            shape(LINES, SEG, 80, 256, dtype=BF16),
-        ),
-        [VM] * 15,
-        scratch=[
-            pltpu.VMEM((256, 320), F32),
-            pltpu.VMEM((192, 640), F32),
-            pltpu.VMEM((LINES, 160, 128), F32),
-            pltpu.VMEM((LINES, 80, 128), F32),
-            pltpu.VMEM((LINES, 80, 256), F32),
-            pltpu.VMEM((LINES, SEG, 80, 128), F32),
-        ],
-        limit=28,
-        flops=10_000_000_000,
-        moved=20_000_000,
+        (shape(64, 320), shape(320, 128), shape(64, 256)),
+        [VM] * 12,
+        scratch=[pltpu.VMEM((256, 320), F32), pltpu.VMEM((192, 640), F32)],
+        limit=20,
+        flops=3_000_000_000,
+        moved=8_000_000,
         name="sweep",
     )(
         flow,
@@ -653,39 +650,52 @@
         source_term.reshape(64, 320),
         pseudo_time.reshape(64, 320),
         tables,
-        wide,
         rows_high,
         rows_low,
-        fwd,
-        bwd,
         fixed,
     )
 
     within = [[SEG * g + m for m in range(SEG)] for g in range(groups)]
 
     def exchange(value):
-        return lax.all_to_all(value, "span", 0, 0, axis_index_groups=within, tiled=True)
-
-    maps = exchange(maps)
-    t_maps, w_maps, whole = call(
-        compose_kernel,
-        (shape(SEG, 128, 128), shape(SEG, 128, 256), shape(80, 256)),
-        [VM],
-        limit=8,
-        name="compose",
-    )(maps)
+        value = value.reshape(SEG, 8, 256)
+        value = lax.all_to_all(value, "span", 0, 0, axis_index_groups=within, tiled=True)
+        return value.reshape(64, 256)
+
+    z_high, z_low, v_high, v_low, t_maps, w_maps, whole = call(
+        maps_kernel,
+        (
+            shape(SEG, SEG, 80, 128, dtype=BF16),
+            shape(SEG, SEG, 80, 128, dtype=BF16),
+            shape(SEG, SEG, 80, 256, dtype=BF16),
+            shape(SEG, SEG, 80, 256, dtype=BF16),
+            shape(SEG, 128, 128),
+            shape(SEG, 128, 256),
+            shape(80, 256),
+        ),
+        [VM] * 3,
+        scratch=[
+            pltpu.VMEM((SEG, SEG, 50, 128), F32),
+            pltpu.VMEM((SEG, 160, 128), F32),
+            pltpu.VMEM((SEG, 80, 128), F32),
+            pltpu.VMEM((SEG, 80, 256), F32),
+            pltpu.VMEM((SEG, SEG, 80, 128), F32),
+            pltpu.VMEM((SEG, 80, 256), F32),
+        ],
+        limit=28,
+        name="maps",
+    )(exchange(sent), fwd, bwd)
     wholes = [whole] + [ring(whole, "span", SEG * distance) for distance in range(1, groups)]
     answers = call(
         solve_kernel,
-        shape(SEG, 8, 256),
-        [VM] * (groups + 2),
+        shape(64, 256),
+        [VM] * (groups + 6),
         scratch=[pltpu.VMEM((groups, 80, 256), F32)],
-        limit=8,
+        limit=24,
         name="solve",
-    )(*wholes, t_maps, w_maps)
-    incoming = exchange(answers)
-    updated = call(finish_kernel, shape(64, 320), [VM] * 10, limit=20, name="finish")(
-        incoming, z_high, z_low, v_high, v_low, turned, inverse_high, inverse_low, flow, fixed
+    )(*wholes, t_maps, w_maps, z_high, z_low, v_high, v_low)
+    updated = call(finish_kernel, shape(64, 320), [VM] * 6, limit=20, name="finish")(
+        exchange(answers), turned, inverse_high, inverse_low, flow, fixed
     )
     return updated.reshape(flow_state.shape), residual.reshape(flow_state.shape)
 

time: 88.4 us -> 70.2 us (0.79)
  local copies, waits for them, and re-layouts: 8.49 us -> 0.9 us
  blocking collectives: 29.7 us -> 23.5 us
  Pallas kernels: 30.4 us -> 25.6 us
    unnamed x24 -> x10, local copies, waits for them, and re-layouts: 8.49 us -> 0.9 us
    all_to_all x2, blocking collectives: 29.7 us -> 23.5 us  [exchange(): lax.all_to_all(value, 'span', 0, 0, axis_index_groups=within, tiled=True)]
    pallas_call x1, Pallas kernels: 9.63 us -> 4.98 us  [on_device(): call(prepare_kernel, (shape(LINES, 320, 320, dtype=BF16), shape(LINES, 32...]
  transfers between devices with their start and end apart: 8 -> 8, of which waited for: 2 -> 2; matrix products, arithmetic and copies ran while one was open for 0% -> 0% of each run, Pallas kernels for 11% -> 7%
where the time goes in v3:
time: 70.2 us; the launch traced here: 69.7 us
  Pallas kernels  25.6 us (36%)
  blocking collectives  23.5 us (33%)
  starting transfers between devices  13.3 us (19%)
  waiting for transfers between devices  5.69 us (8%)
  local copies, waits for them, and re-layouts  0.9 us (1%)
  between operations  0.75 us (1%)
    all_to_all x2, blocking collectives, exchange(): lax.all_to_all(value, 'span', 0, 0, axis_index_groups=within, tiled=True)  23.5 us
    ppermute x8, starting transfers between devices, ring(): lax.ppermute(value, axis, [(i, (i + step) % count) for i in range(count)])  13.3 us
    pallas_call x1, Pallas kernels, on_device(): call(maps_kernel, (shape(SEG, SEG, 80, 128, dtype=BF16), shape(SEG, SEG,...  10.3 us
    ppermute x8, waiting for transfers between devices, ring(): lax.ppermute(value, axis, [(i, (i + step) % count) for i in range(count)])  5.69 us
    pallas_call x1, Pallas kernels, on_device(): call(prepare_kernel, (shape(LINES, 320, 320, dtype=BF16), shape(LINES, 32...  4.98 us
    pallas_call x1, Pallas kernels, on_device(): call(solve_kernel, shape(64, 256), [VM] * (groups + 6), scratch=[pltpu.VM...  4.46 us
    pallas_call x1, Pallas kernels, on_device(): call(sweep_kernel, (shape(64, 320), shape(320, 128), shape(64, 256)), [VM...  3.5 us
    pallas_call x1, Pallas kernels, on_device(): call(finish_kernel, shape(64, 320), [VM] * 6, limit=20, name='finish')  2.36 us
  transfers between devices with their start and end apart: 8, of which 2 were waited for; matrix products, arithmetic and copies ran while one was open for 0% of the time, Pallas kernels for 7%

profile of v3, /device:TPU:2, one launch (start us, length us, event | category | flops | bytes accessed | tf_op | source)
XLA Modules:
  0.0 69.7 jit_solution(7102636156836814275)
XLA Ops:
  0.6 0.0 copy-start.1
  0.6 0.9 %copy-done.1 = f32[4,2,8,320]{3,2,1,0:T(8,128)S(1)} copy-done((f32[4,2,8,320]{3,2,1,0:T(8,128)S(1)}, f32[4,2,8,320]{3,2,1,0:T(8,128)}, u32[]{:S(2)}) %copy-start.1) | copy-done | bytes 81944
  1.6 1.6 %collective-permute-start.3 = (f32[8,320]{1,0:T(8,128)S(1)}, f32[8,320]{1,0:T(8,128)S(1)}, u32[]{:S(2)}, u32[]{:S(2)}) collective-permute-start(f32[8,320]{1,0:T(8,128)S(1)} %get-tuple-element.27), channel_id=1, source_target_pairs={{0,8},{8,16},{16,24},{24,32},{32,40},{40,48},{48,56},{56,64},{64,7... | collective-permute-start | bytes 30728 | tf_op jit(solution)/shard_map/halo/ppermute | solution.py:590
  3.1 0.9 %collective-permute-start.4 = (f32[8,320]{1,0:T(8,128)S(1)}, f32[8,320]{1,0:T(8,128)S(1)}, u32[]{:S(2)}, u32[]{:S(2)}) collective-permute-start(f32[8,320]{1,0:T(8,128)S(1)} %get-tuple-element.28), channel_id=1, source_target_pairs={{0,248},{8,0},{16,8},{24,16},{32,24},{40,32},{48,40},{56,48},{64,5... | collective-permute-start | bytes 30728 | tf_op jit(solution)/shard_map/halo/ppermute | solution.py:590
  4.0 0.0 collective-permute-start
  4.0 1.2 %collective-permute-start.1 = (f32[32,320]{1,0:T(8,128)S(1)}, f32[32,320]{1,0:T(8,128)S(1)}, u32[]{:S(2)}, u32[]{:S(2)}) collective-permute-start(f32[32,320]{1,0:T(8,128)S(1)} %get-tuple-element.25), channel_id=1, source_target_pairs={{0,1},{1,2},{2,3},{3,0},{4,5},{5,6},{6,7},{7,4},{8,9},{9,10},{10,1... | collective-permute-start | bytes 122888 | tf_op jit(solution)/shard_map/halo/ppermute | solution.py:590
  5.2 2.0 %collective-permute-start.2 = (f32[32,320]{1,0:T(8,128)S(1)}, f32[32,320]{1,0:T(8,128)S(1)}, u32[]{:S(2)}, u32[]{:S(2)}) collective-permute-start(f32[32,320]{1,0:T(8,128)S(1)} %get-tuple-element.26), channel_id=1, source_target_pairs={{0,3},{1,0},{2,1},{3,2},{4,7},{5,4},{6,5},{7,6},{8,11},{9,8},{10,9... | collective-permute-start | bytes 122888 | tf_op jit(solution)/shard_map/halo/ppermute | solution.py:590
  7.2 0.0 copy-start
  7.2 0.0 copy-start.2
  7.2 0.0 copy-start.3
  7.2 0.0 copy-start.4
  7.2 5.0 %prepare.1 = (bf16[8,320,320]{2,1,0:T(8,128)(2,1)S(1)}, bf16[8,320,320]{2,1,0:T(8,128)(2,1)S(1)}, bf16[8,160,320]{2,1,0:T(8,128)(2,1)S(1)}, bf16[8,160,320]{2,1,...) custom-call(f32[8,320,320]{2,1,0:T(8,128)} %bitcast.35, ...), custom_call_target="tpu_custom_call" | custom-call | flops 4000000000 | bytes 8000000 | tf_op jit(solution)/shard_map/prepare/pallas_call | solution.py:613
  12.2 0.0 collective-permute-done.3.below
  12.2 0.0 collective-permute-done.4.above
  12.3 0.0 collective-permute-done.plane
  12.3 0.0 collective-permute-done.1.gy_low
  12.3 0.0 collective-permute-done.2.gy_high
  12.3 0.0 copy-done
  12.3 0.0 copy-done.2
  12.3 0.0 copy-done.3
  12.3 0.0 copy-done.4
  12.3 3.5 %sweep.1 = (f32[64,320]{1,0:T(8,128)}, f32[320,128]{1,0:T(8,128)S(1)}, f32[64,256]{1,0:T(8,128)S(1)}) custom-call(f32[64,320]{1,0:T(8,128)S(1)} %bitcast.26, f32[16,320]{1,0:T(8,128)S(1)} %collective-permute-done.plane, f32[32,320]{1,0:T(8,128)S(1)} %collective-permute-done.1.gy_low, f32[32,320]{1,0:T(8,128)S(1)} %collective-permute-done.2.gy_high, ...), custom_call_target="tpu_custom_call" | custom-call | flops 3000000000 | bytes 8000000 | tf_op jit(solution)/shard_map/sweep/pallas_call | solution.py:634
  15.8 13.6 %all_to_all.10 = f32[8,8,256]{2,1,0:T(8,128)S(1)} all-to-all(f32[8,8,256]{2,1,0:T(8,128)S(1)} %bitcast.31), channel_id=1, replica_groups={{0,8,16,24,32,40,48,56},{64,72,80,88,96,104,112,120},{128,136,144,152,1..., dimensions={0} | all-to-all | bytes 131072 | tf_op jit(solution)/shard_map/all_to_all | solution.py:662
  29.4 10.3 %maps.1 = (bf16[8,8,80,128]{3,2,1,0:T(8,128)(2,1)S(1)}, bf16[8,8,80,128]{3,2,1,0:T(8,128)(2,1)S(1)}, bf16[8,8,80,256]{3,2,1,0:T(8,128)(2,1)S(1)}, bf16[8,8,80,25...) custom-call(f32[64,256]{1,0:T(8,128)S(1)} %bitcast.30, ...), custom_call_target="tpu_custom_call" | custom-call | tf_op jit(solution)/shard_map/maps/pallas_call | solution.py:665
  39.7 2.6 %collective-permute-start.7 = (f32[80,256]{1,0:T(8,128)S(1)}, f32[80,256]{1,0:T(8,128)S(1)}, u32[]{:S(2)}, u32[]{:S(2)}) collective-permute-start(f32[80,256]{1,0:T(8,128)S(1)} %get-tuple-element.35.refs_0_), channel_id=1, source_target_pairs={{0,192},{8,200},{16,208},{24,216},{32,224},{40,232},{48,240},{56,2... | collective-permute-start | bytes 245768 | tf_op jit(solution)/shard_map/ppermute | solution.py:590
  42.4 2.2 %collective-permute-start.6 = (f32[80,256]{1,0:T(8,128)S(1)}, f32[80,256]{1,0:T(8,128)S(1)}, u32[]{:S(2)}, u32[]{:S(2)}) collective-permute-start(f32[80,256]{1,0:T(8,128)S(1)} %get-tuple-element.35.refs_0_), channel_id=1, source_target_pairs={{0,128},{8,136},{16,144},{24,152},{32,160},{40,168},{48,176},{56,1... | collective-permute-start | bytes 245768 | tf_op jit(solution)/shard_map/ppermute | solution.py:590
  44.6 2.8 %collective-permute-start.5 = (f32[80,256]{1,0:T(8,128)S(1)}, f32[80,256]{1,0:T(8,128)S(1)}, u32[]{:S(2)}, u32[]{:S(2)}) collective-permute-start(f32[80,256]{1,0:T(8,128)S(1)} %get-tuple-element.35.refs_0_), channel_id=1, source_target_pairs={{0,64},{8,72},{16,80},{24,88},{32,96},{40,104},{48,112},{56,120},{... | collective-permute-start | bytes 245768 | tf_op jit(solution)/shard_map/ppermute | solution.py:590
  47.3 0.0 collective-permute-done.7.refs_3_
  47.3 4.3 %collective-permute-done.6.refs_2_ = f32[80,256]{1,0:T(8,128)S(1)} collective-permute-done((f32[80,256]{1,0:T(8,128)S(1)}, f32[80,256]{1,0:T(8,128)S(1)}, u32[]{:S(2)}, u32[]{:S(2)}) %collective-permute-start.6) | collective-permute-done | bytes 81952 | tf_op jit(solution)/shard_map/ppermute | solution.py:590
  51.7 1.3 %collective-permute-done.5.refs_1_ = f32[80,256]{1,0:T(8,128)S(1)} collective-permute-done((f32[80,256]{1,0:T(8,128)S(1)}, f32[80,256]{1,0:T(8,128)S(1)}, u32[]{:S(2)}, u32[]{:S(2)}) %collective-permute-start.5) | collective-permute-done | bytes 81952 | tf_op jit(solution)/shard_map/ppermute | solution.py:590
  53.0 4.5 %solve.1 = f32[64,256]{1,0:T(8,128)S(1)} custom-call(f32[80,256]{1,0:T(8,128)S(1)} %get-tuple-element.35.refs_0_, f32[80,256]{1,0:T(8,128)S(1)} %collective-permute-done.5.refs_1_, f32[80,256]{1,0:T(8,128)S(1)} %collective-permute-done.6.refs_2_, f32[80,256]{1,0:T(8,128)S(1)} %collective-permute-done.7.refs_3_, ...), custom_call_target="tpu_custom_call" | custom-call | tf_op jit(solution)/shard_map/solve/pallas_call | solution.py:689
  57.5 9.9 %all_to_all.11 = f32[8,8,256]{2,1,0:T(8,128)S(1)} all-to-all(f32[8,8,256]{2,1,0:T(8,128)S(1)} %bitcast.28), channel_id=1, replica_groups={{0,8,16,24,32,40,48,56},{64,72,80,88,96,104,112,120},{128,136,144,152,1..., dimensions={0} | all-to-all | bytes 131072 | tf_op jit(solution)/shard_map/all_to_all | solution.py:662
  67.3 2.4 %finish.1 = f32[64,320]{1,0:T(8,128)} custom-call(f32[64,256]{1,0:T(8,128)S(1)} %bitcast.29, f32[320,128]{1,0:T(8,128)S(1)} %get-tuple-element.42.turned, bf16[8,320,320]{2,1,0:T(8,128)(2,1)S(1)} %get-tuple-element.43.inverse_high, bf16[8,320,320]{2,1,0:T(8,128)(2,1)S(1)} %get-tuple-element.44.inverse_low, f32[64,320]{1,0:T(8,128)S(1)} %bitcast.27, ...), custom_call_target="tpu_custom_call" | custom-call | tf_op jit(solution)/shard_map/finish/pallas_call | solution.py:697
  (1 shorter events, 0.0 us)
Async XLA Ops:
  0.6 0.9 %copy-start.1 = (f32[4,2,8,320]{3,2,1,0:T(8,128)S(1)}, f32[4,2,8,320]{3,2,1,0:T(8,128)}, u32[]{:S(2)}) copy-start(f32[4,2,8,320]{3,2,1,0:T(8,128)} %param.11) | copy-start | bytes 245764
  1.6 10.7 %collective-permute-start.3 = (f32[8,320]{1,0:T(8,128)S(1)}, f32[8,320]{1,0:T(8,128)S(1)}, u32[]{:S(2)}, u32[]{:S(2)}) collective-permute-start(f32[8,320]{1,0:T(8,128)S(1)} %get-tuple-element.27), channel_id=1, source_target_pairs={{0,8},{8,16},{16,24},{24,32},{32,40},{40,48},{48,56},{56,64},{64,7... | collective-permute-start | bytes 30728 | tf_op jit(solution)/shard_map/halo/ppermute | solution.py:590
  3.1 9.1 %collective-permute-start.4 = (f32[8,320]{1,0:T(8,128)S(1)}, f32[8,320]{1,0:T(8,128)S(1)}, u32[]{:S(2)}, u32[]{:S(2)}) collective-permute-start(f32[8,320]{1,0:T(8,128)S(1)} %get-tuple-element.28), channel_id=1, source_target_pairs={{0,248},{8,0},{16,8},{24,16},{32,24},{40,32},{48,40},{56,48},{64,5... | collective-permute-start | bytes 30728 | tf_op jit(solution)/shard_map/halo/ppermute | solution.py:590
  4.0 8.3 %collective-permute-start = (f32[16,320]{1,0:T(8,128)S(1)}, f32[16,320]{1,0:T(8,128)S(1)}, u32[]{:S(2)}, u32[]{:S(2)}) collective-permute-start(f32[16,320]{1,0:T(8,128)S(1)} %get-tuple-element.24), channel_id=1, source_target_pairs={{0,4},{4,0},{1,5},{5,1},{2,6},{6,2},{3,7},{7,3},{8,12},{12,8},{9,1... | collective-permute-start | bytes 61448 | tf_op jit(solution)/shard_map/halo/ppermute | solution.py:590
  4.0 8.3 %collective-permute-start.1 = (f32[32,320]{1,0:T(8,128)S(1)}, f32[32,320]{1,0:T(8,128)S(1)}, u32[]{:S(2)}, u32[]{:S(2)}) collective-permute-start(f32[32,320]{1,0:T(8,128)S(1)} %get-tuple-element.25), channel_id=1, source_target_pairs={{0,1},{1,2},{2,3},{3,0},{4,5},{5,6},{6,7},{7,4},{8,9},{9,10},{10,1... | collective-permute-start | bytes 122888 | tf_op jit(solution)/shard_map/halo/ppermute | solution.py:590
  5.2 7.0 %collective-permute-start.2 = (f32[32,320]{1,0:T(8,128)S(1)}, f32[32,320]{1,0:T(8,128)S(1)}, u32[]{:S(2)}, u32[]{:S(2)}) collective-permute-start(f32[32,320]{1,0:T(8,128)S(1)} %get-tuple-element.26), channel_id=1, source_target_pairs={{0,3},{1,0},{2,1},{3,2},{4,7},{5,4},{6,5},{7,6},{8,11},{9,8},{10,9... | collective-permute-start | bytes 122888 | tf_op jit(solution)/shard_map/halo/ppermute | solution.py:590
  7.2 5.1 %copy-start = (bf16[2912,320]{1,0:T(8,128)(2,1)S(1)}, bf16[2912,320]{1,0:T(8,128)(2,1)}, u32[]{:S(2)}) copy-start(bf16[2912,320]{1,0:T(8,128)(2,1)} %constant.5.clone.fixed) | copy-start | bytes 5591044
  7.2 5.1 %copy-start.2 = (f32[4,2,8,320]{3,2,1,0:T(8,128)S(1)}, f32[4,2,8,320]{3,2,1,0:T(8,128)}, u32[]{:S(2)}) copy-start(f32[4,2,8,320]{3,2,1,0:T(8,128)} %param.11) | copy-start | bytes 245764
  7.2 5.1 %copy-start.3 = (f32[4,2,8,320]{3,2,1,0:T(8,128)S(1)}, f32[4,2,8,320]{3,2,1,0:T(8,128)}, u32[]{:S(2)}) copy-start(f32[4,2,8,320]{3,2,1,0:T(8,128)} %param.12) | copy-start | bytes 245764
  7.2 5.1 %copy-start.4 = (f32[4,2,8,320]{3,2,1,0:T(8,128)S(1)}, f32[4,2,8,320]{3,2,1,0:T(8,128)}, u32[]{:S(2)}) copy-start(f32[4,2,8,320]{3,2,1,0:T(8,128)} %param.13) | copy-start | bytes 245764
  39.7 7.6 %collective-permute-start.7 = (f32[80,256]{1,0:T(8,128)S(1)}, f32[80,256]{1,0:T(8,128)S(1)}, u32[]{:S(2)}, u32[]{:S(2)}) collective-permute-start(f32[80,256]{1,0:T(8,128)S(1)} %get-tuple-element.35.refs_0_), channel_id=1, source_target_pairs={{0,192},{8,200},{16,208},{24,216},{32,224},{40,232},{48,240},{56,2... | collective-permute-start | bytes 245768 | tf_op jit(solution)/shard_map/ppermute | solution.py:590
  42.4 9.3 %collective-permute-start.6 = (f32[80,256]{1,0:T(8,128)S(1)}, f32[80,256]{1,0:T(8,128)S(1)}, u32[]{:S(2)}, u32[]{:S(2)}) collective-permute-start(f32[80,256]{1,0:T(8,128)S(1)} %get-tuple-element.35.refs_0_), channel_id=1, source_target_pairs={{0,128},{8,136},{16,144},{24,152},{32,160},{40,168},{48,176},{56,1... | collective-permute-start | bytes 245768 | tf_op jit(solution)/shard_map/ppermute | solution.py:590
  44.6 8.5 %collective-permute-start.5 = (f32[80,256]{1,0:T(8,128)S(1)}, f32[80,256]{1,0:T(8,128)S(1)}, u32[]{:S(2)}, u32[]{:S(2)}) collective-permute-start(f32[80,256]{1,0:T(8,128)S(1)} %get-tuple-element.35.refs_0_), channel_id=1, source_target_pairs={{0,64},{8,72},{16,80},{24,88},{32,96},{40,104},{48,112},{56,120},{... | collective-permute-start | bytes 245768 | tf_op jit(solution)/shard_map/ppermute | solution.py:590

commit v4 on v3

--- a/solution.py
+++ b/solution.py
@@ -155,6 +155,12 @@
     return jnp.where(lanes(x.shape) < 64, high, roll(x - high, 64)).astype(BF16)
 
 
+def against_both(x):
+    paired = pair_lanes(x)
+    first = jnp.where(lanes(x.shape) < 64, paired.astype(F32), 0.0).astype(BF16)
+    return jnp.concatenate([paired, first], axis=0)
+
+
 def left_cat(x):
     high, low = split(x)
     return jnp.concatenate([high, high, low], axis=1)
@@ -184,8 +190,6 @@
     span_in,
     mirror_in,
     flip_in,
-    high_out,
-    low_out,
     rows_high,
     rows_low,
     fwd_out,
@@ -227,8 +231,6 @@
     for line in range(LINES):
         copies[6 + line].wait()
         high, low = split(held[line])
-        high_out[line] = high
-        low_out[line] = low
         layers = early[640:800, 0:320]
         rows_high[line] = dot(layers, high).astype(BF16)
         rows_low[line] = dot(layers, low).astype(BF16)
@@ -237,6 +239,36 @@
     both = both.astype(BF16)
     fwd_out[...] = both[:, :256]
     bwd_out[...] = both[80:, 256:]
+
+
+def base_kernel(inverse, turned, flow, fixed, base_out, columns_high, columns_low, held, arrived):
+    copies = [
+        pltpu.make_async_copy(inverse.at[line], held.at[line], arrived.at[line])
+        for line in range(LINES)
+    ]
+    for copy in copies:
+        copy.start()
+    load = pair_lanes(turned[...])
+    spread = fixed[SPREAD, 0:160]
+    wide_lane = lanes((320, 128)) % 64
+    total = jnp.zeros((320, 128), F32)
+    for line in range(LINES):
+        copies[line].wait()
+        high, low = split(held[line])
+        total = jnp.where(wide_lane // 8 == line, dot(high, load) + dot(low, load), total)
+        columns_high[line] = dot(high, spread).astype(BF16)
+        columns_low[line] = dot(low, spread).astype(BF16)
+    high, low = split(total)
+    twice = fixed[TWICE, 0:128]
+    base_out[...] = flow[...] + dot_nt(twice, high) + dot_nt(twice, low)
+
+
+def unpack(left, right):
+    lane = lanes((80, 128))
+    forward = jnp.where(lane < 88, roll(right, 88), 0.0)
+    cross = jnp.where(lane < 88, left, 0.0)
+    back = jnp.where(lane < 40, roll(left, 40), jnp.where(lane < 80, roll(right, 40), 0.0))
+    return forward, cross, back
 
 
 def mix(coefficient, slabs):
@@ -369,8 +401,7 @@
     received,
     fwd,
     bwd,
-    z_high,
-    z_low,
+    z_both,
     v_high,
     v_low,
     t_out,
@@ -406,8 +437,8 @@
             cats = []
             for e in (pair, pair + 1):
                 z_hi, z_lo = split(coupled(e, k, 0, t_state[e]))
-                z_high[e, k] = z_hi
-                z_low[e, k] = z_lo
+                z_both[e, k, :, 0:128] = z_hi
+                z_both[e, k, :, 128:256] = z_lo
                 cats.append(jnp.concatenate([z_hi, z_lo, z_hi], axis=0))
             both = dot(fwd[:, 0:240], jnp.concatenate(cats, axis=1))
             for e, y in ((pair, both[:, :128]), (pair + 1, both[:, 128:])):
@@ -415,7 +446,7 @@
                 bottoms[e, k] = y[80:] + jnp.where(mine, started[e, 80:160], 0.0)
         return carry
 
-    lax.fori_loop(0, SEG, forward, 0)
+    lax.fori_loop(0, SEG, forward, 0, unroll=True)
 
     def backward(step, carry):
         k = SEG - 1 - step
@@ -429,7 +460,7 @@
             w_state[e, :, 128:256] = y[:, 128:]
         return carry
 
-    lax.fori_loop(0, SEG, backward, 0)
+    lax.fori_loop(0, SEG, backward, 0, unroll=True)
     for e in range(SEG):
         maps[e, :, 0:128] = w_state[e, :, 0:128]
         maps[e, :, 128:256] = w_state[e, :, 128:256] + roll(t_state[e], 40)
@@ -437,58 +468,41 @@
 
 
 def compose(maps, t_out, w_out, whole_out):
-    lane = lanes((80, 128))
     tall_lane, tall_row = lanes((128, 128)), rows((128, 128))
     zero = jnp.zeros((48, 128), F32)
+    parts = [unpack(maps[e, :, 0:128], maps[e, :, 128:256]) for e in range(SEG)]
     fixed = jnp.where((tall_row < 80) & (tall_lane == tall_row), 1.0, 0.0)
     ones = jnp.where((tall_row >= 80) & (tall_row < 88) & (tall_lane == 80), 1.0, 0.0)
     state = fixed + ones
     coupled = []
     for e in range(SEG):
-        t_out[e] = state
-        left, right = maps[e, :, 0:128], maps[e, :, 128:256]
-        state_cat = right_cat(state)
-        both = jnp.concatenate([jnp.where(lane < 88, roll(right, 88), 0.0), jnp.where(lane < 88, left, 0.0)], axis=0)
-        y = dot(left_cat(both), state_cat)
+        t_out[e] = jnp.concatenate(split(state[:80]), axis=1)
+        y = dot(left_cat(jnp.concatenate(parts[e][:2], axis=0)), right_cat(state))
         coupled.append(y[80:])
         state = jnp.concatenate([y[:80], ones[80:]], axis=0)
     last = state[:80]
-    w0 = jnp.where(tall_lane == tall_row + 81, 1.0, 0.0)
-    w1 = jnp.where((tall_lane == tall_row - 47) & (tall_row < 80), 1.0, 0.0)
+    w0 = jnp.where(tall_lane == tall_row + 88, 1.0, 0.0)
+    w1 = jnp.where((tall_lane == tall_row - 40) & (tall_row < 80), 1.0, 0.0)
     for e in range(SEG - 1, -1, -1):
-        w_out[e, :, 0:128] = w0
-        w_out[e, :, 128:256] = w1
-        left, right = maps[e, :, 0:128], maps[e, :, 128:256]
-        back = jnp.where(lane < 40, roll(left, 40), jnp.where(lane < 80, roll(right, 40), 0.0))
-        back_cat = left_cat(back)
-        y0 = dot(back_cat, right_cat(w0)) + coupled[e]
-        y1 = dot(back_cat, right_cat(w1))
-        w0 = jnp.concatenate([y0, zero], axis=0)
-        w1 = jnp.concatenate([y1, zero], axis=0)
-    second = w1[:80] + roll(last, 33)
+        w_out[e] = jnp.concatenate(split(jnp.concatenate([w0[:80], w1[:80]], axis=1)), axis=1)
+        w = jnp.concatenate([right_cat(w0), right_cat(w1)], axis=1)
+        y = dot(left_cat(parts[e][2]), w)
+        w0 = jnp.concatenate([y[:, :128] + coupled[e], zero], axis=0)
+        w1 = jnp.concatenate([y[:, 128:], zero], axis=0)
     whole_out[:, 0:128] = w0[:80]
-    whole_out[:, 128:256] = second
+    whole_out[:, 128:256] = w1[:80] + roll(last, 40)
 
 
 def solve_kernel(*refs):
-    *parts, t_in, w_in, z_high, z_low, v_high, v_low, out, wholes = refs
+    *parts, t_in, w_in, z_both, v_high, v_low, out, wholes = refs
     groups = len(parts)
     mine = lax.axis_index("span") // SEG
     for distance, part in enumerate(parts):
         wholes[lax.rem(mine - distance + groups, groups)] = part[...]
     lane = lanes((80, 128))
-    tall_row = rows((128, 128))
-    one = jnp.where(tall_row == 80, 1.0, 0.0)
+    one = jnp.where(rows((128, 128)) == 80, 1.0, 0.0)
     zero = jnp.zeros((48, 128), F32)
-
-    def pieces(group):
-        left, right = wholes[group, :, 0:128], wholes[group, :, 128:256]
-        forward = jnp.where(lane < 81, roll(right, -33), 0.0)
-        cross = jnp.where(lane < 81, left, 0.0)
-        back = jnp.where(lane < 47, roll(left, 47), jnp.where(lane < 80, roll(right, 47), 0.0))
-        return forward, cross, back
-
-    parts = [pieces(group) for group in range(groups)]
+    parts = [unpack(wholes[g, :, 0:128], wholes[g, :, 128:256]) for g in range(groups)]
     traces = [one]
     for group in range(groups - 1):
         y = dot(left_cat(parts[group][0]), right_cat(traces[-1]))
@@ -502,32 +516,26 @@
     for group in range(1, groups):
         trace = jnp.where(mine == group, traces[group], trace)
         back = jnp.where(mine == group, backs[group], back)
-    trace_row = jnp.transpose(trace)[0:8]
-    back_row = roll(jnp.transpose(back)[0:8], 81)
-    line_lane = lanes((8, 128))
-    y0 = jnp.where(line_lane < 81, trace_row, back_row)
-    y1 = jnp.where(line_lane < 33, back_row, 0.0)
-    trace_cat = left_cat(trace_row)
-    y_cat = left_cat(jnp.concatenate([y0, y1], axis=1))
-    answers = []
-    for e in range(SEG):
-        high, low = split(t_in[e])
-        t_row = dot_nt(trace_cat, jnp.concatenate([high, low, high], axis=1))
-        high, low = split(w_in[e])
-        c_row = roll(dot_nt(y_cat, jnp.concatenate([high, low, high], axis=1)), 88)
-        first = jnp.where(line_lane < 80, t_row, jnp.where(line_lane < 88, 1.0, c_row))
-        second = jnp.where(line_lane < 40, c_row, 0.0)
-        answers.append(jnp.concatenate([first, second], axis=1))
-    high, low = split(jnp.concatenate(answers, axis=0))
-    y = jnp.concatenate([high, low], axis=0)
+    both = jnp.concatenate([trace[:88], back[:80], jnp.zeros((88, 128), F32)], axis=0)
+    lower_in = dot(t_in[...].reshape(640, 256), against_both(trace))
+    upper_in = dot(w_in[...].reshape(640, 512), against_both(both))
     small_lane = lane % 64
     lower = jnp.zeros((80, 128), F32)
     upper = jnp.zeros((80, 128), F32)
     for e in range(SEG):
-        z_hi, z_lo = z_high[e].reshape(640, 128), z_low[e].reshape(640, 128)
+        mine = small_lane // 8 == e
+        lower = jnp.where(mine, lower_in[80 * e : 80 * e + 80], lower)
+        upper = jnp.where(mine, upper_in[80 * e : 80 * e + 80], upper)
+    lower, upper = lower + roll(lower, 64), upper + roll(upper, 64)
+    y = jnp.concatenate([lower, jnp.ones((8, 128), F32), upper, jnp.zeros((88, 128), F32)], axis=0)
+    y_both = against_both(y[:128])
+    y = pair_lanes(y)
+    lower = jnp.zeros((80, 128), F32)
+    upper = jnp.zeros((80, 128), F32)
+    for e in range(SEG):
         v_hi, v_lo = v_high[e].reshape(640, 256), v_low[e].reshape(640, 256)
-        c = dot_nt(z_hi, y[:, :128]) + dot_nt(z_lo, y[:, :128])
-        d = dot_nt(v_hi, y) + dot_nt(v_lo, y)
+        c = dot(z_both[e].reshape(640, 256), y_both)
+        d = dot(v_hi, y) + dot(v_lo, y)
         for k in range(SEG):
             mine = small_lane == e * SEG + k
             lower = jnp.where(mine, c[80 * k : 80 * k + 80], lower)
@@ -536,18 +544,17 @@
     out[...] = jnp.transpose(both + roll(both, 64))[:64]
 
 
-def finish_kernel(incoming, turned, inverse_high, inverse_low, flow, fixed, out):
+def finish_kernel(incoming, base, columns_high, columns_low, fixed, out):
     high, low = split(incoming[...])
-    added = dot_nt(fixed[SPREAD, 0:160], jnp.concatenate([high, low], axis=0)[:, 0:160])
-    load = pair_lanes(turned[...] + added + roll(added, 64))
+    load = jnp.concatenate([high, low], axis=0)[:, 0:160]
     wide_lane = lanes((320, 128)) % 64
     total = jnp.zeros((320, 128), F32)
     for line in range(LINES):
-        applied = dot(inverse_high[line], load) + dot(inverse_low[line], load)
+        applied = dot_nt(columns_high[line], load) + dot_nt(columns_low[line], load)
         total = jnp.where(wide_lane // 8 == line, applied, total)
     high, low = split(total)
     twice = fixed[TWICE, 0:128]
-    out[...] = flow[...] + dot_nt(twice, high) + dot_nt(twice, low)
+    out[...] = base[...] + dot_nt(twice, high) + dot_nt(twice, low)
 
 
 def call(kernel, out_shape, in_specs, scratch=(), limit=16, flops=0, moved=0, name=None):
@@ -610,11 +617,9 @@
         mirror_face.transpose(0, 1, 3, 2).reshape(LINES, 4, SEG),
         edge_flip.transpose(0, 1, 3, 2).reshape(LINES, 4, SEG),
     ]
-    inverse_high, inverse_low, rows_high, rows_low, fwd, bwd, tables = call(
+    rows_high, rows_low, fwd, bwd, tables = call(
         prepare_kernel,
         (
-            shape(LINES, 320, 320, dtype=BF16),
-            shape(LINES, 320, 320, dtype=BF16),
             shape(LINES, 160, 320, dtype=BF16),
             shape(LINES, 160, 320, dtype=BF16),
             shape(160, 256, dtype=BF16),
@@ -662,15 +667,14 @@
         value = lax.all_to_all(value, "span", 0, 0, axis_index_groups=within, tiled=True)
         return value.reshape(64, 256)
 
-    z_high, z_low, v_high, v_low, t_maps, w_maps, whole = call(
+    z_both, v_high, v_low, t_maps, w_maps, whole = call(
         maps_kernel,
         (
-            shape(SEG, SEG, 80, 128, dtype=BF16),
-            shape(SEG, SEG, 80, 128, dtype=BF16),
             shape(SEG, SEG, 80, 256, dtype=BF16),
             shape(SEG, SEG, 80, 256, dtype=BF16),
-            shape(SEG, 128, 128),
-            shape(SEG, 128, 256),
+            shape(SEG, SEG, 80, 256, dtype=BF16),
+            shape(SEG, 80, 256, dtype=BF16),
+            shape(SEG, 80, 512, dtype=BF16),
             shape(80, 256),
         ),
         [VM] * 3,
@@ -686,16 +690,34 @@
         name="maps",
     )(exchange(sent), fwd, bwd)
     wholes = [whole] + [ring(whole, "span", SEG * distance) for distance in range(1, groups)]
+    late, turned, _ = lax.optimization_barrier((inverse, turned, whole))
+    base, columns_high, columns_low = call(
+        base_kernel,
+        (
+            shape(64, 320),
+            shape(LINES, 320, 160, dtype=BF16),
+            shape(LINES, 320, 160, dtype=BF16),
+        ),
+        [HBM] + [VM] * 3,
+        scratch=[pltpu.VMEM((LINES, 320, 320), F32), pltpu.SemaphoreType.DMA((LINES,))],
+        limit=16,
+        flops=3_000_000_000,
+        moved=16_000_000,
+        name="base",
+    )(pltpu.with_memory_space_constraint(late, pltpu.HBM), turned, flow, fixed)
+    base, columns_high, columns_low, *wholes = lax.optimization_barrier(
+        (base, columns_high, columns_low, *wholes)
+    )
     answers = call(
         solve_kernel,
         shape(64, 256),
-        [VM] * (groups + 6),
+        [VM] * (groups + 5),
         scratch=[pltpu.VMEM((groups, 80, 256), F32)],
         limit=24,
         name="solve",
-    )(*wholes, t_maps, w_maps, z_high, z_low, v_high, v_low)
-    updated = call(finish_kernel, shape(64, 320), [VM] * 6, limit=20, name="finish")(
-        exchange(answers), turned, inverse_high, inverse_low, flow, fixed
+    )(*wholes, t_maps, w_maps, z_both, v_high, v_low)
+    updated = call(finish_kernel, shape(64, 320), [VM] * 5, limit=16, name="finish")(
+        exchange(answers), base, columns_high, columns_low, fixed
     )
     return updated.reshape(flow_state.shape), residual.reshape(flow_state.shape)
 

time: 70.2 us -> 65.2 us (0.929)
  waiting for transfers between devices: 5.69 us -> 0.02 us
  blocking collectives: 23.5 us -> 22.3 us
  starting transfers between devices: 13.3 us -> 14.3 us
  Pallas kernels: 25.6 us -> 26.5 us
    ppermute x8, waiting for transfers between devices: 5.69 us -> 0.02 us  [ring(): lax.ppermute(value, axis, [(i, (i + step) % count) for i in range(count)])]
    all_to_all x2, blocking collectives: 23.5 us -> 22.3 us  [exchange(): lax.all_to_all(value, 'span', 0, 0, axis_index_groups=within, tiled=True)]
    ppermute x8, starting transfers between devices: 13.3 us -> 14.3 us  [ring(): lax.ppermute(value, axis, [(i, (i + step) % count) for i in range(count)])]
    pallas_call x4 -> x5, Pallas kernels: 22.1 us -> 23 us  [the longest x1 7.53 us: on_device(): call(maps_kernel, (shape(SEG, SEG, 80, 256, dtype=BF16), shape(SEG, SEG,...]
  transfers between devices with their start and end apart: 8 -> 8, of which waited for: 2 -> 0; matrix products, arithmetic and copies ran while one was open for 0% -> 0% of each run, Pallas kernels for 7% -> 15%
where the time goes in v4:
time: 65.2 us; the launch traced here: 64.8 us
  Pallas kernels  26.5 us (41%)
  blocking collectives  22.3 us (34%)
  starting transfers between devices  14.3 us (22%)
  local copies, waits for them, and re-layouts  0.9 us (1%)
  between operations  0.78 us (1%)
    all_to_all x2, blocking collectives, exchange(): lax.all_to_all(value, 'span', 0, 0, axis_index_groups=within, tiled=True)  22.3 us
    ppermute x8, starting transfers between devices, ring(): lax.ppermute(value, axis, [(i, (i + step) % count) for i in range(count)])  14.3 us
    pallas_call x1, Pallas kernels, on_device(): call(maps_kernel, (shape(SEG, SEG, 80, 256, dtype=BF16), shape(SEG, SEG,...  7.53 us
    pallas_call x1, Pallas kernels, on_device(): call(base_kernel, (shape(64, 320), shape(LINES, 320, 160, dtype=BF16), sh...  4.9 us
    pallas_call x1, Pallas kernels, on_device(): call(prepare_kernel, (shape(LINES, 160, 320, dtype=BF16), shape(LINES, 16...  4.86 us
    pallas_call x1, Pallas kernels, on_device(): call(solve_kernel, shape(64, 256), [VM] * (groups + 5), scratch=[pltpu.VM...  4.06 us
    pallas_call x1, Pallas kernels, on_device(): call(sweep_kernel, (shape(64, 320), shape(320, 128), shape(64, 256)), [VM...  3.51 us
    pallas_call x1, Pallas kernels, on_device(): call(finish_kernel, shape(64, 320), [VM] * 5, limit=16, name='finish')  1.62 us
  transfers between devices with their start and end apart: 8, of which 0 were waited for; matrix products, arithmetic and copies ran while one was open for 0% of the time, Pallas kernels for 15%

profile of v4, /device:TPU:2, one launch (start us, length us, event | category | flops | bytes accessed | tf_op | source)
XLA Modules:
  0.0 64.8 jit_solution(12832286029772660696)
XLA Ops:
  0.6 0.0 copy-start.1
  0.6 0.9 %copy-done.1 = f32[4,2,8,320]{3,2,1,0:T(8,128)S(1)} copy-done((f32[4,2,8,320]{3,2,1,0:T(8,128)S(1)}, f32[4,2,8,320]{3,2,1,0:T(8,128)}, u32[]{:S(2)}) %copy-start.1) | copy-done | bytes 81944
  1.6 1.7 %collective-permute-start.1 = (f32[32,320]{1,0:T(8,128)S(1)}, f32[32,320]{1,0:T(8,128)S(1)}, u32[]{:S(2)}, u32[]{:S(2)}) collective-permute-start(f32[32,320]{1,0:T(8,128)S(1)} %get-tuple-element.34), channel_id=1, source_target_pairs={{0,1},{1,2},{2,3},{3,0},{4,5},{5,6},{6,7},{7,4},{8,9},{9,10},{10,1... | collective-permute-start | bytes 122888 | tf_op jit(solution)/shard_map/halo/ppermute | solution.py:597
  3.2 1.7 %collective-permute-start.2 = (f32[32,320]{1,0:T(8,128)S(1)}, f32[32,320]{1,0:T(8,128)S(1)}, u32[]{:S(2)}, u32[]{:S(2)}) collective-permute-start(f32[32,320]{1,0:T(8,128)S(1)} %get-tuple-element.35), channel_id=1, source_target_pairs={{0,3},{1,0},{2,1},{3,2},{4,7},{5,4},{6,5},{7,6},{8,11},{9,8},{10,9... | collective-permute-start | bytes 122888 | tf_op jit(solution)/shard_map/halo/ppermute | solution.py:597
  4.9 0.0 collective-permute-start
  4.9 1.5 %collective-permute-start.3 = (f32[8,320]{1,0:T(8,128)S(1)}, f32[8,320]{1,0:T(8,128)S(1)}, u32[]{:S(2)}, u32[]{:S(2)}) collective-permute-start(f32[8,320]{1,0:T(8,128)S(1)} %get-tuple-element.36), channel_id=1, source_target_pairs={{0,8},{8,16},{16,24},{24,32},{32,40},{40,48},{48,56},{56,64},{64,7... | collective-permute-start | bytes 30728 | tf_op jit(solution)/shard_map/halo/ppermute | solution.py:597
  6.4 0.8 %collective-permute-start.4 = (f32[8,320]{1,0:T(8,128)S(1)}, f32[8,320]{1,0:T(8,128)S(1)}, u32[]{:S(2)}, u32[]{:S(2)}) collective-permute-start(f32[8,320]{1,0:T(8,128)S(1)} %get-tuple-element.37), channel_id=1, source_target_pairs={{0,248},{8,0},{16,8},{24,16},{32,24},{40,32},{48,40},{56,48},{64,5... | collective-permute-start | bytes 30728 | tf_op jit(solution)/shard_map/halo/ppermute | solution.py:597
  7.1 0.0 copy-start
  7.1 0.0 copy-start.2
  7.1 0.0 copy-start.3
  7.1 0.0 copy-start.4
  7.2 4.9 %prepare.1 = (bf16[8,160,320]{2,1,0:T(8,128)(2,1)S(1)}, bf16[8,160,320]{2,1,0:T(8,128)(2,1)S(1)}, bf16[160,256]{1,0:T(8,128)(2,1)S(1)}, bf16[80,256]{1,0:T(8,128)(2,1)S(1)}, f32[248,128]{1,0:T(8,128)S(1)}) custom-call(f32[8,320,320]{2,1,0:T(8,128)} %bitcast.35, bf16[800,512]{1,0:T(8,128)(2,1)} %constant.4.clone.early_in, f32[4,75,2,8]{3,2,1,0:T(2,128)} %bitcast.38, ...), custom_call_target="tpu_custom_call" | custom-call | flops 4000000000 | bytes 8000000 | tf_op jit(solution)/shard_map/prepare/pallas_call | solution.py:620
  12.0 0.0 collective-permute-done.3.below
  12.0 0.0 collective-permute-done.4.above
  12.0 0.0 collective-permute-done.plane
  12.1 0.0 collective-permute-done.1.gy_low
  12.1 0.0 collective-permute-done.2.gy_high
  12.1 0.0 copy-done
  12.1 0.0 copy-done.2
  12.1 0.0 copy-done.3
  12.1 0.0 copy-done.4
  12.1 3.5 %sweep.1 = (f32[64,320]{1,0:T(8,128)}, f32[320,128]{1,0:T(8,128)S(1)}, f32[64,256]{1,0:T(8,128)S(1)}) custom-call(f32[64,320]{1,0:T(8,128)S(1)} %bitcast.29, f32[16,320]{1,0:T(8,128)S(1)} %collective-permute-done.plane, f32[32,320]{1,0:T(8,128)S(1)} %collective-permute-done.1.gy_low, f32[32,320]{1,0:T(8,128)S(1)} %collective-permute-done.2.gy_high, ...), custom_call_target="tpu_custom_call" | custom-call | flops 3000000000 | bytes 8000000 | tf_op jit(solution)/shard_map/sweep/pallas_call | solution.py:639
  15.6 13.6 %all_to_all.10 = f32[8,8,256]{2,1,0:T(8,128)S(1)} all-to-all(f32[8,8,256]{2,1,0:T(8,128)S(1)} %bitcast.31), channel_id=1, replica_groups={{0,8,16,24,32,40,48,56},{64,72,80,88,96,104,112,120},{128,136,144,152,1..., dimensions={0} | all-to-all | bytes 131072 | tf_op jit(solution)/shard_map/all_to_all | solution.py:667
  29.2 7.5 %maps.1 = (bf16[8,8,80,256]{3,2,1,0:T(8,128)(2,1)S(1)}, bf16[8,8,80,256]{3,2,1,0:T(8,128)(2,1)S(1)}, bf16[8,8,80,256]{3,2,1,0:T(8,128)(2,1)S(1)}, bf16[8,80,256]...) custom-call(f32[64,256]{1,0:T(8,128)S(1)} %bitcast.27, ...), custom_call_target="tpu_custom_call" | custom-call | tf_op jit(solution)/shard_map/maps/pallas_call | solution.py:670
  36.8 3.2 %collective-permute-start.5 = (f32[80,256]{1,0:T(8,128)S(1)}, f32[80,256]{1,0:T(8,128)S(1)}, u32[]{:S(2)}, u32[]{:S(2)}) collective-permute-start(f32[80,256]{1,0:T(8,128)S(1)} %get-tuple-element.51.refs_0_), channel_id=1, source_target_pairs={{0,64},{8,72},{16,80},{24,88},{32,96},{40,104},{48,112},{56,120},{... | collective-permute-start | bytes 245768 | tf_op jit(solution)/shard_map/ppermute | solution.py:597
  40.0 1.6 %collective-permute-start.6 = (f32[80,256]{1,0:T(8,128)S(1)}, f32[80,256]{1,0:T(8,128)S(1)}, u32[]{:S(2)}, u32[]{:S(2)}) collective-permute-start(f32[80,256]{1,0:T(8,128)S(1)} %get-tuple-element.51.refs_0_), channel_id=1, source_target_pairs={{0,128},{8,136},{16,144},{24,152},{32,160},{40,168},{48,176},{56,1... | collective-permute-start | bytes 245768 | tf_op jit(solution)/shard_map/ppermute | solution.py:597
  41.6 3.8 %collective-permute-start.7 = (f32[80,256]{1,0:T(8,128)S(1)}, f32[80,256]{1,0:T(8,128)S(1)}, u32[]{:S(2)}, u32[]{:S(2)}) collective-permute-start(f32[80,256]{1,0:T(8,128)S(1)} %get-tuple-element.51.refs_0_), channel_id=1, source_target_pairs={{0,192},{8,200},{16,208},{24,216},{32,224},{40,232},{48,240},{56,2... | collective-permute-start | bytes 245768 | tf_op jit(solution)/shard_map/ppermute | solution.py:597
  45.5 4.9 %base.1 = (f32[64,320]{1,0:T(8,128)S(1)}, bf16[8,320,160]{2,1,0:T(8,128)(2,1)S(1)}, bf16[8,320,160]{2,1,0:T(8,128)(2,1)S(1)}) custom-call(f32[8,320,320]{2,1,0:T(8,128)} %bitcast.36, f32[320,128]{1,0:T(8,128)S(1)} %get-tuple-element.47.turned, f32[64,320]{1,0:T(8,128)S(1)} %bitcast.30, bf16[2912,320]{1,0:T(8,128)(2,1)S(1)} %copy-done), custom_call_target="tpu_custom_call" | custom-call | flops 3000000000 | bytes 16000000 | tf_op jit(solution)/shard_map/base/pallas_call | solution.py:694
  50.4 0.0 collective-permute-done.5.refs_1_
  50.4 0.0 collective-permute-done.6.refs_2_
  50.4 0.0 collective-permute-done.7.refs_3_
  50.4 4.1 %solve.1 = f32[64,256]{1,0:T(8,128)S(1)} custom-call(f32[80,256]{1,0:T(8,128)S(1)} %get-tuple-element.51.refs_0_, f32[80,256]{1,0:T(8,128)S(1)} %collective-permute-done.5.refs_1_, f32[80,256]{1,0:T(8,128)S(1)} %collective-permute-done.6.refs_2_, f32[80,256]{1,0:T(8,128)S(1)} %collective-permute-done.7.refs_3_, ...), custom_call_target="tpu_custom_call" | custom-call | tf_op jit(solution)/shard_map/solve/pallas_call | solution.py:711
  54.5 8.7 %all_to_all.11 = f32[8,8,256]{2,1,0:T(8,128)S(1)} all-to-all(f32[8,8,256]{2,1,0:T(8,128)S(1)} %bitcast.25), channel_id=1, replica_groups={{0,8,16,24,32,40,48,56},{64,72,80,88,96,104,112,120},{128,136,144,152,1..., dimensions={0} | all-to-all | bytes 131072 | tf_op jit(solution)/shard_map/all_to_all | solution.py:667
  63.2 1.6 %finish.1 = f32[64,320]{1,0:T(8,128)} custom-call(f32[64,256]{1,0:T(8,128)S(1)} %bitcast.26, f32[64,320]{1,0:T(8,128)S(1)} %get-tuple-element.60.base, bf16[8,320,160]{2,1,0:T(8,128)(2,1)S(1)} %get-tuple-element.61.columns_high, bf16[8,320,160]{2,1,0:T(8,128)(2,1)S(1)} %get-tuple-element.62.columns_low, bf16[2912,320]{1,0:T(8,128)(2,1)S(1)} %copy-done), custom_call_target="tpu_custom_call" | custom-call | tf_op jit(solution)/shard_map/finish/pallas_call | solution.py:719
  (1 shorter events, 0.0 us)
Async XLA Ops:
  0.6 0.9 %copy-start.1 = (f32[4,2,8,320]{3,2,1,0:T(8,128)S(1)}, f32[4,2,8,320]{3,2,1,0:T(8,128)}, u32[]{:S(2)}) copy-start(f32[4,2,8,320]{3,2,1,0:T(8,128)} %param.11) | copy-start | bytes 245764
  1.6 10.5 %collective-permute-start.1 = (f32[32,320]{1,0:T(8,128)S(1)}, f32[32,320]{1,0:T(8,128)S(1)}, u32[]{:S(2)}, u32[]{:S(2)}) collective-permute-start(f32[32,320]{1,0:T(8,128)S(1)} %get-tuple-element.34), channel_id=1, source_target_pairs={{0,1},{1,2},{2,3},{3,0},{4,5},{5,6},{6,7},{7,4},{8,9},{9,10},{10,1... | collective-permute-start | bytes 122888 | tf_op jit(solution)/shard_map/halo/ppermute | solution.py:597
  3.2 8.9 %collective-permute-start.2 = (f32[32,320]{1,0:T(8,128)S(1)}, f32[32,320]{1,0:T(8,128)S(1)}, u32[]{:S(2)}, u32[]{:S(2)}) collective-permute-start(f32[32,320]{1,0:T(8,128)S(1)} %get-tuple-element.35), channel_id=1, source_target_pairs={{0,3},{1,0},{2,1},{3,2},{4,7},{5,4},{6,5},{7,6},{8,11},{9,8},{10,9... | collective-permute-start | bytes 122888 | tf_op jit(solution)/shard_map/halo/ppermute | solution.py:597
  4.9 7.2 %collective-permute-start = (f32[16,320]{1,0:T(8,128)S(1)}, f32[16,320]{1,0:T(8,128)S(1)}, u32[]{:S(2)}, u32[]{:S(2)}) collective-permute-start(f32[16,320]{1,0:T(8,128)S(1)} %get-tuple-element.33), channel_id=1, source_target_pairs={{0,4},{4,0},{1,5},{5,1},{2,6},{6,2},{3,7},{7,3},{8,12},{12,8},{9,1... | collective-permute-start | bytes 61448 | tf_op jit(solution)/shard_map/halo/ppermute | solution.py:597
  4.9 7.2 %collective-permute-start.3 = (f32[8,320]{1,0:T(8,128)S(1)}, f32[8,320]{1,0:T(8,128)S(1)}, u32[]{:S(2)}, u32[]{:S(2)}) collective-permute-start(f32[8,320]{1,0:T(8,128)S(1)} %get-tuple-element.36), channel_id=1, source_target_pairs={{0,8},{8,16},{16,24},{24,32},{32,40},{40,48},{48,56},{56,64},{64,7... | collective-permute-start | bytes 30728 | tf_op jit(solution)/shard_map/halo/ppermute | solution.py:597
  6.4 5.7 %collective-permute-start.4 = (f32[8,320]{1,0:T(8,128)S(1)}, f32[8,320]{1,0:T(8,128)S(1)}, u32[]{:S(2)}, u32[]{:S(2)}) collective-permute-start(f32[8,320]{1,0:T(8,128)S(1)} %get-tuple-element.37), channel_id=1, source_target_pairs={{0,248},{8,0},{16,8},{24,16},{32,24},{40,32},{48,40},{56,48},{64,5... | collective-permute-start | bytes 30728 | tf_op jit(solution)/shard_map/halo/ppermute | solution.py:597
  7.1 4.9 %copy-start = (bf16[2912,320]{1,0:T(8,128)(2,1)S(1)}, bf16[2912,320]{1,0:T(8,128)(2,1)}, u32[]{:S(2)}) copy-start(bf16[2912,320]{1,0:T(8,128)(2,1)} %constant.5.clone.fixed) | copy-start | bytes 5591044
  7.1 4.9 %copy-start.2 = (f32[4,2,8,320]{3,2,1,0:T(8,128)S(1)}, f32[4,2,8,320]{3,2,1,0:T(8,128)}, u32[]{:S(2)}) copy-start(f32[4,2,8,320]{3,2,1,0:T(8,128)} %param.11) | copy-start | bytes 245764
  7.1 5.0 %copy-start.3 = (f32[4,2,8,320]{3,2,1,0:T(8,128)S(1)}, f32[4,2,8,320]{3,2,1,0:T(8,128)}, u32[]{:S(2)}) copy-start(f32[4,2,8,320]{3,2,1,0:T(8,128)} %param.12) | copy-start | bytes 245764
  7.1 5.0 %copy-start.4 = (f32[4,2,8,320]{3,2,1,0:T(8,128)S(1)}, f32[4,2,8,320]{3,2,1,0:T(8,128)}, u32[]{:S(2)}) copy-start(f32[4,2,8,320]{3,2,1,0:T(8,128)} %param.13) | copy-start | bytes 245764
  36.8 13.6 %collective-permute-start.5 = (f32[80,256]{1,0:T(8,128)S(1)}, f32[80,256]{1,0:T(8,128)S(1)}, u32[]{:S(2)}, u32[]{:S(2)}) collective-permute-start(f32[80,256]{1,0:T(8,128)S(1)} %get-tuple-element.51.refs_0_), channel_id=1, source_target_pairs={{0,64},{8,72},{16,80},{24,88},{32,96},{40,104},{48,112},{56,120},{... | collective-permute-start | bytes 245768 | tf_op jit(solution)/shard_map/ppermute | solution.py:597
  40.0 10.4 %collective-permute-start.6 = (f32[80,256]{1,0:T(8,128)S(1)}, f32[80,256]{1,0:T(8,128)S(1)}, u32[]{:S(2)}, u32[]{:S(2)}) collective-permute-start(f32[80,256]{1,0:T(8,128)S(1)} %get-tuple-element.51.refs_0_), channel_id=1, source_target_pairs={{0,128},{8,136},{16,144},{24,152},{32,160},{40,168},{48,176},{56,1... | collective-permute-start | bytes 245768 | tf_op jit(solution)/shard_map/ppermute | solution.py:597
  41.6 8.8 %collective-permute-start.7 = (f32[80,256]{1,0:T(8,128)S(1)}, f32[80,256]{1,0:T(8,128)S(1)}, u32[]{:S(2)}, u32[]{:S(2)}) collective-permute-start(f32[80,256]{1,0:T(8,128)S(1)} %get-tuple-element.51.refs_0_), channel_id=1, source_target_pairs={{0,192},{8,200},{16,208},{24,216},{32,224},{40,232},{48,240},{56,2... | collective-permute-start | bytes 245768 | tf_op jit(solution)/shard_map/ppermute | solution.py:597

commit v5 on v4

--- a/solution.py
+++ b/solution.py
@@ -101,6 +101,7 @@
         twice,
         eye_320,
         spread,
+        layers,
     ]
     fixed = np.zeros((sum(len(block) for block in blocks), 320), np.float32)
     at = 0
@@ -112,9 +113,16 @@
     return early.astype(jnp.bfloat16), fixed.astype(jnp.bfloat16)
 
 
+SELECT_VOLUME, SELECT_A, SELECT_B, SELECT_LAYERS = (
+    slice(0, 320),
+    slice(320, 640),
+    slice(640, 960),
+    slice(960, 1120),
+)
 SELECT, PLACE_A, PLACE_B, PLACE_C = slice(0, 1120), slice(1120, 1440), slice(1440, 1760), slice(1760, 2080)
-ALONG_HIGH, ALONG_LOW, TWICE = slice(2080, 2144), slice(2144, 2208), slice(2208, 2272)
-EYE, SPREAD = slice(2272, 2592), slice(2592, 2912)
+ALONG, ALONG_HIGH, ALONG_LOW = slice(2080, 2208), slice(2080, 2144), slice(2144, 2208)
+TWICE = slice(2208, 2272)
+EYE, SPREAD, LAYERS = slice(2272, 2592), slice(2592, 2912), slice(2912, 3072)
 SIDE, SPAN, MIRROR, FLIP = 80, 184, 240, 244
 
 
@@ -185,23 +193,32 @@
 def prepare_kernel(
     inverse,
     early_in,
+    fixed_in,
+    flow_in,
     volume_in,
     side_in,
     span_in,
     mirror_in,
     flip_in,
+    high_out,
+    low_out,
     rows_high,
     rows_low,
     fwd_out,
     bwd_out,
     tables,
+    own_out,
+    volume_out,
     held,
     early,
+    fixed,
+    flow,
     volume_jacobian,
     side_jacobian,
     span_jacobian,
     mirror_face,
     edge_flip,
+    flux,
     arrived,
 ):
     pairs = [
@@ -210,16 +227,18 @@
         (span_in, span_jacobian),
         (mirror_in, mirror_face),
         (flip_in, edge_flip),
-        (early_in, early),
+        (flow_in, flow),
+        (fixed_in.at[SELECT], fixed.at[SELECT]),
+        (fixed_in.at[ALONG], fixed.at[ALONG]),
     ]
-    pairs += [(inverse.at[line], held.at[line]) for line in range(LINES)]
+    pairs += [(inverse.at[lax.rem(lax.axis_index("span"), LINES)], held), (early_in, early)]
     copies = [
         pltpu.make_async_copy(source, target, arrived.at[at])
         for at, (source, target) in enumerate(pairs)
     ]
     for copy in copies:
         copy.start()
-    for copy in copies[:6]:
+    for copy in copies[:5]:
         copy.wait()
     for line in range(LINES):
         here = slice(8 * line, 8 * line + 8)
@@ -228,39 +247,33 @@
         tables[SPAN : SPAN + 50, here] = LIFT * span_jacobian[line].reshape(50, 8)
         tables[MIRROR : MIRROR + 4, here] = mirror_face[line].astype(F32)
         tables[FLIP : FLIP + 4, here] = edge_flip[line].astype(F32)
-    for line in range(LINES):
-        copies[6 + line].wait()
-        high, low = split(held[line])
-        layers = early[640:800, 0:320]
-        rows_high[line] = dot(layers, high).astype(BF16)
-        rows_low[line] = dot(layers, low).astype(BF16)
-    mine = lax.rem(lax.axis_index("span"), LINES)
-    both = dot(rows_high[mine], early[0:320]) + dot(rows_low[mine], early[320:640])
+    for copy in copies[5:8]:
+        copy.wait()
+
+    padded = jnp.concatenate([flow[...], jnp.zeros((64, 320), F32)], axis=0)
+    own = sum(dot_nt(fixed[SELECT], part) for part in split(padded))
+    own_out[...] = own[320:]
+    by_variable = slabs_of(own[0:320], 64)
+    for d in range(3):
+        mixed = mix(lambda w, v: tables[d * 25 + w * 5 + v : d * 25 + w * 5 + v + 1, :], by_variable)
+        for w in range(5):
+            flux[d * 64 : d * 64 + 64, w * 128 : w * 128 + 128] = mixed[w]
+    flux_high, flux_low = split(flux[...])
+    volume = dot(fixed[ALONG_HIGH, 0:192], flux_high) + dot(fixed[ALONG_HIGH, 0:192], flux_low)
+    volume = volume + dot(fixed[ALONG_LOW, 0:192], flux_high)
+    for w in range(5):
+        volume_out[w * 64 : w * 64 + 64] = volume[:, w * 128 : w * 128 + 128]
+
+    for copy in copies[8:]:
+        copy.wait()
+    high_out[...], low_out[...] = split(held[...])
+    layers = early[640:800, 0:320]
+    rows_high[...] = dot(layers, high_out[...]).astype(BF16)
+    rows_low[...] = dot(layers, low_out[...]).astype(BF16)
+    both = dot(rows_high[...], early[0:320]) + dot(rows_low[...], early[320:640])
     both = both.astype(BF16)
     fwd_out[...] = both[:, :256]
     bwd_out[...] = both[80:, 256:]
-
-
-def base_kernel(inverse, turned, flow, fixed, base_out, columns_high, columns_low, held, arrived):
-    copies = [
-        pltpu.make_async_copy(inverse.at[line], held.at[line], arrived.at[line])
-        for line in range(LINES)
-    ]
-    for copy in copies:
-        copy.start()
-    load = pair_lanes(turned[...])
-    spread = fixed[SPREAD, 0:160]
-    wide_lane = lanes((320, 128)) % 64
-    total = jnp.zeros((320, 128), F32)
-    for line in range(LINES):
-        copies[line].wait()
-        high, low = split(held[line])
-        total = jnp.where(wide_lane // 8 == line, dot(high, load) + dot(low, load), total)
-        columns_high[line] = dot(high, spread).astype(BF16)
-        columns_low[line] = dot(low, spread).astype(BF16)
-    high, low = split(total)
-    twice = fixed[TWICE, 0:128]
-    base_out[...] = flow[...] + dot_nt(twice, high) + dot_nt(twice, low)
 
 
 def unpack(left, right):
@@ -295,53 +308,50 @@
     source,
     pseudo,
     tables,
-    rows_high,
-    rows_low,
+    own_in,
+    volume_in,
     fixed,
     residual_out,
-    turned_out,
     sent_out,
     extended,
-    flux,
 ):
     gx_at, gy_at = lax.axis_index("gx"), lax.axis_index("gy")
     first_lo = (gx_at > 0).astype(F32)
     second_lo = (gy_at > 0).astype(F32)
     second_hi = (gy_at < lax.axis_size("gy") - 1).astype(F32)
     u = flow[...]
-    extended[0:64] = u
+    nothing = jnp.zeros((64, 320), F32)
+    extended[0:64] = nothing
     extended[64:80] = plane[...] * (1.0 - first_lo)
-    extended[80:112] = jnp.zeros((32, 320), F32)
+    extended[80:112] = nothing[:32]
     extended[112:128] = plane[...] * first_lo
     for i in range(4):
         extended[128 + 16 * i : 136 + 16 * i] = gy_low[8 * i : 8 * i + 8] * second_lo
         extended[136 + 16 * i : 144 + 16 * i] = gy_high[8 * i : 8 * i + 8] * second_hi
+    extended[192:256] = nothing
     position = rows((8, 320))
     for line in range(LINES):
-        extended[192 + 8 * line : 200 + 8 * line] = jnp.where(
+        extended[256 + 8 * line : 264 + 8 * line] = jnp.where(
             position == 0,
             below[line : line + 1],
             jnp.where(position == 7, above[line : line + 1], 0.0),
         )
-    chosen = sum(dot_nt(fixed[SELECT], part) for part in split(extended[...]))
-    near, far = chosen[:, :128], chosen[:, 128:]
+    extended[320:384] = nothing
+
+    def outside(chosen, at):
+        return sum(dot_nt(fixed[chosen], part) for part in split(extended[at : at + 128]))
+
+    near_a = own_in[0:320] + outside(SELECT_A, 0)
+    near_b, far_b = own_in[320:640], outside(SELECT_B, 128)
+    far_layers = outside(SELECT_LAYERS, 256)
     lane = lanes((1, 128))
     table = lambda r: tables[r : r + 1, :]
-
-    by_variable = slabs_of(near[0:320], 64)
-    for d in range(3):
-        mixed = mix(lambda w, v: table(d * 25 + w * 5 + v), by_variable)
-        for w in range(5):
-            flux[d * 64 : d * 64 + 64, w * 128 : w * 128 + 128] = mixed[w]
-    flux_high, flux_low = split(flux[...])
-    volume = dot(fixed[ALONG_HIGH, 0:192], flux_high) + dot(fixed[ALONG_HIGH, 0:192], flux_low)
-    volume = volume + dot(fixed[ALONG_LOW, 0:192], flux_high)
-    pieces = [volume[:, w * 128 : w * 128 + 128] for w in range(5)]
+    pieces = []
 
     for f in range(4):
-        base = 320 + 320 * (f // 2)
-        candidates = [near[base + 80 * n : base + 80 * n + 80] for n in range(4)]
-        outer = [far[base + 80 * n : base + 80 * n + 80] for n in range(4)]
+        near = near_a if f < 2 else near_b
+        candidates = [near[80 * n : 80 * n + 80] for n in range(4)]
+        outer = [far_b[80 * n : 80 * n + 80] for n in range(4)]
         own = candidates[2 * (f % 2)]
         if f == 0:
             shifted = [roll(x, 16) for x in candidates]
@@ -365,14 +375,16 @@
         jump = LIFT * (neighbour - own)
         pieces += mix(lambda w, v: table(SIDE + (w * 5 + v) * 4 + f), slabs_of(jump, 16))
 
-    top, bottom = near[960:1040], near[1040:1120]
-    outer_top, outer_bottom = roll(far[960:1040], 64), roll(far[1040:1120], 64)
+    top, bottom = own_in[640:720], own_in[720:800]
+    outer_top, outer_bottom = far_layers[0:80], far_layers[80:160]
     lower_jump = jnp.where(lane % 8 == 0, outer_top, roll(top, 1)) - bottom
     upper_jump = jnp.where(lane % 8 == 7, outer_bottom, roll(bottom, -1)) - top
     pieces += mix(lambda w, v: table(SPAN + (w * 5 + v) * 2), slabs_of(lower_jump, 16))
     pieces += mix(lambda w, v: table(SPAN + (w * 5 + v) * 2 + 1), slabs_of(upper_jump, 16))
     pieces = [
-        pair_lanes(jnp.concatenate(group, axis=0)) for group in (pieces[:5], pieces[5:25], pieces[25:])
+        pair_lanes(volume_in[...]),
+        pair_lanes(jnp.concatenate(pieces[:20], axis=0)),
+        pair_lanes(jnp.concatenate(pieces[20:], axis=0)),
     ]
     operator = dot(fixed[PLACE_A], pieces[0]) + dot(fixed[PLACE_B], pieces[1])
     operator = operator + dot(fixed[PLACE_C, 0:160], pieces[2])
@@ -382,31 +394,24 @@
     residual = source[...] - (pseudo[...] * u + operator_rows)
     residual_out[...] = residual
 
-    high, low = split(residual)
-    turned = dot_nt(fixed[EYE], jnp.concatenate([high, low], axis=0))
-    turned_out[...] = turned + roll(turned, 64)
-    turned = turned.astype(BF16)
-    trace_lane = lanes((160, 128))
-    traces = jnp.zeros((160, 128), F32)
-    for line in range(LINES):
-        applied = dot(rows_high[line], turned) + dot(rows_low[line], turned)
-        traces = jnp.where(trace_lane % 64 // 8 == line, applied, traces)
-    traces = traces + roll(traces, 64)
-
-    sent = jnp.concatenate([traces, tables[SPAN : SPAN + 56], jnp.zeros((40, 128), F32)], axis=0)
-    sent_out[...] = jnp.transpose(sent)[:64]
+    turned = [jnp.zeros((64, 128), F32), tables[SPAN : SPAN + 56], jnp.zeros((8, 128), F32)]
+    sent_out[:, 256:384] = jnp.transpose(jnp.concatenate(turned, axis=0))[:64]
+    sent_out[:, 0:320] = residual
 
 
 def maps_kernel(
     received,
+    rows_high,
+    rows_low,
     fwd,
     bwd,
+    fixed,
     z_both,
-    v_high,
-    v_low,
+    v_both,
     t_out,
     w_out,
     whole_out,
+    turned_out,
     wide,
     started,
     t_state,
@@ -414,15 +419,21 @@
     bottoms,
     maps,
 ):
-    turned = jnp.transpose(jnp.concatenate([received[...], jnp.zeros((64, 256), F32)], axis=0))
-    jacobians = turned[160:210]
+    last = jnp.concatenate([received[:, 256:384], jnp.zeros((64, 128), F32)], axis=0)
+    jacobians = jnp.transpose(last)[64:114]
+    high, low = split(received[:, 0:320])
+    turned = dot_nt(fixed[EYE], jnp.concatenate([high, low], axis=0))
+    turned_out[...] = turned + roll(turned, 64)
+    turned = turned.astype(BF16)
+    traces = dot(rows_high[...], turned) + dot(rows_low[...], turned)
+    traces = traces + roll(traces, 64)
     trace_lane = lanes((160, 128))
     small_lane, small_row = lanes((80, 128)), rows((80, 128))
     for e in range(SEG):
         for k in range(SEG):
             at = e * SEG + k
             wide[e, k] = jnp.broadcast_to(jacobians[:, at : at + 1], (50, 128))
-        moved = roll(turned[0:160], 80 - 8 * e)
+        moved = roll(traces, 80 - 8 * e)
         started[e] = jnp.where((trace_lane >= 80) & (trace_lane < 88), moved, 0.0)
         t_state[e] = jnp.where(small_lane == small_row, 1.0, 0.0)
         w_state[e] = jnp.where(lanes((80, 256)) == rows((80, 256)) + 88, 1.0, 0.0)
@@ -453,8 +464,8 @@
         for e in range(SEG):
             z = [coupled(e, k, 1, w_state[e, :, half]) for half in (slice(0, 128), slice(128, 256))]
             z_hi, z_lo = split(jnp.concatenate(z, axis=1))
-            v_high[e, k] = z_hi
-            v_low[e, k] = z_lo
+            v_both[e, k, :, 0:256] = z_hi
+            v_both[e, k, :, 256:512] = z_lo
             y = dot(bwd[:, 0:240], jnp.concatenate([z_hi, z_lo, z_hi], axis=0))
             w_state[e, :, 0:128] = y[:, :128] + bottoms[e, k]
             w_state[e, :, 128:256] = y[:, 128:]
@@ -494,7 +505,7 @@
 
 
 def solve_kernel(*refs):
-    *parts, t_in, w_in, z_both, v_high, v_low, out, wholes = refs
+    *parts, t_in, w_in, z_both, v_both, turned, high, low, fixed, out, wholes = refs
     groups = len(parts)
     mine = lax.axis_index("span") // SEG
     for distance, part in enumerate(parts):
@@ -528,33 +539,27 @@
         upper = jnp.where(mine, upper_in[80 * e : 80 * e + 80], upper)
     lower, upper = lower + roll(lower, 64), upper + roll(upper, 64)
     y = jnp.concatenate([lower, jnp.ones((8, 128), F32), upper, jnp.zeros((88, 128), F32)], axis=0)
-    y_both = against_both(y[:128])
-    y = pair_lanes(y)
+    y_both, y_all = against_both(y[:128]), against_both(y)
     lower = jnp.zeros((80, 128), F32)
     upper = jnp.zeros((80, 128), F32)
     for e in range(SEG):
-        v_hi, v_lo = v_high[e].reshape(640, 256), v_low[e].reshape(640, 256)
         c = dot(z_both[e].reshape(640, 256), y_both)
-        d = dot(v_hi, y) + dot(v_lo, y)
+        d = dot(v_both[e].reshape(640, 512), y_all)
         for k in range(SEG):
             mine = small_lane == e * SEG + k
             lower = jnp.where(mine, c[80 * k : 80 * k + 80], lower)
             upper = jnp.where(mine, d[80 * k : 80 * k + 80], upper)
-    both = jnp.concatenate([lower, upper, jnp.zeros((96, 128), F32)], axis=0)
-    out[...] = jnp.transpose(both + roll(both, 64))[:64]
-
-
-def finish_kernel(incoming, base, columns_high, columns_low, fixed, out):
-    high, low = split(incoming[...])
-    load = jnp.concatenate([high, low], axis=0)[:, 0:160]
-    wide_lane = lanes((320, 128)) % 64
-    total = jnp.zeros((320, 128), F32)
-    for line in range(LINES):
-        applied = dot_nt(columns_high[line], load) + dot_nt(columns_low[line], load)
-        total = jnp.where(wide_lane // 8 == line, applied, total)
-    high, low = split(total)
+    both = jnp.concatenate([lower, upper], axis=0)
+    added = dot(fixed[SPREAD, 0:160], pair_lanes(both + roll(both, 64)))
+    load = pair_lanes(turned[...] + added + roll(added, 64))
+    total_high, total_low = split(dot(high[...], load) + dot(low[...], load))
     twice = fixed[TWICE, 0:128]
-    out[...] = base[...] + dot_nt(twice, high) + dot_nt(twice, low)
+    out[:, 0:320] = dot_nt(twice, total_high) + dot_nt(twice, total_low)
+    out[:, 320:384] = jnp.zeros((64, 64), F32)
+
+
+def finish_kernel(incoming, flow, out):
+    out[...] = flow[...] + incoming[:, 0:320]
 
 
 def call(kernel, out_shape, in_specs, scratch=(), limit=16, flops=0, moved=0, name=None):
@@ -617,31 +622,45 @@
         mirror_face.transpose(0, 1, 3, 2).reshape(LINES, 4, SEG),
         edge_flip.transpose(0, 1, 3, 2).reshape(LINES, 4, SEG),
     ]
-    rows_high, rows_low, fwd, bwd, tables = call(
+    high, low, rows_high, rows_low, fwd, bwd, tables, own, volume = call(
         prepare_kernel,
         (
-            shape(LINES, 160, 320, dtype=BF16),
-            shape(LINES, 160, 320, dtype=BF16),
+            shape(320, 320, dtype=BF16),
+            shape(320, 320, dtype=BF16),
+            shape(160, 320, dtype=BF16),
+            shape(160, 320, dtype=BF16),
             shape(160, 256, dtype=BF16),
             shape(80, 256, dtype=BF16),
             shape(248, 128),
+            shape(800, 128),
+            shape(320, 128),
         ),
-        [HBM] * 7,
-        scratch=[pltpu.VMEM((LINES, 320, 320), F32), pltpu.VMEM(early.shape, BF16)]
+        [HBM] * 9,
+        scratch=[
+            pltpu.VMEM((320, 320), F32),
+            pltpu.VMEM(early.shape, BF16),
+            pltpu.VMEM(fixed.shape, BF16),
+            pltpu.VMEM(flow.shape, F32),
+        ]
         + [pltpu.VMEM(x.shape, x.dtype) for x in natural]
-        + [pltpu.SemaphoreType.DMA((LINES + 6,))],
-        limit=24,
+        + [pltpu.VMEM((192, 640), F32), pltpu.SemaphoreType.DMA((10,))],
+        limit=28,
         flops=4_000_000_000,
         moved=8_000_000,
         name="prepare",
-    )(*(pltpu.with_memory_space_constraint(x, pltpu.HBM) for x in (inverse, early, *natural)))
-
-    residual, turned, sent = call(
+    )(
+        *(
+            pltpu.with_memory_space_constraint(x, pltpu.HBM)
+            for x in (inverse, early, fixed, flow, *natural)
+        )
+    )
+
+    residual, sent = call(
         sweep_kernel,
-        (shape(64, 320), shape(320, 128), shape(64, 256)),
+        (shape(64, 320), shape(64, 384)),
         [VM] * 12,
-        scratch=[pltpu.VMEM((256, 320), F32), pltpu.VMEM((192, 640), F32)],
-        limit=20,
+        scratch=[pltpu.VMEM((384, 320), F32)],
+        limit=24,
         flops=3_000_000_000,
         moved=8_000_000,
         name="sweep",
@@ -655,29 +674,29 @@
         source_term.reshape(64, 320),
         pseudo_time.reshape(64, 320),
         tables,
-        rows_high,
-        rows_low,
+        own,
+        volume,
         fixed,
     )
 
     within = [[SEG * g + m for m in range(SEG)] for g in range(groups)]
 
     def exchange(value):
-        value = value.reshape(SEG, 8, 256)
+        value = value.reshape(SEG, 8, 384)
         value = lax.all_to_all(value, "span", 0, 0, axis_index_groups=within, tiled=True)
-        return value.reshape(64, 256)
-
-    z_both, v_high, v_low, t_maps, w_maps, whole = call(
+        return value.reshape(64, 384)
+
+    z_both, v_both, t_maps, w_maps, whole, turned = call(
         maps_kernel,
         (
             shape(SEG, SEG, 80, 256, dtype=BF16),
-            shape(SEG, SEG, 80, 256, dtype=BF16),
-            shape(SEG, SEG, 80, 256, dtype=BF16),
+            shape(SEG, SEG, 80, 512, dtype=BF16),
             shape(SEG, 80, 256, dtype=BF16),
             shape(SEG, 80, 512, dtype=BF16),
             shape(80, 256),
+            shape(320, 128),
         ),
-        [VM] * 3,
+        [VM] * 6,
         scratch=[
             pltpu.VMEM((SEG, SEG, 50, 128), F32),
             pltpu.VMEM((SEG, 160, 128), F32),
@@ -688,36 +707,18 @@
         ],
         limit=28,
         name="maps",
-    )(exchange(sent), fwd, bwd)
+    )(exchange(sent), rows_high, rows_low, fwd, bwd, fixed)
     wholes = [whole] + [ring(whole, "span", SEG * distance) for distance in range(1, groups)]
-    late, turned, _ = lax.optimization_barrier((inverse, turned, whole))
-    base, columns_high, columns_low = call(
-        base_kernel,
-        (
-            shape(64, 320),
-            shape(LINES, 320, 160, dtype=BF16),
-            shape(LINES, 320, 160, dtype=BF16),
-        ),
-        [HBM] + [VM] * 3,
-        scratch=[pltpu.VMEM((LINES, 320, 320), F32), pltpu.SemaphoreType.DMA((LINES,))],
-        limit=16,
-        flops=3_000_000_000,
-        moved=16_000_000,
-        name="base",
-    )(pltpu.with_memory_space_constraint(late, pltpu.HBM), turned, flow, fixed)
-    base, columns_high, columns_low, *wholes = lax.optimization_barrier(
-        (base, columns_high, columns_low, *wholes)
-    )
     answers = call(
         solve_kernel,
-        shape(64, 256),
-        [VM] * (groups + 5),
+        shape(64, 384),
+        [VM] * (groups + 8),
         scratch=[pltpu.VMEM((groups, 80, 256), F32)],
         limit=24,
         name="solve",
-    )(*wholes, t_maps, w_maps, z_both, v_high, v_low)
-    updated = call(finish_kernel, shape(64, 320), [VM] * 5, limit=16, name="finish")(
-        exchange(answers), base, columns_high, columns_low, fixed
+    )(*wholes, t_maps, w_maps, z_both, v_both, turned, high, low, fixed)
+    updated = call(finish_kernel, shape(64, 320), [VM] * 2, limit=4, name="finish")(
+        exchange(answers), flow
     )
     return updated.reshape(flow_state.shape), residual.reshape(flow_state.shape)
 

time: 65.2 us -> 62.8 us (0.963)
  Pallas kernels: 26.5 us -> 18.5 us
  waiting for transfers between devices: 0.02 us -> 5.47 us
  blocking collectives: 22.3 us -> 23.9 us
  starting transfers between devices: 14.3 us -> 13.1 us
    pallas_call x5 -> x4, Pallas kernels: 19 us -> 10.7 us  [the longest x1 4.94 us: on_device(): call(solve_kernel, shape(64, 384), [VM] * (groups + 8), scratch=[pltpu.VM...]
    ppermute x8, waiting for transfers between devices: 0.02 us -> 5.47 us  [ring(): lax.ppermute(value, axis, [(i, (i + step) % count) for i in range(count)])]
    all_to_all x2, blocking collectives: 22.3 us -> 23.9 us  [exchange(): lax.all_to_all(value, 'span', 0, 0, axis_index_groups=within, tiled=True)]
    ppermute x8, starting transfers between devices: 14.3 us -> 13.1 us  [ring(): lax.ppermute(value, axis, [(i, (i + step) % count) for i in range(count)])]
  transfers between devices with their start and end apart: 8 -> 8, of which waited for: 0 -> 2; matrix products, arithmetic and copies ran while one was open for 0% -> 0% of each run, Pallas kernels for 15% -> 5%
where the time goes in v5:
time: 62.8 us; the launch traced here: 62.6 us
  blocking collectives  23.9 us (38%)
  Pallas kernels  18.5 us (29%)
  starting transfers between devices  13.1 us (21%)
  waiting for transfers between devices  5.47 us (9%)
  local copies, waits for them, and re-layouts  0.9 us (1%)
  between operations  0.75 us (1%)
    all_to_all x2, blocking collectives, exchange(): lax.all_to_all(value, 'span', 0, 0, axis_index_groups=within, tiled=True)  23.9 us
    ppermute x8, starting transfers between devices, ring(): lax.ppermute(value, axis, [(i, (i + step) % count) for i in range(count)])  13.1 us
    pallas_call x1, Pallas kernels, on_device(): call(maps_kernel, (shape(SEG, SEG, 80, 256, dtype=BF16), shape(SEG, SEG,...  7.73 us
    ppermute x8, waiting for transfers between devices, ring(): lax.ppermute(value, axis, [(i, (i + step) % count) for i in range(count)])  5.47 us
    pallas_call x1, Pallas kernels, on_device(): call(solve_kernel, shape(64, 384), [VM] * (groups + 8), scratch=[pltpu.VM...  4.94 us
    pallas_call x1, Pallas kernels, on_device(): call(prepare_kernel, (shape(320, 320, dtype=BF16), shape(320, 320, dtype=...  3.36 us
    pallas_call x1, Pallas kernels, on_device(): call(sweep_kernel, (shape(64, 320), shape(64, 384)), [VM] * 12, scratch=[...  1.79 us
  transfers between devices with their start and end apart: 8, of which 2 were waited for; matrix products, arithmetic and copies ran while one was open for 0% of the time, Pallas kernels for 5%

profile of v5, /device:TPU:2, one launch (start us, length us, event | category | flops | bytes accessed | tf_op | source)
XLA Modules:
  0.0 62.6 jit_solution(4174214515430494464)
XLA Ops:
  0.6 0.0 copy-start.1
  0.6 0.9 %copy-done.1 = f32[4,2,8,320]{3,2,1,0:T(8,128)S(1)} copy-done((f32[4,2,8,320]{3,2,1,0:T(8,128)S(1)}, f32[4,2,8,320]{3,2,1,0:T(8,128)}, u32[]{:S(2)}) %copy-start.1) | copy-done | bytes 81944
  1.6 1.6 %collective-permute-start.3 = (f32[8,320]{1,0:T(8,128)S(1)}, f32[8,320]{1,0:T(8,128)S(1)}, u32[]{:S(2)}, u32[]{:S(2)}) collective-permute-start(f32[8,320]{1,0:T(8,128)S(1)} %get-tuple-element.27), channel_id=1, source_target_pairs={{0,8},{8,16},{16,24},{24,32},{32,40},{40,48},{48,56},{56,64},{64,7... | collective-permute-start | bytes 30728 | tf_op jit(solution)/shard_map/halo/ppermute | solution.py:602
  3.1 0.9 %collective-permute-start.4 = (f32[8,320]{1,0:T(8,128)S(1)}, f32[8,320]{1,0:T(8,128)S(1)}, u32[]{:S(2)}, u32[]{:S(2)}) collective-permute-start(f32[8,320]{1,0:T(8,128)S(1)} %get-tuple-element.28), channel_id=1, source_target_pairs={{0,248},{8,0},{16,8},{24,16},{32,24},{40,32},{48,40},{56,48},{64,5... | collective-permute-start | bytes 30728 | tf_op jit(solution)/shard_map/halo/ppermute | solution.py:602
  4.0 0.0 collective-permute-start
  4.0 1.2 %collective-permute-start.1 = (f32[32,320]{1,0:T(8,128)S(1)}, f32[32,320]{1,0:T(8,128)S(1)}, u32[]{:S(2)}, u32[]{:S(2)}) collective-permute-start(f32[32,320]{1,0:T(8,128)S(1)} %get-tuple-element.25), channel_id=1, source_target_pairs={{0,1},{1,2},{2,3},{3,0},{4,5},{5,6},{6,7},{7,4},{8,9},{9,10},{10,1... | collective-permute-start | bytes 122888 | tf_op jit(solution)/shard_map/halo/ppermute | solution.py:602
  5.2 2.0 %collective-permute-start.2 = (f32[32,320]{1,0:T(8,128)S(1)}, f32[32,320]{1,0:T(8,128)S(1)}, u32[]{:S(2)}, u32[]{:S(2)}) collective-permute-start(f32[32,320]{1,0:T(8,128)S(1)} %get-tuple-element.26), channel_id=1, source_target_pairs={{0,3},{1,0},{2,1},{3,2},{4,7},{5,4},{6,5},{7,6},{8,11},{9,8},{10,9... | collective-permute-start | bytes 122888 | tf_op jit(solution)/shard_map/halo/ppermute | solution.py:602
  7.2 0.0 copy-start
  7.2 0.0 copy-start.2
  7.2 0.0 copy-start.3
  7.2 0.0 copy-start.4
  7.2 3.4 %prepare.1 = (bf16[320,320]{1,0:T(8,128)(2,1)S(1)}, bf16[320,320]{1,0:T(8,128)(2,1)S(1)}, bf16[160,320]{1,0:T(8,128)(2,1)S(1)}, bf16[160,320]{1,0:T(8,128)(2,1)S...) custom-call(f32[8,320,320]{2,1,0:T(8,128)} %bitcast.36, ...), custom_call_target="tpu_custom_call" | custom-call | flops 4000000000 | bytes 8000000 | tf_op jit(solution)/shard_map/prepare/pallas_call | solution.py:625
  10.6 0.0 collective-permute-done.3.below
  10.6 0.0 collective-permute-done.4.above
  10.6 0.0 collective-permute-done.plane
  10.6 0.0 collective-permute-done.1.gy_low
  10.7 0.0 collective-permute-done.2.gy_high
  10.7 0.0 copy-done
  10.7 0.0 copy-done.2
  10.7 0.0 copy-done.3
  10.7 0.0 copy-done.4
  10.7 1.8 %sweep.1 = (f32[64,320]{1,0:T(8,128)}, f32[64,384]{1,0:T(8,128)S(1)}) custom-call(f32[64,320]{1,0:T(8,128)S(1)} %bitcast.29, f32[16,320]{1,0:T(8,128)S(1)} %collective-permute-done.plane, f32[32,320]{1,0:T(8,128)S(1)} %collective-permute-done.1.gy_low, f32[32,320]{1,0:T(8,128)S(1)} %collective-permute-done.2.gy_high, ...), custom_call_target="tpu_custom_call" | custom-call | flops 3000000000 | bytes 8000000 | tf_op jit(solution)/shard_map/sweep/pallas_call | solution.py:658
  12.5 13.7 %all_to_all.10 = f32[8,8,384]{2,1,0:T(8,128)S(1)} all-to-all(f32[8,8,384]{2,1,0:T(8,128)S(1)} %bitcast.32), channel_id=1, replica_groups={{0,8,16,24,32,40,48,56},{64,72,80,88,96,104,112,120},{128,136,144,152,1..., dimensions={0} | all-to-all | bytes 196608 | tf_op jit(solution)/shard_map/all_to_all | solution.py:686
  26.2 7.7 %maps.1 = (bf16[8,8,80,256]{3,2,1,0:T(8,128)(2,1)S(1)}, bf16[8,8,80,512]{3,2,1,0:T(8,128)(2,1)S(1)}, bf16[8,80,256]{2,1,0:T(8,128)(2,1)S(1)}, bf16[8,80,512]{2,1...) custom-call(f32[64,384]{1,0:T(8,128)S(1)} %bitcast.26, ...), custom_call_target="tpu_custom_call" | custom-call | tf_op jit(solution)/shard_map/maps/pallas_call | solution.py:689
  33.9 2.4 %collective-permute-start.7 = (f32[80,256]{1,0:T(8,128)S(1)}, f32[80,256]{1,0:T(8,128)S(1)}, u32[]{:S(2)}, u32[]{:S(2)}) collective-permute-start(f32[80,256]{1,0:T(8,128)S(1)} %get-tuple-element.37.refs_0_), channel_id=1, source_target_pairs={{0,192},{8,200},{16,208},{24,216},{32,224},{40,232},{48,240},{56,2... | collective-permute-start | bytes 245768 | tf_op jit(solution)/shard_map/ppermute | solution.py:602
  36.3 2.5 %collective-permute-start.6 = (f32[80,256]{1,0:T(8,128)S(1)}, f32[80,256]{1,0:T(8,128)S(1)}, u32[]{:S(2)}, u32[]{:S(2)}) collective-permute-start(f32[80,256]{1,0:T(8,128)S(1)} %get-tuple-element.37.refs_0_), channel_id=1, source_target_pairs={{0,128},{8,136},{16,144},{24,152},{32,160},{40,168},{48,176},{56,1... | collective-permute-start | bytes 245768 | tf_op jit(solution)/shard_map/ppermute | solution.py:602
  38.9 2.4 %collective-permute-start.5 = (f32[80,256]{1,0:T(8,128)S(1)}, f32[80,256]{1,0:T(8,128)S(1)}, u32[]{:S(2)}, u32[]{:S(2)}) collective-permute-start(f32[80,256]{1,0:T(8,128)S(1)} %get-tuple-element.37.refs_0_), channel_id=1, source_target_pairs={{0,64},{8,72},{16,80},{24,88},{32,96},{40,104},{48,112},{56,120},{... | collective-permute-start | bytes 245768 | tf_op jit(solution)/shard_map/ppermute | solution.py:602
  41.3 0.0 collective-permute-done.7.refs_3_
  41.3 4.5 %collective-permute-done.6.refs_2_ = f32[80,256]{1,0:T(8,128)S(1)} collective-permute-done((f32[80,256]{1,0:T(8,128)S(1)}, f32[80,256]{1,0:T(8,128)S(1)}, u32[]{:S(2)}, u32[]{:S(2)}) %collective-permute-start.6) | collective-permute-done | bytes 81952 | tf_op jit(solution)/shard_map/ppermute | solution.py:602
  45.7 1.0 %collective-permute-done.5.refs_1_ = f32[80,256]{1,0:T(8,128)S(1)} collective-permute-done((f32[80,256]{1,0:T(8,128)S(1)}, f32[80,256]{1,0:T(8,128)S(1)}, u32[]{:S(2)}, u32[]{:S(2)}) %collective-permute-start.5) | collective-permute-done | bytes 81952 | tf_op jit(solution)/shard_map/ppermute | solution.py:602
  46.7 4.9 %solve.1 = f32[64,384]{1,0:T(8,128)S(1)} custom-call(f32[80,256]{1,0:T(8,128)S(1)} %get-tuple-element.37.refs_0_, f32[80,256]{1,0:T(8,128)S(1)} %collective-permute-done.5.refs_1_, f32[80,256]{1,0:T(8,128)S(1)} %collective-permute-done.6.refs_2_, f32[80,256]{1,0:T(8,128)S(1)} %collective-permute-done.7.refs_3_, ...), custom_call_target="tpu_custom_call" | custom-call | tf_op jit(solution)/shard_map/solve/pallas_call | solution.py:712
  51.7 10.2 %all_to_all.11 = f32[8,8,384]{2,1,0:T(8,128)S(1)} all-to-all(f32[8,8,384]{2,1,0:T(8,128)S(1)} %bitcast.25), channel_id=1, replica_groups={{0,8,16,24,32,40,48,56},{64,72,80,88,96,104,112,120},{128,136,144,152,1..., dimensions={0} | all-to-all | bytes 196608 | tf_op jit(solution)/shard_map/all_to_all | solution.py:686
  61.9 0.7 %finish.1 = f32[64,320]{1,0:T(8,128)} custom-call(f32[64,384]{1,0:T(8,128)S(1)} %bitcast.31, f32[64,320]{1,0:T(8,128)S(1)} %bitcast.30), custom_call_target="tpu_custom_call" | custom-call | tf_op jit(solution)/shard_map/finish/pallas_call | solution.py:720
  (1 shorter events, 0.0 us)
Async XLA Ops:
  0.6 0.9 %copy-start.1 = (f32[4,2,8,320]{3,2,1,0:T(8,128)S(1)}, f32[4,2,8,320]{3,2,1,0:T(8,128)}, u32[]{:S(2)}) copy-start(f32[4,2,8,320]{3,2,1,0:T(8,128)} %param.11) | copy-start | bytes 245764
  1.6 9.1 %collective-permute-start.3 = (f32[8,320]{1,0:T(8,128)S(1)}, f32[8,320]{1,0:T(8,128)S(1)}, u32[]{:S(2)}, u32[]{:S(2)}) collective-permute-start(f32[8,320]{1,0:T(8,128)S(1)} %get-tuple-element.27), channel_id=1, source_target_pairs={{0,8},{8,16},{16,24},{24,32},{32,40},{40,48},{48,56},{56,64},{64,7... | collective-permute-start | bytes 30728 | tf_op jit(solution)/shard_map/halo/ppermute | solution.py:602
  3.1 7.5 %collective-permute-start.4 = (f32[8,320]{1,0:T(8,128)S(1)}, f32[8,320]{1,0:T(8,128)S(1)}, u32[]{:S(2)}, u32[]{:S(2)}) collective-permute-start(f32[8,320]{1,0:T(8,128)S(1)} %get-tuple-element.28), channel_id=1, source_target_pairs={{0,248},{8,0},{16,8},{24,16},{32,24},{40,32},{48,40},{56,48},{64,5... | collective-permute-start | bytes 30728 | tf_op jit(solution)/shard_map/halo/ppermute | solution.py:602
  4.0 6.6 %collective-permute-start = (f32[16,320]{1,0:T(8,128)S(1)}, f32[16,320]{1,0:T(8,128)S(1)}, u32[]{:S(2)}, u32[]{:S(2)}) collective-permute-start(f32[16,320]{1,0:T(8,128)S(1)} %get-tuple-element.24), channel_id=1, source_target_pairs={{0,4},{4,0},{1,5},{5,1},{2,6},{6,2},{3,7},{7,3},{8,12},{12,8},{9,1... | collective-permute-start | bytes 61448 | tf_op jit(solution)/shard_map/halo/ppermute | solution.py:602
  4.0 6.7 %collective-permute-start.1 = (f32[32,320]{1,0:T(8,128)S(1)}, f32[32,320]{1,0:T(8,128)S(1)}, u32[]{:S(2)}, u32[]{:S(2)}) collective-permute-start(f32[32,320]{1,0:T(8,128)S(1)} %get-tuple-element.25), channel_id=1, source_target_pairs={{0,1},{1,2},{2,3},{3,0},{4,5},{5,6},{6,7},{7,4},{8,9},{9,10},{10,1... | collective-permute-start | bytes 122888 | tf_op jit(solution)/shard_map/halo/ppermute | solution.py:602
  5.2 5.4 %collective-permute-start.2 = (f32[32,320]{1,0:T(8,128)S(1)}, f32[32,320]{1,0:T(8,128)S(1)}, u32[]{:S(2)}, u32[]{:S(2)}) collective-permute-start(f32[32,320]{1,0:T(8,128)S(1)} %get-tuple-element.26), channel_id=1, source_target_pairs={{0,3},{1,0},{2,1},{3,2},{4,7},{5,4},{6,5},{7,6},{8,11},{9,8},{10,9... | collective-permute-start | bytes 122888 | tf_op jit(solution)/shard_map/halo/ppermute | solution.py:602
  7.2 3.4 %copy-start = (bf16[3072,320]{1,0:T(8,128)(2,1)S(1)}, bf16[3072,320]{1,0:T(8,128)(2,1)}, u32[]{:S(2)}) copy-start(bf16[3072,320]{1,0:T(8,128)(2,1)} %constant.5.clone.fixed_in.fixed.refs_11_) | copy-start | bytes 5898244
  7.2 3.4 %copy-start.2 = (f32[4,2,8,320]{3,2,1,0:T(8,128)S(1)}, f32[4,2,8,320]{3,2,1,0:T(8,128)}, u32[]{:S(2)}) copy-start(f32[4,2,8,320]{3,2,1,0:T(8,128)} %param.11) | copy-start | bytes 245764
  7.2 3.5 %copy-start.3 = (f32[4,2,8,320]{3,2,1,0:T(8,128)S(1)}, f32[4,2,8,320]{3,2,1,0:T(8,128)}, u32[]{:S(2)}) copy-start(f32[4,2,8,320]{3,2,1,0:T(8,128)} %param.12) | copy-start | bytes 245764
  7.2 3.5 %copy-start.4 = (f32[4,2,8,320]{3,2,1,0:T(8,128)S(1)}, f32[4,2,8,320]{3,2,1,0:T(8,128)}, u32[]{:S(2)}) copy-start(f32[4,2,8,320]{3,2,1,0:T(8,128)} %param.13) | copy-start | bytes 245764
  33.9 7.4 %collective-permute-start.7 = (f32[80,256]{1,0:T(8,128)S(1)}, f32[80,256]{1,0:T(8,128)S(1)}, u32[]{:S(2)}, u32[]{:S(2)}) collective-permute-start(f32[80,256]{1,0:T(8,128)S(1)} %get-tuple-element.37.refs_0_), channel_id=1, source_target_pairs={{0,192},{8,200},{16,208},{24,216},{32,224},{40,232},{48,240},{56,2... | collective-permute-start | bytes 245768 | tf_op jit(solution)/shard_map/ppermute | solution.py:602
  36.3 9.4 %collective-permute-start.6 = (f32[80,256]{1,0:T(8,128)S(1)}, f32[80,256]{1,0:T(8,128)S(1)}, u32[]{:S(2)}, u32[]{:S(2)}) collective-permute-start(f32[80,256]{1,0:T(8,128)S(1)} %get-tuple-element.37.refs_0_), channel_id=1, source_target_pairs={{0,128},{8,136},{16,144},{24,152},{32,160},{40,168},{48,176},{56,1... | collective-permute-start | bytes 245768 | tf_op jit(solution)/shard_map/ppermute | solution.py:602
  38.9 7.9 %collective-permute-start.5 = (f32[80,256]{1,0:T(8,128)S(1)}, f32[80,256]{1,0:T(8,128)S(1)}, u32[]{:S(2)}, u32[]{:S(2)}) collective-permute-start(f32[80,256]{1,0:T(8,128)S(1)} %get-tuple-element.37.refs_0_), channel_id=1, source_target_pairs={{0,64},{8,72},{16,80},{24,88},{32,96},{40,104},{48,112},{56,120},{... | collective-permute-start | bytes 245768 | tf_op jit(solution)/shard_map/ppermute | solution.py:602

commit v6 on v5

--- a/solution.py
+++ b/solution.py
@@ -77,7 +77,8 @@
         columns_high[:, base : base + 80] = chosen
         columns_high[:, base + 80 : base + 160] = chosen
         columns_low[:, base + 160 : base + 240] = chosen
-    spread = np.concatenate([bottom, top], axis=1)
+    spread = np.zeros((320, 256))
+    spread[:, :80], spread[:, 128:208] = bottom, top
     eye, d = np.eye(4), derivative_matrix()
     along = np.concatenate(
         [
@@ -90,6 +91,10 @@
     high = along.astype(jnp.bfloat16).astype(np.float64)
     along = np.concatenate([high, high, along - high], axis=1)
     twice = np.concatenate([np.eye(64), np.eye(64)], axis=1)
+    ordered = np.zeros((64, 128))
+    for e in range(8):
+        for k in range(8):
+            ordered[8 * e + k, [8 * k + e, 64 + 8 * k + e]] = 1
     eye_320 = np.eye(320)
     blocks = [
         select,
@@ -102,6 +107,7 @@
         eye_320,
         spread,
         layers,
+        ordered,
     ]
     fixed = np.zeros((sum(len(block) for block in blocks), 320), np.float32)
     at = 0
@@ -123,6 +129,7 @@
 ALONG, ALONG_HIGH, ALONG_LOW = slice(2080, 2208), slice(2080, 2144), slice(2144, 2208)
 TWICE = slice(2208, 2272)
 EYE, SPREAD, LAYERS = slice(2272, 2592), slice(2592, 2912), slice(2912, 3072)
+ORDERED = slice(3072, 3136)
 SIDE, SPAN, MIRROR, FLIP = 80, 184, 240, 244
 
 
@@ -161,12 +168,6 @@
 def pair_lanes(x):
     high = x.astype(BF16).astype(F32)
     return jnp.where(lanes(x.shape) < 64, high, roll(x - high, 64)).astype(BF16)
-
-
-def against_both(x):
-    paired = pair_lanes(x)
-    first = jnp.where(lanes(x.shape) < 64, paired.astype(F32), 0.0).astype(BF16)
-    return jnp.concatenate([paired, first], axis=0)
 
 
 def left_cat(x):
@@ -411,6 +412,7 @@
     t_out,
     w_out,
     whole_out,
+    short_out,
     turned_out,
     wide,
     started,
@@ -475,10 +477,10 @@
     for e in range(SEG):
         maps[e, :, 0:128] = w_state[e, :, 0:128]
         maps[e, :, 128:256] = w_state[e, :, 128:256] + roll(t_state[e], 40)
-    compose(maps, t_out, w_out, whole_out)
-
-
-def compose(maps, t_out, w_out, whole_out):
+    compose(maps, t_out, w_out, whole_out, short_out)
+
+
+def compose(maps, t_out, w_out, whole_out, short_out):
     tall_lane, tall_row = lanes((128, 128)), rows((128, 128))
     zero = jnp.zeros((48, 128), F32)
     parts = [unpack(maps[e, :, 0:128], maps[e, :, 128:256]) for e in range(SEG)]
@@ -487,7 +489,7 @@
     state = fixed + ones
     coupled = []
     for e in range(SEG):
-        t_out[e] = jnp.concatenate(split(state[:80]), axis=1)
+        t_out[e] = state
         y = dot(left_cat(jnp.concatenate(parts[e][:2], axis=0)), right_cat(state))
         coupled.append(y[80:])
         state = jnp.concatenate([y[:80], ones[80:]], axis=0)
@@ -495,66 +497,95 @@
     w0 = jnp.where(tall_lane == tall_row + 88, 1.0, 0.0)
     w1 = jnp.where((tall_lane == tall_row - 40) & (tall_row < 80), 1.0, 0.0)
     for e in range(SEG - 1, -1, -1):
-        w_out[e] = jnp.concatenate(split(jnp.concatenate([w0[:80], w1[:80]], axis=1)), axis=1)
+        w_out[e, :, 0:128] = w0[:80]
+        w_out[e, :, 128:256] = w1[:80]
         w = jnp.concatenate([right_cat(w0), right_cat(w1)], axis=1)
         y = dot(left_cat(parts[e][2]), w)
         w0 = jnp.concatenate([y[:, :128] + coupled[e], zero], axis=0)
         w1 = jnp.concatenate([y[:, 128:], zero], axis=0)
     whole_out[:, 0:128] = w0[:80]
     whole_out[:, 128:256] = w1[:80] + roll(last, 40)
+    groups = lax.axis_size("span") // SEG
+    short_out[...] = jnp.where(lax.axis_index("span") // SEG == groups - 1, w0[:80], last)
+
+
+def against_pair(x):
+    high, low = split(x)
+    upper = jnp.concatenate([high, high], axis=1)
+    return jnp.concatenate([upper, jnp.concatenate([low, jnp.zeros_like(low)], axis=1)], axis=0)
+
+
+def fuse_kernel(
+    z_both, v_both, t_in, w_in, turned, high, low, fixed, r_out, q_out, base_out, gs_high, gs_low
+):
+    for e in range(SEG):
+        state = t_in[e]
+        r = dot_nt(against_pair(jnp.transpose(state)[:96]), z_both[e].reshape(640, 256))
+        r_out[e] = r[:88] + r[96:184]
+        first = jnp.concatenate([state[:88], jnp.zeros((88, 128), F32)], axis=1)
+        both = jnp.concatenate([first, w_in[e], jnp.zeros((88, 256), F32)], axis=0)
+        q = dot_nt(against_pair(jnp.transpose(both)[:176]), v_both[e].reshape(640, 512))
+        q_out[e] = q[:168] + q[176:344]
+    load = pair_lanes(turned[...])
+    total_high, total_low = split(dot(high[...], load) + dot(low[...], load))
+    twice = fixed[TWICE, 0:128]
+    base_out[...] = dot_nt(twice, total_high) + dot_nt(twice, total_low)
+    gs_high[...] = dot(high[...], fixed[SPREAD, 0:256]).astype(BF16)
+    gs_low[...] = dot(low[...], fixed[SPREAD, 0:256]).astype(BF16)
+
+
+def by_element(x):
+    tiles = [x[:, 128 * n : 128 * n + 128] for n in range(5)]
+    lane = lanes((8, 128))
+    out = []
+    for k in range(SEG):
+        at, shift = divmod(80 * k, 128)
+        y = roll(tiles[at], -shift)
+        if shift + 80 > 128:
+            y = jnp.where(lane < 128 - shift, y, roll(tiles[at + 1], -shift))
+        out.append(jnp.where(lane < 80, y, 0.0))
+    return jnp.concatenate(out, axis=0)
 
 
 def solve_kernel(*refs):
-    *parts, t_in, w_in, z_both, v_both, turned, high, low, fixed, out, wholes = refs
+    *parts, r_in, q_in, base, gs_high, gs_low, fixed, out, forwards, crosses, backs_in = refs
     groups = len(parts)
     mine = lax.axis_index("span") // SEG
+    lane = lanes((80, 128))
     for distance, part in enumerate(parts):
-        wholes[lax.rem(mine - distance + groups, groups)] = part[...]
-    lane = lanes((80, 128))
+        group = lax.rem(mine - distance + groups, groups)
+        if distance == 1:
+            pieces = part[...], part[...], part[...]
+        else:
+            pieces = unpack(part[:, 0:128], part[:, 128:256])
+        forwards[group], crosses[group], backs_in[group] = pieces
     one = jnp.where(rows((128, 128)) == 80, 1.0, 0.0)
     zero = jnp.zeros((48, 128), F32)
-    parts = [unpack(wholes[g, :, 0:128], wholes[g, :, 128:256]) for g in range(groups)]
     traces = [one]
     for group in range(groups - 1):
-        y = dot(left_cat(parts[group][0]), right_cat(traces[-1]))
+        y = dot(left_cat(forwards[group]), right_cat(traces[-1]))
         traces.append(jnp.concatenate([y, zero], axis=0) + one)
     backs = [jnp.zeros((128, 128), F32)]
     for group in range(groups - 1, 0, -1):
-        y = dot(left_cat(parts[group][1]), right_cat(traces[group]))
-        y = y + dot(left_cat(parts[group][2]), right_cat(backs[0]))
+        y = dot(left_cat(crosses[group]), right_cat(traces[group]))
+        if group < groups - 1:
+            y = y + dot(left_cat(backs_in[group]), right_cat(backs[0]))
         backs.insert(0, jnp.concatenate([y, zero], axis=0))
     trace, back = traces[0], backs[0]
     for group in range(1, groups):
         trace = jnp.where(mine == group, traces[group], trace)
         back = jnp.where(mine == group, backs[group], back)
-    both = jnp.concatenate([trace[:88], back[:80], jnp.zeros((88, 128), F32)], axis=0)
-    lower_in = dot(t_in[...].reshape(640, 256), against_both(trace))
-    upper_in = dot(w_in[...].reshape(640, 512), against_both(both))
-    small_lane = lane % 64
-    lower = jnp.zeros((80, 128), F32)
-    upper = jnp.zeros((80, 128), F32)
-    for e in range(SEG):
-        mine = small_lane // 8 == e
-        lower = jnp.where(mine, lower_in[80 * e : 80 * e + 80], lower)
-        upper = jnp.where(mine, upper_in[80 * e : 80 * e + 80], upper)
-    lower, upper = lower + roll(lower, 64), upper + roll(upper, 64)
-    y = jnp.concatenate([lower, jnp.ones((8, 128), F32), upper, jnp.zeros((88, 128), F32)], axis=0)
-    y_both, y_all = against_both(y[:128]), against_both(y)
-    lower = jnp.zeros((80, 128), F32)
-    upper = jnp.zeros((80, 128), F32)
-    for e in range(SEG):
-        c = dot(z_both[e].reshape(640, 256), y_both)
-        d = dot(v_both[e].reshape(640, 512), y_all)
-        for k in range(SEG):
-            mine = small_lane == e * SEG + k
-            lower = jnp.where(mine, c[80 * k : 80 * k + 80], lower)
-            upper = jnp.where(mine, d[80 * k : 80 * k + 80], upper)
-    both = jnp.concatenate([lower, upper], axis=0)
-    added = dot(fixed[SPREAD, 0:160], pair_lanes(both + roll(both, 64)))
-    load = pair_lanes(turned[...] + added + roll(added, 64))
-    total_high, total_low = split(dot(high[...], load) + dot(low[...], load))
-    twice = fixed[TWICE, 0:128]
-    out[:, 0:320] = dot_nt(twice, total_high) + dot_nt(twice, total_low)
+    lower_in = jnp.concatenate([trace[:88]] * 5, axis=1)
+    upper_in = jnp.concatenate([lower_in, jnp.concatenate([back[:80]] * 5, axis=1)], axis=0)
+    lower = [jnp.sum(r_in[e] * lower_in, axis=0, keepdims=True) for e in range(SEG)]
+    upper = [jnp.sum(q_in[e] * upper_in, axis=0, keepdims=True) for e in range(SEG)]
+    coupled = [by_element(jnp.concatenate(x, axis=0)) for x in (lower, upper)]
+    high, low = split(jnp.concatenate(coupled, axis=1))
+    coupled = jnp.concatenate([high, low], axis=0)
+    total = dot_nt(gs_high[...], coupled) + dot_nt(gs_low[...], coupled)
+    total_high, total_low = split(total)
+    ordered = fixed[ORDERED, 0:128]
+    out[:, 0:320] = base[...] + dot_nt(ordered, total_high) + dot_nt(ordered, total_low)
     out[:, 320:384] = jnp.zeros((64, 64), F32)
 
 
@@ -686,14 +717,15 @@
         value = lax.all_to_all(value, "span", 0, 0, axis_index_groups=within, tiled=True)
         return value.reshape(64, 384)
 
-    z_both, v_both, t_maps, w_maps, whole, turned = call(
+    z_both, v_both, t_maps, w_maps, whole, short, turned = call(
         maps_kernel,
         (
             shape(SEG, SEG, 80, 256, dtype=BF16),
             shape(SEG, SEG, 80, 512, dtype=BF16),
-            shape(SEG, 80, 256, dtype=BF16),
-            shape(SEG, 80, 512, dtype=BF16),
+            shape(SEG, 128, 128),
+            shape(SEG, 80, 256),
             shape(80, 256),
+            shape(80, 128),
             shape(320, 128),
         ),
         [VM] * 6,
@@ -708,15 +740,33 @@
         limit=28,
         name="maps",
     )(exchange(sent), rows_high, rows_low, fwd, bwd, fixed)
-    wholes = [whole] + [ring(whole, "span", SEG * distance) for distance in range(1, groups)]
+    wholes = [whole] + [
+        ring(short if distance == 1 else whole, "span", SEG * distance)
+        for distance in range(1, groups)
+    ]
+    fused = call(
+        fuse_kernel,
+        (
+            shape(SEG, 88, 640),
+            shape(SEG, 168, 640),
+            shape(64, 320),
+            shape(320, 256, dtype=BF16),
+            shape(320, 256, dtype=BF16),
+        ),
+        [VM] * 8,
+        limit=24,
+        flops=5_000_000_000,
+        moved=12_000_000,
+        name="fuse",
+    )(z_both, v_both, t_maps, w_maps, turned, high, low, fixed)
     answers = call(
         solve_kernel,
         shape(64, 384),
-        [VM] * (groups + 8),
-        scratch=[pltpu.VMEM((groups, 80, 256), F32)],
-        limit=24,
+        [VM] * (groups + 6),
+        scratch=[pltpu.VMEM((groups, 80, 128), F32)] * 3,
+        limit=16,
         name="solve",
-    )(*wholes, t_maps, w_maps, z_both, v_both, turned, high, low, fixed)
+    )(*wholes, *fused, fixed)
     updated = call(finish_kernel, shape(64, 320), [VM] * 2, limit=4, name="finish")(
         exchange(answers), flow
     )

time: 62.8 us -> 59.8 us (0.952)
  waiting for transfers between devices: 5.47 us -> 2.27 us
  blocking collectives: 23.9 us -> 22.6 us
  starting transfers between devices: 13.1 us -> 13.9 us
  Pallas kernels: 18.5 us -> 19.2 us
    ppermute x8, waiting for transfers between devices: 5.47 us -> 2.27 us  [ring(): lax.ppermute(value, axis, [(i, (i + step) % count) for i in range(count)])]
    all_to_all x2, blocking collectives: 23.9 us -> 22.6 us  [exchange(): lax.all_to_all(value, 'span', 0, 0, axis_index_groups=within, tiled=True)]
    ppermute x8, starting transfers between devices: 13.1 us -> 13.9 us  [ring(): lax.ppermute(value, axis, [(i, (i + step) % count) for i in range(count)])]
    pallas_call x1 -> x2, Pallas kernels: 4.94 us -> 5.65 us  [the longest x1 3.85 us: on_device(): call(fuse_kernel, (shape(SEG, 88, 640), shape(SEG, 168, 640), shape(64, 3...]
  transfers between devices with their start and end apart: 8 -> 8, of which waited for: 2 -> 1; matrix products, arithmetic and copies ran while one was open for 0% -> 0% of each run, Pallas kernels for 5% -> 12%
where the time goes in v6:
time: 59.8 us; the launch traced here: 59.7 us
  blocking collectives  22.6 us (38%)
  Pallas kernels  19.2 us (32%)
  starting transfers between devices  13.9 us (23%)
  waiting for transfers between devices  2.27 us (4%)
  local copies, waits for them, and re-layouts  0.9 us (2%)
  between operations  0.76 us (1%)
    all_to_all x2, blocking collectives, exchange(): lax.all_to_all(value, 'span', 0, 0, axis_index_groups=within, tiled=True)  22.6 us
    ppermute x8, starting transfers between devices, ring(): lax.ppermute(value, axis, [(i, (i + step) % count) for i in range(count)])  13.9 us
    pallas_call x1, Pallas kernels, on_device(): call(maps_kernel, (shape(SEG, SEG, 80, 256, dtype=BF16), shape(SEG, SEG,...  7.74 us
    pallas_call x1, Pallas kernels, on_device(): call(fuse_kernel, (shape(SEG, 88, 640), shape(SEG, 168, 640), shape(64, 3...  3.85 us
    pallas_call x1, Pallas kernels, on_device(): call(prepare_kernel, (shape(320, 320, dtype=BF16), shape(320, 320, dtype=...  3.39 us
    ppermute x8, waiting for transfers between devices, ring(): lax.ppermute(value, axis, [(i, (i + step) % count) for i in range(count)])  2.27 us
    pallas_call x1, Pallas kernels, on_device(): call(solve_kernel, shape(64, 384), [VM] * (groups + 6), scratch=[pltpu.VM...  1.8 us
    pallas_call x1, Pallas kernels, on_device(): call(sweep_kernel, (shape(64, 320), shape(64, 384)), [VM] * 12, scratch=[...  1.78 us
  transfers between devices with their start and end apart: 8, of which 1 were waited for; matrix products, arithmetic and copies ran while one was open for 0% of the time, Pallas kernels for 12%

profile of v6, /device:TPU:2, one launch (start us, length us, event | category | flops | bytes accessed | tf_op | source)
XLA Modules:
  0.0 59.7 jit_solution(17277487078851629750)
XLA Ops:
  0.6 0.0 copy-start.1
  0.6 0.9 %copy-done.1 = f32[4,2,8,320]{3,2,1,0:T(8,128)S(1)} copy-done((f32[4,2,8,320]{3,2,1,0:T(8,128)S(1)}, f32[4,2,8,320]{3,2,1,0:T(8,128)}, u32[]{:S(2)}) %copy-start.1) | copy-done | bytes 81944
  1.6 1.7 %collective-permute-start.1 = (f32[32,320]{1,0:T(8,128)S(1)}, f32[32,320]{1,0:T(8,128)S(1)}, u32[]{:S(2)}, u32[]{:S(2)}) collective-permute-start(f32[32,320]{1,0:T(8,128)S(1)} %get-tuple-element.31), channel_id=1, source_target_pairs={{0,1},{1,2},{2,3},{3,0},{4,5},{5,6},{6,7},{7,4},{8,9},{9,10},{10,1... | collective-permute-start | bytes 122888 | tf_op jit(solution)/shard_map/halo/ppermute | solution.py:633
  3.2 1.7 %collective-permute-start.2 = (f32[32,320]{1,0:T(8,128)S(1)}, f32[32,320]{1,0:T(8,128)S(1)}, u32[]{:S(2)}, u32[]{:S(2)}) collective-permute-start(f32[32,320]{1,0:T(8,128)S(1)} %get-tuple-element.32), channel_id=1, source_target_pairs={{0,3},{1,0},{2,1},{3,2},{4,7},{5,4},{6,5},{7,6},{8,11},{9,8},{10,9... | collective-permute-start | bytes 122888 | tf_op jit(solution)/shard_map/halo/ppermute | solution.py:633
  4.9 0.0 collective-permute-start
  4.9 1.5 %collective-permute-start.3 = (f32[8,320]{1,0:T(8,128)S(1)}, f32[8,320]{1,0:T(8,128)S(1)}, u32[]{:S(2)}, u32[]{:S(2)}) collective-permute-start(f32[8,320]{1,0:T(8,128)S(1)} %get-tuple-element.33), channel_id=1, source_target_pairs={{0,8},{8,16},{16,24},{24,32},{32,40},{40,48},{48,56},{56,64},{64,7... | collective-permute-start | bytes 30728 | tf_op jit(solution)/shard_map/halo/ppermute | solution.py:633
  6.4 0.8 %collective-permute-start.4 = (f32[8,320]{1,0:T(8,128)S(1)}, f32[8,320]{1,0:T(8,128)S(1)}, u32[]{:S(2)}, u32[]{:S(2)}) collective-permute-start(f32[8,320]{1,0:T(8,128)S(1)} %get-tuple-element.34), channel_id=1, source_target_pairs={{0,248},{8,0},{16,8},{24,16},{32,24},{40,32},{48,40},{56,48},{64,5... | collective-permute-start | bytes 30728 | tf_op jit(solution)/shard_map/halo/ppermute | solution.py:633
  7.1 0.0 copy-start
  7.1 0.0 copy-start.2
  7.1 0.0 copy-start.3
  7.1 0.0 copy-start.4
  7.2 3.4 %prepare.1 = (bf16[320,320]{1,0:T(8,128)(2,1)S(1)}, bf16[320,320]{1,0:T(8,128)(2,1)S(1)}, bf16[160,320]{1,0:T(8,128)(2,1)S(1)}, bf16[160,320]{1,0:T(8,128)(2,1)S...) custom-call(f32[8,320,320]{2,1,0:T(8,128)} %bitcast.36, ...), custom_call_target="tpu_custom_call" | custom-call | flops 4000000000 | bytes 8000000 | tf_op jit(solution)/shard_map/prepare/pallas_call | solution.py:656
  10.6 0.0 collective-permute-done.3.below
  10.6 0.0 collective-permute-done.4.above
  10.6 0.0 collective-permute-done.plane
  10.6 0.0 collective-permute-done.1.gy_low
  10.6 0.0 collective-permute-done.2.gy_high
  10.6 0.0 copy-done
  10.6 0.0 copy-done.2
  10.6 0.0 copy-done.3
  10.6 0.0 copy-done.4
  10.6 1.8 %sweep.1 = (f32[64,320]{1,0:T(8,128)}, f32[64,384]{1,0:T(8,128)S(1)}) custom-call(f32[64,320]{1,0:T(8,128)S(1)} %bitcast.29, f32[16,320]{1,0:T(8,128)S(1)} %collective-permute-done.plane, f32[32,320]{1,0:T(8,128)S(1)} %collective-permute-done.1.gy_low, f32[32,320]{1,0:T(8,128)S(1)} %collective-permute-done.2.gy_high, ...), custom_call_target="tpu_custom_call" | custom-call | flops 3000000000 | bytes 8000000 | tf_op jit(solution)/shard_map/sweep/pallas_call | solution.py:689
  12.4 13.7 %all_to_all.10 = f32[8,8,384]{2,1,0:T(8,128)S(1)} all-to-all(f32[8,8,384]{2,1,0:T(8,128)S(1)} %bitcast.32), channel_id=1, replica_groups={{0,8,16,24,32,40,48,56},{64,72,80,88,96,104,112,120},{128,136,144,152,1..., dimensions={0} | all-to-all | bytes 196608 | tf_op jit(solution)/shard_map/all_to_all | solution.py:717
  26.1 7.7 %maps.1 = (bf16[8,8,80,256]{3,2,1,0:T(8,128)(2,1)S(1)}, bf16[8,8,80,512]{3,2,1,0:T(8,128)(2,1)S(1)}, f32[8,128,128]{2,1,0:T(8,128)S(1)}, f32[8,80,256]{2,1,0:T(8...) custom-call(f32[64,384]{1,0:T(8,128)S(1)} %bitcast.26, ...), custom_call_target="tpu_custom_call" | custom-call | tf_op jit(solution)/shard_map/maps/pallas_call | solution.py:720
  33.9 4.6 %collective-permute-start.6 = (f32[80,256]{1,0:T(8,128)S(1)}, f32[80,256]{1,0:T(8,128)S(1)}, u32[]{:S(2)}, u32[]{:S(2)}) collective-permute-start(f32[80,256]{1,0:T(8,128)S(1)} %get-tuple-element.43.refs_0_), channel_id=1, source_target_pairs={{0,128},{8,136},{16,144},{24,152},{32,160},{40,168},{48,176},{56,1... | collective-permute-start | bytes 245768 | tf_op jit(solution)/shard_map/ppermute | solution.py:633
  38.4 3.7 %collective-permute-start.7 = (f32[80,256]{1,0:T(8,128)S(1)}, f32[80,256]{1,0:T(8,128)S(1)}, u32[]{:S(2)}, u32[]{:S(2)}) collective-permute-start(f32[80,256]{1,0:T(8,128)S(1)} %get-tuple-element.43.refs_0_), channel_id=1, source_target_pairs={{0,192},{8,200},{16,208},{24,216},{32,224},{40,232},{48,240},{56,2... | collective-permute-start | bytes 245768 | tf_op jit(solution)/shard_map/ppermute | solution.py:633
  42.1 0.0 collective-permute-start.5
  42.1 3.9 %fuse.1 = (f32[8,88,640]{2,1,0:T(8,128)S(1)}, f32[8,168,640]{2,1,0:T(8,128)S(1)}, f32[64,320]{1,0:T(8,128)S(1)}, bf16[320,256]{1,0:T(8,128)(2,1)S(1)}, bf16[320,256]{1,0:T(8,128)(2,1)S(1)}) custom-call(bf16[8,8,80,256]{3,2,1,0:T(8,128)(2,1)S(1)} %get-tuple-element.45.z_both, bf16[8,8,80,512]{3,2,1,0:T(8,128)(2,1)S(1)} %get-tuple-element.46.v_both, ...), custom_call_target="tpu_custom_call" | custom-call | flops 5000000000 | bytes 12000000 | tf_op jit(solution)/shard_map/fuse/pallas_call | solution.py:747
  46.0 2.2 %collective-permute-done.5.refs_1_ = f32[80,128]{1,0:T(8,128)S(1)} collective-permute-done((f32[80,128]{1,0:T(8,128)S(1)}, f32[80,128]{1,0:T(8,128)S(1)}, u32[]{:S(2)}, u32[]{:S(2)}) %collective-permute-start.5) | collective-permute-done | bytes 40992 | tf_op jit(solution)/shard_map/ppermute | solution.py:633
  48.2 0.0 collective-permute-done.6.refs_2_
  48.2 0.0 collective-permute-done.7.refs_3_
  48.2 1.8 %solve.1 = f32[64,384]{1,0:T(8,128)S(1)} custom-call(f32[80,256]{1,0:T(8,128)S(1)} %get-tuple-element.43.refs_0_, f32[80,128]{1,0:T(8,128)S(1)} %collective-permute-done.5.refs_1_, f32[80,256]{1,0:T(8,128)S(1)} %collective-permute-done.6.refs_2_, f32[80,256]{1,0:T(8,128)S(1)} %collective-permute-done.7.refs_3_, f32[8,88,640]{2,1,0:T(8,128)S(1)} %get-tuple-element.52.refs_4_, ...), custom_call_target="tpu_custom_call" | custom-call | tf_op jit(solution)/shard_map/solve/pallas_call | solution.py:762
  50.1 8.9 %all_to_all.11 = f32[8,8,384]{2,1,0:T(8,128)S(1)} all-to-all(f32[8,8,384]{2,1,0:T(8,128)S(1)} %bitcast.25), channel_id=1, replica_groups={{0,8,16,24,32,40,48,56},{64,72,80,88,96,104,112,120},{128,136,144,152,1..., dimensions={0} | all-to-all | bytes 196608 | tf_op jit(solution)/shard_map/all_to_all | solution.py:717
  59.0 0.7 %finish.1 = f32[64,320]{1,0:T(8,128)} custom-call(f32[64,384]{1,0:T(8,128)S(1)} %bitcast.31, f32[64,320]{1,0:T(8,128)S(1)} %bitcast.30), custom_call_target="tpu_custom_call" | custom-call | tf_op jit(solution)/shard_map/finish/pallas_call | solution.py:770
  (1 shorter events, 0.0 us)
Async XLA Ops:
  0.6 0.9 %copy-start.1 = (f32[4,2,8,320]{3,2,1,0:T(8,128)S(1)}, f32[4,2,8,320]{3,2,1,0:T(8,128)}, u32[]{:S(2)}) copy-start(f32[4,2,8,320]{3,2,1,0:T(8,128)} %param.11) | copy-start | bytes 245764
  1.6 9.0 %collective-permute-start.1 = (f32[32,320]{1,0:T(8,128)S(1)}, f32[32,320]{1,0:T(8,128)S(1)}, u32[]{:S(2)}, u32[]{:S(2)}) collective-permute-start(f32[32,320]{1,0:T(8,128)S(1)} %get-tuple-element.31), channel_id=1, source_target_pairs={{0,1},{1,2},{2,3},{3,0},{4,5},{5,6},{6,7},{7,4},{8,9},{9,10},{10,1... | collective-permute-start | bytes 122888 | tf_op jit(solution)/shard_map/halo/ppermute | solution.py:633
  3.2 7.4 %collective-permute-start.2 = (f32[32,320]{1,0:T(8,128)S(1)}, f32[32,320]{1,0:T(8,128)S(1)}, u32[]{:S(2)}, u32[]{:S(2)}) collective-permute-start(f32[32,320]{1,0:T(8,128)S(1)} %get-tuple-element.32), channel_id=1, source_target_pairs={{0,3},{1,0},{2,1},{3,2},{4,7},{5,4},{6,5},{7,6},{8,11},{9,8},{10,9... | collective-permute-start | bytes 122888 | tf_op jit(solution)/shard_map/halo/ppermute | solution.py:633
  4.9 5.7 %collective-permute-start = (f32[16,320]{1,0:T(8,128)S(1)}, f32[16,320]{1,0:T(8,128)S(1)}, u32[]{:S(2)}, u32[]{:S(2)}) collective-permute-start(f32[16,320]{1,0:T(8,128)S(1)} %get-tuple-element.30), channel_id=1, source_target_pairs={{0,4},{4,0},{1,5},{5,1},{2,6},{6,2},{3,7},{7,3},{8,12},{12,8},{9,1... | collective-permute-start | bytes 61448 | tf_op jit(solution)/shard_map/halo/ppermute | solution.py:633
  4.9 5.7 %collective-permute-start.3 = (f32[8,320]{1,0:T(8,128)S(1)}, f32[8,320]{1,0:T(8,128)S(1)}, u32[]{:S(2)}, u32[]{:S(2)}) collective-permute-start(f32[8,320]{1,0:T(8,128)S(1)} %get-tuple-element.33), channel_id=1, source_target_pairs={{0,8},{8,16},{16,24},{24,32},{32,40},{40,48},{48,56},{56,64},{64,7... | collective-permute-start | bytes 30728 | tf_op jit(solution)/shard_map/halo/ppermute | solution.py:633
  6.4 4.2 %collective-permute-start.4 = (f32[8,320]{1,0:T(8,128)S(1)}, f32[8,320]{1,0:T(8,128)S(1)}, u32[]{:S(2)}, u32[]{:S(2)}) collective-permute-start(f32[8,320]{1,0:T(8,128)S(1)} %get-tuple-element.34), channel_id=1, source_target_pairs={{0,248},{8,0},{16,8},{24,16},{32,24},{40,32},{48,40},{56,48},{64,5... | collective-permute-start | bytes 30728 | tf_op jit(solution)/shard_map/halo/ppermute | solution.py:633
  7.1 3.5 %copy-start = (bf16[3136,320]{1,0:T(8,128)(2,1)S(1)}, bf16[3136,320]{1,0:T(8,128)(2,1)}, u32[]{:S(2)}) copy-start(bf16[3136,320]{1,0:T(8,128)(2,1)} %constant.5.clone.fixed_in.fixed.refs_9_) | copy-start | bytes 6021124
  7.1 3.5 %copy-start.2 = (f32[4,2,8,320]{3,2,1,0:T(8,128)S(1)}, f32[4,2,8,320]{3,2,1,0:T(8,128)}, u32[]{:S(2)}) copy-start(f32[4,2,8,320]{3,2,1,0:T(8,128)} %param.11) | copy-start | bytes 245764
  7.1 3.5 %copy-start.3 = (f32[4,2,8,320]{3,2,1,0:T(8,128)S(1)}, f32[4,2,8,320]{3,2,1,0:T(8,128)}, u32[]{:S(2)}) copy-start(f32[4,2,8,320]{3,2,1,0:T(8,128)} %param.12) | copy-start | bytes 245764
  7.1 3.5 %copy-start.4 = (f32[4,2,8,320]{3,2,1,0:T(8,128)S(1)}, f32[4,2,8,320]{3,2,1,0:T(8,128)}, u32[]{:S(2)}) copy-start(f32[4,2,8,320]{3,2,1,0:T(8,128)} %param.13) | copy-start | bytes 245764
  33.9 14.4 %collective-permute-start.6 = (f32[80,256]{1,0:T(8,128)S(1)}, f32[80,256]{1,0:T(8,128)S(1)}, u32[]{:S(2)}, u32[]{:S(2)}) collective-permute-start(f32[80,256]{1,0:T(8,128)S(1)} %get-tuple-element.43.refs_0_), channel_id=1, source_target_pairs={{0,128},{8,136},{16,144},{24,152},{32,160},{40,168},{48,176},{56,1... | collective-permute-start | bytes 245768 | tf_op jit(solution)/shard_map/ppermute | solution.py:633
  38.4 9.8 %collective-permute-start.7 = (f32[80,256]{1,0:T(8,128)S(1)}, f32[80,256]{1,0:T(8,128)S(1)}, u32[]{:S(2)}, u32[]{:S(2)}) collective-permute-start(f32[80,256]{1,0:T(8,128)S(1)} %get-tuple-element.43.refs_0_), channel_id=1, source_target_pairs={{0,192},{8,200},{16,208},{24,216},{32,224},{40,232},{48,240},{56,2... | collective-permute-start | bytes 245768 | tf_op jit(solution)/shard_map/ppermute | solution.py:633
  42.1 6.1 %collective-permute-start.5 = (f32[80,128]{1,0:T(8,128)S(1)}, f32[80,128]{1,0:T(8,128)S(1)}, u32[]{:S(2)}, u32[]{:S(2)}) collective-permute-start(f32[80,128]{1,0:T(8,128)S(1)} %get-tuple-element.44), channel_id=1, source_target_pairs={{0,64},{8,72},{16,80},{24,88},{32,96},{40,104},{48,112},{56,120},{... | collective-permute-start | bytes 122888 | tf_op jit(solution)/shard_map/ppermute | solution.py:633

commit v7 on v6

--- a/solution.py
+++ b/solution.py
@@ -299,28 +299,15 @@
     return [x[v * size : (v + 1) * size] for v in range(5)]
 
 
-def sweep_kernel(
-    flow,
-    plane,
-    gy_low,
-    gy_high,
-    below,
-    above,
-    source,
-    pseudo,
-    tables,
-    own_in,
-    volume_in,
-    fixed,
-    residual_out,
-    sent_out,
-    extended,
-):
+def outside(fixed, chosen, values):
+    return sum(dot_nt(fixed[chosen], part) for part in split(values))
+
+
+def faces_kernel(plane, gy_low, gy_high, tables, own_in, volume_in, fixed, operator_out, extended):
     gx_at, gy_at = lax.axis_index("gx"), lax.axis_index("gy")
     first_lo = (gx_at > 0).astype(F32)
     second_lo = (gy_at > 0).astype(F32)
     second_hi = (gy_at < lax.axis_size("gy") - 1).astype(F32)
-    u = flow[...]
     nothing = jnp.zeros((64, 320), F32)
     extended[0:64] = nothing
     extended[64:80] = plane[...] * (1.0 - first_lo)
@@ -330,21 +317,8 @@
         extended[128 + 16 * i : 136 + 16 * i] = gy_low[8 * i : 8 * i + 8] * second_lo
         extended[136 + 16 * i : 144 + 16 * i] = gy_high[8 * i : 8 * i + 8] * second_hi
     extended[192:256] = nothing
-    position = rows((8, 320))
-    for line in range(LINES):
-        extended[256 + 8 * line : 264 + 8 * line] = jnp.where(
-            position == 0,
-            below[line : line + 1],
-            jnp.where(position == 7, above[line : line + 1], 0.0),
-        )
-    extended[320:384] = nothing
-
-    def outside(chosen, at):
-        return sum(dot_nt(fixed[chosen], part) for part in split(extended[at : at + 128]))
-
-    near_a = own_in[0:320] + outside(SELECT_A, 0)
-    near_b, far_b = own_in[320:640], outside(SELECT_B, 128)
-    far_layers = outside(SELECT_LAYERS, 256)
+    near_a = own_in[0:320] + outside(fixed, SELECT_A, extended[0:128])
+    near_b, far_b = own_in[320:640], outside(fixed, SELECT_B, extended[128:256])
     lane = lanes((1, 128))
     table = lambda r: tables[r : r + 1, :]
     pieces = []
@@ -376,23 +350,37 @@
         jump = LIFT * (neighbour - own)
         pieces += mix(lambda w, v: table(SIDE + (w * 5 + v) * 4 + f), slabs_of(jump, 16))
 
+    operator = dot(fixed[PLACE_A], pair_lanes(volume_in[...]))
+    operator_out[...] = operator + dot(fixed[PLACE_B], pair_lanes(jnp.concatenate(pieces, axis=0)))
+
+
+def sweep_kernel(
+    flow, below, above, source, pseudo, tables, own_in, operator_in, fixed, residual_out, sent_out, extended
+):
+    position = rows((8, 320))
+    for line in range(LINES):
+        extended[8 * line : 8 * line + 8] = jnp.where(
+            position == 0,
+            below[line : line + 1],
+            jnp.where(position == 7, above[line : line + 1], 0.0),
+        )
+    extended[64:128] = jnp.zeros((64, 320), F32)
+    far_layers = outside(fixed, SELECT_LAYERS, extended[...])
+    lane = lanes((1, 128))
+    table = lambda r: tables[r : r + 1, :]
+    pieces = []
     top, bottom = own_in[640:720], own_in[720:800]
     outer_top, outer_bottom = far_layers[0:80], far_layers[80:160]
     lower_jump = jnp.where(lane % 8 == 0, outer_top, roll(top, 1)) - bottom
     upper_jump = jnp.where(lane % 8 == 7, outer_bottom, roll(bottom, -1)) - top
     pieces += mix(lambda w, v: table(SPAN + (w * 5 + v) * 2), slabs_of(lower_jump, 16))
     pieces += mix(lambda w, v: table(SPAN + (w * 5 + v) * 2 + 1), slabs_of(upper_jump, 16))
-    pieces = [
-        pair_lanes(volume_in[...]),
-        pair_lanes(jnp.concatenate(pieces[:20], axis=0)),
-        pair_lanes(jnp.concatenate(pieces[20:], axis=0)),
-    ]
-    operator = dot(fixed[PLACE_A], pieces[0]) + dot(fixed[PLACE_B], pieces[1])
-    operator = operator + dot(fixed[PLACE_C, 0:160], pieces[2])
+    pieces = pair_lanes(jnp.concatenate(pieces, axis=0))
+    operator = operator_in[...] + dot(fixed[PLACE_C, 0:160], pieces)
     operator_high, operator_low = split(operator)
     twice = fixed[TWICE, 0:128]
     operator_rows = dot_nt(twice, operator_high) + dot_nt(twice, operator_low)
-    residual = source[...] - (pseudo[...] * u + operator_rows)
+    residual = source[...] - (pseudo[...] * flow[...] + operator_rows)
     residual_out[...] = residual
 
     turned = [jnp.zeros((64, 128), F32), tables[SPAN : SPAN + 56], jnp.zeros((8, 128), F32)]
@@ -419,7 +407,6 @@
     t_state,
     w_state,
     bottoms,
-    maps,
 ):
     last = jnp.concatenate([received[:, 256:384], jnp.zeros((64, 128), F32)], axis=0)
     jacobians = jnp.transpose(last)[64:114]
@@ -444,7 +431,7 @@
         out = mix(lambda w, v: wide[e, k, pl.ds((w * 5 + v) * 2 + side, 1)], slabs_of(state, 16))
         return jnp.concatenate(out, axis=0)
 
-    def forward(k, carry):
+    for k in range(SEG):
         mine = small_lane == 80 + k
         for pair in range(0, SEG, 2):
             cats = []
@@ -457,11 +444,12 @@
             for e, y in ((pair, both[:, :128]), (pair + 1, both[:, 128:])):
                 t_state[e] = y[:80] + jnp.where(mine, started[e, 0:80], 0.0)
                 bottoms[e, k] = y[80:] + jnp.where(mine, started[e, 80:160], 0.0)
-        return carry
-
-    lax.fori_loop(0, SEG, forward, 0, unroll=True)
-
-    def backward(step, carry):
+
+    tall_lane, tall_row = lanes((128, 128)), rows((128, 128))
+    ones = jnp.where((tall_row >= 80) & (tall_row < 88) & (tall_lane == 80), 1.0, 0.0)
+    state = jnp.where((tall_row < 80) & (tall_lane == tall_row), 1.0, 0.0) + ones
+    states = []
+    for step in range(SEG):
         k = SEG - 1 - step
         for e in range(SEG):
             z = [coupled(e, k, 1, w_state[e, :, half]) for half in (slice(0, 128), slice(128, 256))]
@@ -471,42 +459,28 @@
             y = dot(bwd[:, 0:240], jnp.concatenate([z_hi, z_lo, z_hi], axis=0))
             w_state[e, :, 0:128] = y[:, :128] + bottoms[e, k]
             w_state[e, :, 128:256] = y[:, 128:]
-        return carry
-
-    lax.fori_loop(0, SEG, backward, 0, unroll=True)
-    for e in range(SEG):
-        maps[e, :, 0:128] = w_state[e, :, 0:128]
-        maps[e, :, 128:256] = w_state[e, :, 128:256] + roll(t_state[e], 40)
-    compose(maps, t_out, w_out, whole_out, short_out)
-
-
-def compose(maps, t_out, w_out, whole_out, short_out):
-    tall_lane, tall_row = lanes((128, 128)), rows((128, 128))
+        t_out[step] = state
+        states.append(right_cat(state))
+        y = dot(left_cat(t_state[step]), states[-1])
+        state = jnp.concatenate([y, ones[80:]], axis=0)
+
+    parts = [unpack(w_state[e, :, 0:128], w_state[e, :, 128:256])[1:] for e in range(SEG)]
+    crossed = [dot(left_cat(parts[e][0]), states[e]) for e in range(SEG)]
+    lefts = [left_cat(parts[e][1]) for e in range(SEG)]
     zero = jnp.zeros((48, 128), F32)
-    parts = [unpack(maps[e, :, 0:128], maps[e, :, 128:256]) for e in range(SEG)]
-    fixed = jnp.where((tall_row < 80) & (tall_lane == tall_row), 1.0, 0.0)
-    ones = jnp.where((tall_row >= 80) & (tall_row < 88) & (tall_lane == 80), 1.0, 0.0)
-    state = fixed + ones
-    coupled = []
-    for e in range(SEG):
-        t_out[e] = state
-        y = dot(left_cat(jnp.concatenate(parts[e][:2], axis=0)), right_cat(state))
-        coupled.append(y[80:])
-        state = jnp.concatenate([y[:80], ones[80:]], axis=0)
-    last = state[:80]
     w0 = jnp.where(tall_lane == tall_row + 88, 1.0, 0.0)
     w1 = jnp.where((tall_lane == tall_row - 40) & (tall_row < 80), 1.0, 0.0)
     for e in range(SEG - 1, -1, -1):
         w_out[e, :, 0:128] = w0[:80]
         w_out[e, :, 128:256] = w1[:80]
-        w = jnp.concatenate([right_cat(w0), right_cat(w1)], axis=1)
-        y = dot(left_cat(parts[e][2]), w)
-        w0 = jnp.concatenate([y[:, :128] + coupled[e], zero], axis=0)
+        y = dot(lefts[e], jnp.concatenate([right_cat(w0), right_cat(w1)], axis=1))
+        w0 = jnp.concatenate([y[:, :128] + crossed[e], zero], axis=0)
         w1 = jnp.concatenate([y[:, 128:], zero], axis=0)
     whole_out[:, 0:128] = w0[:80]
-    whole_out[:, 128:256] = w1[:80] + roll(last, 40)
+    whole_out[:, 128:256] = w1[:80] + roll(state[:80], 40)
     groups = lax.axis_size("span") // SEG
-    short_out[...] = jnp.where(lax.axis_index("span") // SEG == groups - 1, w0[:80], last)
+    last = lax.axis_index("span") // SEG == groups - 1
+    short_out[...] = jnp.where(last, w0[:80], state[:80])
 
 
 def against_pair(x):
@@ -686,27 +660,34 @@
         )
     )
 
+    operator = call(
+        faces_kernel,
+        shape(320, 128),
+        [VM] * 7,
+        scratch=[pltpu.VMEM((256, 320), F32)],
+        limit=16,
+        flops=1_000_000_000,
+        moved=3_000_000,
+        name="faces",
+    )(plane, gy_low, gy_high, tables, own, volume, fixed)
     residual, sent = call(
         sweep_kernel,
         (shape(64, 320), shape(64, 384)),
-        [VM] * 12,
-        scratch=[pltpu.VMEM((384, 320), F32)],
-        limit=24,
-        flops=3_000_000_000,
-        moved=8_000_000,
+        [VM] * 9,
+        scratch=[pltpu.VMEM((128, 320), F32)],
+        limit=16,
+        flops=1_000_000_000,
+        moved=3_000_000,
         name="sweep",
     )(
         flow,
-        plane,
-        gy_low,
-        gy_high,
         below,
         above,
         source_term.reshape(64, 320),
         pseudo_time.reshape(64, 320),
         tables,
         own,
-        volume,
+        operator,
         fixed,
     )
 
@@ -735,7 +716,6 @@
             pltpu.VMEM((SEG, 80, 128), F32),
             pltpu.VMEM((SEG, 80, 256), F32),
             pltpu.VMEM((SEG, SEG, 80, 128), F32),
-            pltpu.VMEM((SEG, 80, 256), F32),
         ],
         limit=28,
         name="maps",

time: 59.8 us -> 58.6 us (0.980)
  starting transfers between devices: 13.9 us -> 13.1 us
    pallas_call x1, Pallas kernels: 7.74 us -> 6.92 us  [on_device(): call(maps_kernel, (shape(SEG, SEG, 80, 256, dtype=BF16), shape(SEG, SEG,...]
    ppermute x8, starting transfers between devices: 13.9 us -> 13.1 us  [ring(): lax.ppermute(value, axis, [(i, (i + step) % count) for i in range(count)])]
    pallas_call x1 -> x2, Pallas kernels: 1.78 us -> 2.21 us  [the longest x1 1.37 us: on_device(): call(sweep_kernel, (shape(64, 320), shape(64, 384)), [VM] * 9, scratch=[p...]
  transfers between devices with their start and end apart: 8 -> 8, of which waited for: 1 -> 1; matrix products, arithmetic and copies ran while one was open for 0% -> 0% of each run, Pallas kernels for 12% -> 14%
where the time goes in v7:
time: 58.6 us; the launch traced here: 58.4 us
  blocking collectives  22.6 us (39%)
  Pallas kernels  18.7 us (32%)
  starting transfers between devices  13.1 us (22%)
  waiting for transfers between devices  2.23 us (4%)
  local copies, waits for them, and re-layouts  0.93 us (2%)
  between operations  0.77 us (1%)
    all_to_all x2, blocking collectives, exchange(): lax.all_to_all(value, 'span', 0, 0, axis_index_groups=within, tiled=True)  22.6 us
    ppermute x8, starting transfers between devices, ring(): lax.ppermute(value, axis, [(i, (i + step) % count) for i in range(count)])  13.1 us
    pallas_call x1, Pallas kernels, on_device(): call(maps_kernel, (shape(SEG, SEG, 80, 256, dtype=BF16), shape(SEG, SEG,...  6.92 us
    pallas_call x1, Pallas kernels, on_device(): call(fuse_kernel, (shape(SEG, 88, 640), shape(SEG, 168, 640), shape(64, 3...  3.85 us
    pallas_call x1, Pallas kernels, on_device(): call(prepare_kernel, (shape(320, 320, dtype=BF16), shape(320, 320, dtype=...  3.29 us
    ppermute x8, waiting for transfers between devices, ring(): lax.ppermute(value, axis, [(i, (i + step) % count) for i in range(count)])  2.23 us
    pallas_call x1, Pallas kernels, on_device(): call(solve_kernel, shape(64, 384), [VM] * (groups + 6), scratch=[pltpu.VM...  1.8 us
    pallas_call x1, Pallas kernels, on_device(): call(sweep_kernel, (shape(64, 320), shape(64, 384)), [VM] * 9, scratch=[p...  1.37 us
  transfers between devices with their start and end apart: 8, of which 1 were waited for; matrix products, arithmetic and copies ran while one was open for 0% of the time, Pallas kernels for 14%

profile of v7, /device:TPU:2, one launch (start us, length us, event | category | flops | bytes accessed | tf_op | source)
XLA Modules:
  0.0 58.4 jit_solution(8585816212179454035)
XLA Ops:
  0.6 0.0 copy-start.1
  0.6 0.9 %copy-done.1 = f32[4,2,8,320]{3,2,1,0:T(8,128)S(1)} copy-done((f32[4,2,8,320]{3,2,1,0:T(8,128)S(1)}, f32[4,2,8,320]{3,2,1,0:T(8,128)}, u32[]{:S(2)}) %copy-start.1) | copy-done | bytes 81944
  1.6 1.7 %collective-permute-start.3 = (f32[32,320]{1,0:T(8,128)S(1)}, f32[32,320]{1,0:T(8,128)S(1)}, u32[]{:S(2)}, u32[]{:S(2)}) collective-permute-start(f32[32,320]{1,0:T(8,128)S(1)} %get-tuple-element.35), channel_id=1, source_target_pairs={{0,1},{1,2},{2,3},{3,0},{4,5},{5,6},{6,7},{7,4},{8,9},{9,10},{10,1... | collective-permute-start | bytes 122888 | tf_op jit(solution)/shard_map/halo/ppermute | solution.py:607
  3.2 1.7 %collective-permute-start.4 = (f32[32,320]{1,0:T(8,128)S(1)}, f32[32,320]{1,0:T(8,128)S(1)}, u32[]{:S(2)}, u32[]{:S(2)}) collective-permute-start(f32[32,320]{1,0:T(8,128)S(1)} %get-tuple-element.36), channel_id=1, source_target_pairs={{0,3},{1,0},{2,1},{3,2},{4,7},{5,4},{6,5},{7,6},{8,11},{9,8},{10,9... | collective-permute-start | bytes 122888 | tf_op jit(solution)/shard_map/halo/ppermute | solution.py:607
  4.9 0.0 collective-permute-start.2
  4.9 1.5 %collective-permute-start = (f32[8,320]{1,0:T(8,128)S(1)}, f32[8,320]{1,0:T(8,128)S(1)}, u32[]{:S(2)}, u32[]{:S(2)}) collective-permute-start(f32[8,320]{1,0:T(8,128)S(1)} %get-tuple-element.30), channel_id=1, source_target_pairs={{0,8},{8,16},{16,24},{24,32},{32,40},{40,48},{48,56},{56,64},{64,7... | collective-permute-start | bytes 30728 | tf_op jit(solution)/shard_map/halo/ppermute | solution.py:607
  6.4 0.8 %collective-permute-start.1 = (f32[8,320]{1,0:T(8,128)S(1)}, f32[8,320]{1,0:T(8,128)S(1)}, u32[]{:S(2)}, u32[]{:S(2)}) collective-permute-start(f32[8,320]{1,0:T(8,128)S(1)} %get-tuple-element.31), channel_id=1, source_target_pairs={{0,248},{8,0},{16,8},{24,16},{32,24},{40,32},{48,40},{56,48},{64,5... | collective-permute-start | bytes 30728 | tf_op jit(solution)/shard_map/halo/ppermute | solution.py:607
  7.1 0.0 copy-start
  7.1 3.3 %prepare.1 = (bf16[320,320]{1,0:T(8,128)(2,1)S(1)}, bf16[320,320]{1,0:T(8,128)(2,1)S(1)}, bf16[160,320]{1,0:T(8,128)(2,1)S(1)}, bf16[160,320]{1,0:T(8,128)(2,1)S...) custom-call(f32[8,320,320]{2,1,0:T(8,128)} %bitcast.36, ...), custom_call_target="tpu_custom_call" | custom-call | flops 4000000000 | bytes 8000000 | tf_op jit(solution)/shard_map/prepare/pallas_call | solution.py:630
  10.4 0.0 copy-start.2
  10.5 0.0 copy-start.3
  10.5 0.0 copy-start.4
  10.5 0.0 collective-permute-done.2.plane
  10.5 0.0 collective-permute-done.3.gy_low
  10.5 0.0 collective-permute-done.4.gy_high
  10.5 0.0 copy-done
  10.5 0.8 %faces.1.operator_in = f32[320,128]{1,0:T(8,128)S(1)} custom-call(f32[16,320]{1,0:T(8,128)S(1)} %collective-permute-done.2.plane, f32[32,320]{1,0:T(8,128)S(1)} %collective-permute-done.3.gy_low, f32[32,320]{1,0:T(8,128)S(1)} %collective-permute-done.4.gy_high, f32[248,128]{1,0:T(8,128)S(1)} %get-tuple-element.32.tables, ...), custom_call_target="tpu_custom_call" | custom-call | flops 1000000000 | bytes 3000000 | tf_op jit(solution)/shard_map/faces/pallas_call | solution.py:663
  11.4 0.0 collective-permute-done.below
  11.4 0.0 collective-permute-done.1.above
  11.4 0.0 copy-done.2
  11.4 0.0 copy-done.3
  11.4 0.0 copy-done.4
  11.4 1.4 %sweep.1 = (f32[64,320]{1,0:T(8,128)}, f32[64,384]{1,0:T(8,128)S(1)}) custom-call(f32[64,320]{1,0:T(8,128)S(1)} %bitcast.29, f32[8,320]{1,0:T(8,128)S(1)} %collective-permute-done.below, f32[8,320]{1,0:T(8,128)S(1)} %collective-permute-done.1.above, f32[64,320]{1,0:T(8,128)S(1)} %bitcast.33, f32[64,320]{1,0:T(8,128)S(1)} %bitcast.34, ...), custom_call_target="tpu_custom_call" | custom-call | flops 1000000000 | bytes 3000000 | tf_op jit(solution)/shard_map/sweep/pallas_call | solution.py:673
  12.8 13.7 %all_to_all.10 = f32[8,8,384]{2,1,0:T(8,128)S(1)} all-to-all(f32[8,8,384]{2,1,0:T(8,128)S(1)} %bitcast.32), channel_id=1, replica_groups={{0,8,16,24,32,40,48,56},{64,72,80,88,96,104,112,120},{128,136,144,152,1..., dimensions={0} | all-to-all | bytes 196608 | tf_op jit(solution)/shard_map/all_to_all | solution.py:698
  26.5 6.9 %maps.1 = (bf16[8,8,80,256]{3,2,1,0:T(8,128)(2,1)S(1)}, bf16[8,8,80,512]{3,2,1,0:T(8,128)(2,1)S(1)}, f32[8,128,128]{2,1,0:T(8,128)S(1)}, f32[8,80,256]{2,1,0:T(8...) custom-call(f32[64,384]{1,0:T(8,128)S(1)} %bitcast.26, ...), custom_call_target="tpu_custom_call" | custom-call | tf_op jit(solution)/shard_map/maps/pallas_call | solution.py:701
  33.4 4.6 %collective-permute-start.6 = (f32[80,256]{1,0:T(8,128)S(1)}, f32[80,256]{1,0:T(8,128)S(1)}, u32[]{:S(2)}, u32[]{:S(2)}) collective-permute-start(f32[80,256]{1,0:T(8,128)S(1)} %get-tuple-element.43.refs_0_), channel_id=1, source_target_pairs={{0,128},{8,136},{16,144},{24,152},{32,160},{40,168},{48,176},{56,1... | collective-permute-start | bytes 245768 | tf_op jit(solution)/shard_map/ppermute | solution.py:607
  38.0 2.9 %collective-permute-start.7 = (f32[80,256]{1,0:T(8,128)S(1)}, f32[80,256]{1,0:T(8,128)S(1)}, u32[]{:S(2)}, u32[]{:S(2)}) collective-permute-start(f32[80,256]{1,0:T(8,128)S(1)} %get-tuple-element.43.refs_0_), channel_id=1, source_target_pairs={{0,192},{8,200},{16,208},{24,216},{32,224},{40,232},{48,240},{56,2... | collective-permute-start | bytes 245768 | tf_op jit(solution)/shard_map/ppermute | solution.py:607
  40.9 0.0 collective-permute-start.5
  40.9 3.9 %fuse.1 = (f32[8,88,640]{2,1,0:T(8,128)S(1)}, f32[8,168,640]{2,1,0:T(8,128)S(1)}, f32[64,320]{1,0:T(8,128)S(1)}, bf16[320,256]{1,0:T(8,128)(2,1)S(1)}, bf16[320,256]{1,0:T(8,128)(2,1)S(1)}) custom-call(bf16[8,8,80,256]{3,2,1,0:T(8,128)(2,1)S(1)} %get-tuple-element.45.z_both, bf16[8,8,80,512]{3,2,1,0:T(8,128)(2,1)S(1)} %get-tuple-element.46.v_both, ...), custom_call_target="tpu_custom_call" | custom-call | flops 5000000000 | bytes 12000000 | tf_op jit(solution)/shard_map/fuse/pallas_call | solution.py:727
  44.7 2.2 %collective-permute-done.5.refs_1_ = f32[80,128]{1,0:T(8,128)S(1)} collective-permute-done((f32[80,128]{1,0:T(8,128)S(1)}, f32[80,128]{1,0:T(8,128)S(1)}, u32[]{:S(2)}, u32[]{:S(2)}) %collective-permute-start.5) | collective-permute-done | bytes 40992 | tf_op jit(solution)/shard_map/ppermute | solution.py:607
  47.0 0.0 collective-permute-done.6.refs_2_
  47.0 0.0 collective-permute-done.7.refs_3_
  47.0 1.8 %solve.1 = f32[64,384]{1,0:T(8,128)S(1)} custom-call(f32[80,256]{1,0:T(8,128)S(1)} %get-tuple-element.43.refs_0_, f32[80,128]{1,0:T(8,128)S(1)} %collective-permute-done.5.refs_1_, f32[80,256]{1,0:T(8,128)S(1)} %collective-permute-done.6.refs_2_, f32[80,256]{1,0:T(8,128)S(1)} %collective-permute-done.7.refs_3_, f32[8,88,640]{2,1,0:T(8,128)S(1)} %get-tuple-element.52.refs_4_, ...), custom_call_target="tpu_custom_call" | custom-call | tf_op jit(solution)/shard_map/solve/pallas_call | solution.py:742
  48.8 8.9 %all_to_all.11 = f32[8,8,384]{2,1,0:T(8,128)S(1)} all-to-all(f32[8,8,384]{2,1,0:T(8,128)S(1)} %bitcast.25), channel_id=1, replica_groups={{0,8,16,24,32,40,48,56},{64,72,80,88,96,104,112,120},{128,136,144,152,1..., dimensions={0} | all-to-all | bytes 196608 | tf_op jit(solution)/shard_map/all_to_all | solution.py:698
  57.7 0.7 %finish.1 = f32[64,320]{1,0:T(8,128)} custom-call(f32[64,384]{1,0:T(8,128)S(1)} %bitcast.31, f32[64,320]{1,0:T(8,128)S(1)} %bitcast.30), custom_call_target="tpu_custom_call" | custom-call | tf_op jit(solution)/shard_map/finish/pallas_call | solution.py:750
  (1 shorter events, 0.0 us)
Async XLA Ops:
  0.6 0.9 %copy-start.1 = (f32[4,2,8,320]{3,2,1,0:T(8,128)S(1)}, f32[4,2,8,320]{3,2,1,0:T(8,128)}, u32[]{:S(2)}) copy-start(f32[4,2,8,320]{3,2,1,0:T(8,128)} %param.11) | copy-start | bytes 245764
  1.6 8.9 %collective-permute-start.3 = (f32[32,320]{1,0:T(8,128)S(1)}, f32[32,320]{1,0:T(8,128)S(1)}, u32[]{:S(2)}, u32[]{:S(2)}) collective-permute-start(f32[32,320]{1,0:T(8,128)S(1)} %get-tuple-element.35), channel_id=1, source_target_pairs={{0,1},{1,2},{2,3},{3,0},{4,5},{5,6},{6,7},{7,4},{8,9},{9,10},{10,1... | collective-permute-start | bytes 122888 | tf_op jit(solution)/shard_map/halo/ppermute | solution.py:607
  3.2 7.3 %collective-permute-start.4 = (f32[32,320]{1,0:T(8,128)S(1)}, f32[32,320]{1,0:T(8,128)S(1)}, u32[]{:S(2)}, u32[]{:S(2)}) collective-permute-start(f32[32,320]{1,0:T(8,128)S(1)} %get-tuple-element.36), channel_id=1, source_target_pairs={{0,3},{1,0},{2,1},{3,2},{4,7},{5,4},{6,5},{7,6},{8,11},{9,8},{10,9... | collective-permute-start | bytes 122888 | tf_op jit(solution)/shard_map/halo/ppermute | solution.py:607
  4.9 5.6 %collective-permute-start.2 = (f32[16,320]{1,0:T(8,128)S(1)}, f32[16,320]{1,0:T(8,128)S(1)}, u32[]{:S(2)}, u32[]{:S(2)}) collective-permute-start(f32[16,320]{1,0:T(8,128)S(1)} %get-tuple-element.34), channel_id=1, source_target_pairs={{0,4},{4,0},{1,5},{5,1},{2,6},{6,2},{3,7},{7,3},{8,12},{12,8},{9,1... | collective-permute-start | bytes 61448 | tf_op jit(solution)/shard_map/halo/ppermute | solution.py:607
  4.9 6.5 %collective-permute-start = (f32[8,320]{1,0:T(8,128)S(1)}, f32[8,320]{1,0:T(8,128)S(1)}, u32[]{:S(2)}, u32[]{:S(2)}) collective-permute-start(f32[8,320]{1,0:T(8,128)S(1)} %get-tuple-element.30), channel_id=1, source_target_pairs={{0,8},{8,16},{16,24},{24,32},{32,40},{40,48},{48,56},{56,64},{64,7... | collective-permute-start | bytes 30728 | tf_op jit(solution)/shard_map/halo/ppermute | solution.py:607
  6.4 5.0 %collective-permute-start.1 = (f32[8,320]{1,0:T(8,128)S(1)}, f32[8,320]{1,0:T(8,128)S(1)}, u32[]{:S(2)}, u32[]{:S(2)}) collective-permute-start(f32[8,320]{1,0:T(8,128)S(1)} %get-tuple-element.31), channel_id=1, source_target_pairs={{0,248},{8,0},{16,8},{24,16},{32,24},{40,32},{48,40},{56,48},{64,5... | collective-permute-start | bytes 30728 | tf_op jit(solution)/shard_map/halo/ppermute | solution.py:607
  7.1 3.4 %copy-start = (bf16[3136,320]{1,0:T(8,128)(2,1)S(1)}, bf16[3136,320]{1,0:T(8,128)(2,1)}, u32[]{:S(2)}) copy-start(bf16[3136,320]{1,0:T(8,128)(2,1)} %constant.5.clone.fixed_in.fixed.refs_9_) | copy-start | bytes 6021124
  10.4 1.0 %copy-start.2 = (f32[4,2,8,320]{3,2,1,0:T(8,128)S(1)}, f32[4,2,8,320]{3,2,1,0:T(8,128)}, u32[]{:S(2)}) copy-start(f32[4,2,8,320]{3,2,1,0:T(8,128)} %param.11) | copy-start | bytes 245764
  10.5 0.9 %copy-start.3 = (f32[4,2,8,320]{3,2,1,0:T(8,128)S(1)}, f32[4,2,8,320]{3,2,1,0:T(8,128)}, u32[]{:S(2)}) copy-start(f32[4,2,8,320]{3,2,1,0:T(8,128)} %param.12) | copy-start | bytes 245764
  10.5 1.0 %copy-start.4 = (f32[4,2,8,320]{3,2,1,0:T(8,128)S(1)}, f32[4,2,8,320]{3,2,1,0:T(8,128)}, u32[]{:S(2)}) copy-start(f32[4,2,8,320]{3,2,1,0:T(8,128)} %param.13) | copy-start | bytes 245764
  33.4 13.6 %collective-permute-start.6 = (f32[80,256]{1,0:T(8,128)S(1)}, f32[80,256]{1,0:T(8,128)S(1)}, u32[]{:S(2)}, u32[]{:S(2)}) collective-permute-start(f32[80,256]{1,0:T(8,128)S(1)} %get-tuple-element.43.refs_0_), channel_id=1, source_target_pairs={{0,128},{8,136},{16,144},{24,152},{32,160},{40,168},{48,176},{56,1... | collective-permute-start | bytes 245768 | tf_op jit(solution)/shard_map/ppermute | solution.py:607
  38.0 9.0 %collective-permute-start.7 = (f32[80,256]{1,0:T(8,128)S(1)}, f32[80,256]{1,0:T(8,128)S(1)}, u32[]{:S(2)}, u32[]{:S(2)}) collective-permute-start(f32[80,256]{1,0:T(8,128)S(1)} %get-tuple-element.43.refs_0_), channel_id=1, source_target_pairs={{0,192},{8,200},{16,208},{24,216},{32,224},{40,232},{48,240},{56,2... | collective-permute-start | bytes 245768 | tf_op jit(solution)/shard_map/ppermute | solution.py:607
  40.9 6.1 %collective-permute-start.5 = (f32[80,128]{1,0:T(8,128)S(1)}, f32[80,128]{1,0:T(8,128)S(1)}, u32[]{:S(2)}, u32[]{:S(2)}) collective-permute-start(f32[80,128]{1,0:T(8,128)S(1)} %get-tuple-element.44), channel_id=1, source_target_pairs={{0,64},{8,72},{16,80},{24,88},{32,96},{40,104},{48,112},{56,120},{... | collective-permute-start | bytes 122888 | tf_op jit(solution)/shard_map/ppermute | solution.py:607

commit v8 on v7

--- a/solution.py
+++ b/solution.py
@@ -191,6 +191,11 @@
         last_out[line : line + 1] = flow[8 * line + 7 : 8 * line + 8]
 
 
+def chosen_of(matrix, values):
+    both = dot_nt(matrix, jnp.concatenate(split(values), axis=0))
+    return both + roll(both, 64)
+
+
 def prepare_kernel(
     inverse,
     early_in,
@@ -251,9 +256,8 @@
     for copy in copies[5:8]:
         copy.wait()
 
-    padded = jnp.concatenate([flow[...], jnp.zeros((64, 320), F32)], axis=0)
-    own = sum(dot_nt(fixed[SELECT], part) for part in split(padded))
-    own_out[...] = own[320:]
+    own = chosen_of(fixed[SELECT], flow[...])
+    own_out[...] = jnp.where(lanes((800, 128)) < 64, own[320:], 0.0)
     by_variable = slabs_of(own[0:320], 64)
     for d in range(3):
         mixed = mix(lambda w, v: tables[d * 25 + w * 5 + v : d * 25 + w * 5 + v + 1, :], by_variable)
@@ -299,26 +303,57 @@
     return [x[v * size : (v + 1) * size] for v in range(5)]
 
 
-def outside(fixed, chosen, values):
-    return sum(dot_nt(fixed[chosen], part) for part in split(values))
-
-
-def faces_kernel(plane, gy_low, gy_high, tables, own_in, volume_in, fixed, operator_out, extended):
+def span_kernel(below, above, tables, own_in, volume_in, fixed, operator_out, extended):
+    position = rows((8, 320))
+    for line in range(LINES):
+        extended[8 * line : 8 * line + 8] = jnp.where(
+            position == 0,
+            below[line : line + 1],
+            jnp.where(position == 7, above[line : line + 1], 0.0),
+        )
+    far_layers = chosen_of(fixed[SELECT_LAYERS], extended[...])
+    lane = lanes((1, 128))
+    table = lambda r: tables[r : r + 1, :]
+    pieces = []
+    top, bottom = own_in[640:720], own_in[720:800]
+    outer_top, outer_bottom = far_layers[0:80], far_layers[80:160]
+    lower_jump = jnp.where(lane % 8 == 0, outer_top, roll(top, 1)) - bottom
+    upper_jump = jnp.where(lane % 8 == 7, outer_bottom, roll(bottom, -1)) - top
+    pieces += mix(lambda w, v: table(SPAN + (w * 5 + v) * 2), slabs_of(lower_jump, 16))
+    pieces += mix(lambda w, v: table(SPAN + (w * 5 + v) * 2 + 1), slabs_of(upper_jump, 16))
+    operator = dot(fixed[PLACE_A], pair_lanes(volume_in[...]))
+    pieces = pair_lanes(jnp.concatenate(pieces, axis=0))
+    operator_out[...] = operator + dot(fixed[PLACE_C, 0:160], pieces)
+
+
+def sweep_kernel(
+    flow,
+    plane,
+    gy_low,
+    gy_high,
+    source,
+    pseudo,
+    tables,
+    own_in,
+    operator_in,
+    fixed,
+    residual_out,
+    sent_out,
+    extended,
+):
     gx_at, gy_at = lax.axis_index("gx"), lax.axis_index("gy")
     first_lo = (gx_at > 0).astype(F32)
     second_lo = (gy_at > 0).astype(F32)
     second_hi = (gy_at < lax.axis_size("gy") - 1).astype(F32)
-    nothing = jnp.zeros((64, 320), F32)
-    extended[0:64] = nothing
+    extended[0:64] = jnp.zeros((64, 320), F32)
     extended[64:80] = plane[...] * (1.0 - first_lo)
-    extended[80:112] = nothing[:32]
+    extended[80:112] = jnp.zeros((32, 320), F32)
     extended[112:128] = plane[...] * first_lo
     for i in range(4):
         extended[128 + 16 * i : 136 + 16 * i] = gy_low[8 * i : 8 * i + 8] * second_lo
         extended[136 + 16 * i : 144 + 16 * i] = gy_high[8 * i : 8 * i + 8] * second_hi
-    extended[192:256] = nothing
-    near_a = own_in[0:320] + outside(fixed, SELECT_A, extended[0:128])
-    near_b, far_b = own_in[320:640], outside(fixed, SELECT_B, extended[128:256])
+    near_a = sum(dot_nt(fixed[SELECT_A], part) for part in split(extended[0:128])) + own_in[0:320]
+    near_b, far_b = own_in[320:640], chosen_of(fixed[SELECT_B], extended[128:192])
     lane = lanes((1, 128))
     table = lambda r: tables[r : r + 1, :]
     pieces = []
@@ -350,33 +385,8 @@
         jump = LIFT * (neighbour - own)
         pieces += mix(lambda w, v: table(SIDE + (w * 5 + v) * 4 + f), slabs_of(jump, 16))
 
-    operator = dot(fixed[PLACE_A], pair_lanes(volume_in[...]))
-    operator_out[...] = operator + dot(fixed[PLACE_B], pair_lanes(jnp.concatenate(pieces, axis=0)))
-
-
-def sweep_kernel(
-    flow, below, above, source, pseudo, tables, own_in, operator_in, fixed, residual_out, sent_out, extended
-):
-    position = rows((8, 320))
-    for line in range(LINES):
-        extended[8 * line : 8 * line + 8] = jnp.where(
-            position == 0,
-            below[line : line + 1],
-            jnp.where(position == 7, above[line : line + 1], 0.0),
-        )
-    extended[64:128] = jnp.zeros((64, 320), F32)
-    far_layers = outside(fixed, SELECT_LAYERS, extended[...])
-    lane = lanes((1, 128))
-    table = lambda r: tables[r : r + 1, :]
-    pieces = []
-    top, bottom = own_in[640:720], own_in[720:800]
-    outer_top, outer_bottom = far_layers[0:80], far_layers[80:160]
-    lower_jump = jnp.where(lane % 8 == 0, outer_top, roll(top, 1)) - bottom
-    upper_jump = jnp.where(lane % 8 == 7, outer_bottom, roll(bottom, -1)) - top
-    pieces += mix(lambda w, v: table(SPAN + (w * 5 + v) * 2), slabs_of(lower_jump, 16))
-    pieces += mix(lambda w, v: table(SPAN + (w * 5 + v) * 2 + 1), slabs_of(upper_jump, 16))
     pieces = pair_lanes(jnp.concatenate(pieces, axis=0))
-    operator = operator_in[...] + dot(fixed[PLACE_C, 0:160], pieces)
+    operator = operator_in[...] + dot(fixed[PLACE_B], pieces)
     operator_high, operator_low = split(operator)
     twice = fixed[TWICE, 0:128]
     operator_rows = dot_nt(twice, operator_high) + dot_nt(twice, operator_low)
@@ -398,7 +408,8 @@
     z_both,
     v_both,
     t_out,
-    w_out,
+    crossed_out,
+    lefts_out,
     whole_out,
     short_out,
     turned_out,
@@ -424,11 +435,21 @@
             wide[e, k] = jnp.broadcast_to(jacobians[:, at : at + 1], (50, 128))
         moved = roll(traces, 80 - 8 * e)
         started[e] = jnp.where((trace_lane >= 80) & (trace_lane < 88), moved, 0.0)
-        t_state[e] = jnp.where(small_lane == small_row, 1.0, 0.0)
-        w_state[e] = jnp.where(lanes((80, 256)) == rows((80, 256)) + 88, 1.0, 0.0)
 
     def coupled(e, k, side, state):
         out = mix(lambda w, v: wide[e, k, pl.ds((w * 5 + v) * 2 + side, 1)], slabs_of(state, 16))
+        return jnp.concatenate(out, axis=0)
+
+    diagonal = (small_lane[:16] % 16 == small_row[:16]) & (small_lane[:16] < 80)
+
+    def coupled_identity(e, k, side):
+        out = []
+        for w in range(5):
+            line = [wide[e, k, pl.ds((w * 5 + v) * 2 + side, 1)] for v in range(5)]
+            row = line[4]
+            for v in range(3, -1, -1):
+                row = jnp.where(small_lane[:1] < 16 * v + 16, line[v], row)
+            out.append(jnp.where(diagonal, row, 0.0))
         return jnp.concatenate(out, axis=0)
 
     for k in range(SEG):
@@ -436,7 +457,8 @@
         for pair in range(0, SEG, 2):
             cats = []
             for e in (pair, pair + 1):
-                z_hi, z_lo = split(coupled(e, k, 0, t_state[e]))
+                z = coupled(e, k, 0, t_state[e]) if k else coupled_identity(e, k, 0)
+                z_hi, z_lo = split(z)
                 z_both[e, k, :, 0:128] = z_hi
                 z_both[e, k, :, 128:256] = z_lo
                 cats.append(jnp.concatenate([z_hi, z_lo, z_hi], axis=0))
@@ -452,7 +474,15 @@
     for step in range(SEG):
         k = SEG - 1 - step
         for e in range(SEG):
-            z = [coupled(e, k, 1, w_state[e, :, half]) for half in (slice(0, 128), slice(128, 256))]
+            if step:
+                halves = (w_state[e, :, 0:128], w_state[e, :, 128:256])
+                z = [coupled(e, k, 1, half) for half in halves]
+            else:
+                z = coupled_identity(e, k, 1)
+                z = [
+                    jnp.where(small_lane >= 88, roll(z, 88), 0.0),
+                    jnp.where(small_lane < 40, roll(z, 88), 0.0),
+                ]
             z_hi, z_lo = split(jnp.concatenate(z, axis=1))
             v_both[e, k, :, 0:256] = z_hi
             v_both[e, k, :, 256:512] = z_lo
@@ -464,40 +494,56 @@
         y = dot(left_cat(t_state[step]), states[-1])
         state = jnp.concatenate([y, ones[80:]], axis=0)
 
-    parts = [unpack(w_state[e, :, 0:128], w_state[e, :, 128:256])[1:] for e in range(SEG)]
-    crossed = [dot(left_cat(parts[e][0]), states[e]) for e in range(SEG)]
-    lefts = [left_cat(parts[e][1]) for e in range(SEG)]
+    maps = []
+    for e in range(SEG):
+        left, right = w_state[e, :, 0:128], w_state[e, :, 128:256]
+        _, cross, back = unpack(left, right)
+        crossed = dot(left_cat(cross), states[e])
+        lefts_out[e] = left_cat(back)
+        crossed_out[e] = crossed
+        maps.append((crossed + jnp.where(small_lane < 88, 0.0, left), right))
+    zero = jnp.zeros((48, 128), F32)
+    lefts = [lefts_out[e] for e in range(SEG)]
+    while len(maps) > 1:
+        joined = []
+        for at in range(0, len(maps), 2):
+            after = [right_cat(jnp.concatenate([x, zero], axis=0)) for x in maps[at + 1]]
+            y = dot(lefts[at], jnp.concatenate(after, axis=1))
+            kept = jnp.where(small_lane < 88, maps[at][0], 0.0)
+            joined.append((y[:, :128] + kept, y[:, 128:]))
+        maps = joined
+        lefts = [left_cat(unpack(*both)[2]) for both in maps]
+    whole_out[:, 0:128] = maps[0][0]
+    whole_out[:, 128:256] = maps[0][1] + roll(state[:80], 40)
+    groups = lax.axis_size("span") // SEG
+    last = lax.axis_index("span") // SEG == groups - 1
+    short_out[...] = jnp.where(last, maps[0][0], state[:80])
+
+
+def against_pair(x):
+    high, low = split(x)
+    upper = jnp.concatenate([high, high], axis=1)
+    return jnp.concatenate([upper, jnp.concatenate([low, jnp.zeros_like(low)], axis=1)], axis=0)
+
+
+def fuse_kernel(
+    z_both, v_both, t_in, crossed, lefts, turned, high, low, fixed, r_out, q_out, base_out, gs_high, gs_low
+):
+    tall_lane, tall_row = lanes((128, 128)), rows((128, 128))
     zero = jnp.zeros((48, 128), F32)
     w0 = jnp.where(tall_lane == tall_row + 88, 1.0, 0.0)
     w1 = jnp.where((tall_lane == tall_row - 40) & (tall_row < 80), 1.0, 0.0)
     for e in range(SEG - 1, -1, -1):
-        w_out[e, :, 0:128] = w0[:80]
-        w_out[e, :, 128:256] = w1[:80]
-        y = dot(lefts[e], jnp.concatenate([right_cat(w0), right_cat(w1)], axis=1))
-        w0 = jnp.concatenate([y[:, :128] + crossed[e], zero], axis=0)
-        w1 = jnp.concatenate([y[:, 128:], zero], axis=0)
-    whole_out[:, 0:128] = w0[:80]
-    whole_out[:, 128:256] = w1[:80] + roll(state[:80], 40)
-    groups = lax.axis_size("span") // SEG
-    last = lax.axis_index("span") // SEG == groups - 1
-    short_out[...] = jnp.where(last, w0[:80], state[:80])
-
-
-def against_pair(x):
-    high, low = split(x)
-    upper = jnp.concatenate([high, high], axis=1)
-    return jnp.concatenate([upper, jnp.concatenate([low, jnp.zeros_like(low)], axis=1)], axis=0)
-
-
-def fuse_kernel(
-    z_both, v_both, t_in, w_in, turned, high, low, fixed, r_out, q_out, base_out, gs_high, gs_low
-):
-    for e in range(SEG):
+        behind = jnp.concatenate([w0[:80], w1[:80]], axis=1)
+        if e > 0:
+            y = dot(lefts[e], jnp.concatenate([right_cat(w0), right_cat(w1)], axis=1))
+            w0 = jnp.concatenate([y[:, :128] + crossed[e], zero], axis=0)
+            w1 = jnp.concatenate([y[:, 128:], zero], axis=0)
         state = t_in[e]
         r = dot_nt(against_pair(jnp.transpose(state)[:96]), z_both[e].reshape(640, 256))
         r_out[e] = r[:88] + r[96:184]
         first = jnp.concatenate([state[:88], jnp.zeros((88, 128), F32)], axis=1)
-        both = jnp.concatenate([first, w_in[e], jnp.zeros((88, 256), F32)], axis=0)
+        both = jnp.concatenate([first, behind, jnp.zeros((88, 256), F32)], axis=0)
         q = dot_nt(against_pair(jnp.transpose(both)[:176]), v_both[e].reshape(640, 512))
         q_out[e] = q[:168] + q[176:344]
     load = pair_lanes(turned[...])
@@ -661,28 +707,29 @@
     )
 
     operator = call(
-        faces_kernel,
+        span_kernel,
         shape(320, 128),
-        [VM] * 7,
-        scratch=[pltpu.VMEM((256, 320), F32)],
+        [VM] * 6,
+        scratch=[pltpu.VMEM((64, 320), F32)],
         limit=16,
         flops=1_000_000_000,
         moved=3_000_000,
-        name="faces",
-    )(plane, gy_low, gy_high, tables, own, volume, fixed)
+        name="span",
+    )(below, above, tables, own, volume, fixed)
     residual, sent = call(
         sweep_kernel,
         (shape(64, 320), shape(64, 384)),
-        [VM] * 9,
-        scratch=[pltpu.VMEM((128, 320), F32)],
+        [VM] * 10,
+        scratch=[pltpu.VMEM((192, 320), F32)],
         limit=16,
         flops=1_000_000_000,
         moved=3_000_000,
         name="sweep",
     )(
         flow,
-        below,
-        above,
+        plane,
+        gy_low,
+        gy_high,
         source_term.reshape(64, 320),
         pseudo_time.reshape(64, 320),
         tables,
@@ -698,13 +745,14 @@
         value = lax.all_to_all(value, "span", 0, 0, axis_index_groups=within, tiled=True)
         return value.reshape(64, 384)
 
-    z_both, v_both, t_maps, w_maps, whole, short, turned = call(
+    z_both, v_both, t_maps, crossed, lefts, whole, short, turned = call(
         maps_kernel,
         (
             shape(SEG, SEG, 80, 256, dtype=BF16),
             shape(SEG, SEG, 80, 512, dtype=BF16),
             shape(SEG, 128, 128),
-            shape(SEG, 80, 256),
+            shape(SEG, 80, 128),
+            shape(SEG, 80, 384, dtype=BF16),
             shape(80, 256),
             shape(80, 128),
             shape(320, 128),
@@ -733,12 +781,12 @@
             shape(320, 256, dtype=BF16),
             shape(320, 256, dtype=BF16),
         ),
-        [VM] * 8,
+        [VM] * 9,
         limit=24,
         flops=5_000_000_000,
         moved=12_000_000,
         name="fuse",
-    )(z_both, v_both, t_maps, w_maps, turned, high, low, fixed)
+    )(z_both, v_both, t_maps, crossed, lefts, turned, high, low, fixed)
     answers = call(
         solve_kernel,
         shape(64, 384),

time: 58.6 us -> 57.9 us (0.988)
  waiting for transfers between devices: 2.23 us -> 1.05 us
    ppermute x8, waiting for transfers between devices: 2.23 us -> 1.05 us  [ring(): lax.ppermute(value, axis, [(i, (i + step) % count) for i in range(count)])]
where the time goes in v8:
time: 57.9 us; the launch traced here: 57.2 us
  blocking collectives  22.4 us (39%)
  Pallas kernels  18.7 us (32%)
  starting transfers between devices  13.1 us (23%)
  local copies, waits for them, and re-layouts  1.18 us (2%)
  waiting for transfers between devices  1.05 us (2%)
  between operations  0.77 us (1%)
    all_to_all x2, blocking collectives, exchange(): lax.all_to_all(value, 'span', 0, 0, axis_index_groups=within, tiled=True)  22.4 us
    ppermute x8, starting transfers between devices, ring(): lax.ppermute(value, axis, [(i, (i + step) % count) for i in range(count)])  13.1 us
    pallas_call x1, Pallas kernels, on_device(): call(maps_kernel, (shape(SEG, SEG, 80, 256, dtype=BF16), shape(SEG, SEG,...  6.66 us
    pallas_call x1, Pallas kernels, on_device(): call(fuse_kernel, (shape(SEG, 88, 640), shape(SEG, 168, 640), shape(64, 3...  4.2 us
    pallas_call x1, Pallas kernels, on_device(): call(prepare_kernel, (shape(320, 320, dtype=BF16), shape(320, 320, dtype=...  3.12 us
    pallas_call x1, Pallas kernels, on_device(): call(solve_kernel, shape(64, 384), [VM] * (groups + 6), scratch=[pltpu.VM...  1.8 us
    pallas_call x1, Pallas kernels, on_device(): call(sweep_kernel, (shape(64, 320), shape(64, 384)), [VM] * 10, scratch=[...  1.6 us
    unnamed x10, local copies, waits for them, and re-layouts  1.18 us
  transfers between devices with their start and end apart: 8, of which 1 were waited for; matrix products, arithmetic and copies ran while one was open for 0% of the time, Pallas kernels for 14%

profile of v8, /device:TPU:2, one launch (start us, length us, event | category | flops | bytes accessed | tf_op | source)
XLA Modules:
  0.0 57.2 jit_solution(10613832968267283652)
XLA Ops:
  0.6 0.0 copy-start.1
  0.6 0.9 %copy-done.1 = f32[4,2,8,320]{3,2,1,0:T(8,128)S(1)} copy-done((f32[4,2,8,320]{3,2,1,0:T(8,128)S(1)}, f32[4,2,8,320]{3,2,1,0:T(8,128)}, u32[]{:S(2)}) %copy-start.1) | copy-done | bytes 81944
  1.6 1.6 %collective-permute-start.3 = (f32[8,320]{1,0:T(8,128)S(1)}, f32[8,320]{1,0:T(8,128)S(1)}, u32[]{:S(2)}, u32[]{:S(2)}) collective-permute-start(f32[8,320]{1,0:T(8,128)S(1)} %get-tuple-element.36), channel_id=1, source_target_pairs={{0,8},{8,16},{16,24},{24,32},{32,40},{40,48},{48,56},{56,64},{64,7... | collective-permute-start | bytes 30728 | tf_op jit(solution)/shard_map/halo/ppermute | solution.py:653
  3.1 0.9 %collective-permute-start.4 = (f32[8,320]{1,0:T(8,128)S(1)}, f32[8,320]{1,0:T(8,128)S(1)}, u32[]{:S(2)}, u32[]{:S(2)}) collective-permute-start(f32[8,320]{1,0:T(8,128)S(1)} %get-tuple-element.37), channel_id=1, source_target_pairs={{0,248},{8,0},{16,8},{24,16},{32,24},{40,32},{48,40},{56,48},{64,5... | collective-permute-start | bytes 30728 | tf_op jit(solution)/shard_map/halo/ppermute | solution.py:653
  4.0 1.2 %collective-permute-start.1 = (f32[32,320]{1,0:T(8,128)S(1)}, f32[32,320]{1,0:T(8,128)S(1)}, u32[]{:S(2)}, u32[]{:S(2)}) collective-permute-start(f32[32,320]{1,0:T(8,128)S(1)} %get-tuple-element.32), channel_id=1, source_target_pairs={{0,1},{1,2},{2,3},{3,0},{4,5},{5,6},{6,7},{7,4},{8,9},{9,10},{10,1... | collective-permute-start | bytes 122888 | tf_op jit(solution)/shard_map/halo/ppermute | solution.py:653
  5.2 2.0 %collective-permute-start.2 = (f32[32,320]{1,0:T(8,128)S(1)}, f32[32,320]{1,0:T(8,128)S(1)}, u32[]{:S(2)}, u32[]{:S(2)}) collective-permute-start(f32[32,320]{1,0:T(8,128)S(1)} %get-tuple-element.33), channel_id=1, source_target_pairs={{0,3},{1,0},{2,1},{3,2},{4,7},{5,4},{6,5},{7,6},{8,11},{9,8},{10,9... | collective-permute-start | bytes 122888 | tf_op jit(solution)/shard_map/halo/ppermute | solution.py:653
  7.2 0.0 collective-permute-start
  7.2 0.0 copy-start
  7.2 3.1 %prepare.1 = (bf16[320,320]{1,0:T(8,128)(2,1)S(1)}, bf16[320,320]{1,0:T(8,128)(2,1)S(1)}, bf16[160,320]{1,0:T(8,128)(2,1)S(1)}, bf16[160,320]{1,0:T(8,128)(2,1)S...) custom-call(f32[8,320,320]{2,1,0:T(8,128)} %bitcast.36, ...), custom_call_target="tpu_custom_call" | custom-call | flops 4000000000 | bytes 8000000 | tf_op jit(solution)/shard_map/prepare/pallas_call | solution.py:676
  10.4 0.0 copy-start.2
  10.4 0.0 copy-start.3
  10.4 0.0 copy-start.4
  10.4 0.0 collective-permute-done.3.below
  10.4 0.0 collective-permute-done.4.above
  10.4 0.0 copy-done
  10.4 0.6 %span.1.operator_in = f32[320,128]{1,0:T(8,128)S(1)} custom-call(f32[8,320]{1,0:T(8,128)S(1)} %collective-permute-done.3.below, f32[8,320]{1,0:T(8,128)S(1)} %collective-permute-done.4.above, f32[248,128]{1,0:T(8,128)S(1)} %get-tuple-element.34.tables, f32[800,128]{1,0:T(8,128)S(1)} %get-tuple-element.35.own_in, f32[320,128]{1,0:T(8,128)S(1)} %get-tuple-element.38.volume_in, ...), custom_call_target="tpu_custom_call" | custom-call | flops 1000000000 | bytes 3000000 | tf_op jit(solution)/shard_map/span/pallas_call | solution.py:709
  11.0 0.0 collective-permute-done.plane
  11.1 0.0 collective-permute-done.1.gy_low
  11.1 0.0 collective-permute-done.2.gy_high
  11.1 0.2 copy-done.2
  11.3 0.0 copy-done.3
  11.3 0.0 copy-done.4
  11.4 1.6 %sweep.1 = (f32[64,320]{1,0:T(8,128)}, f32[64,384]{1,0:T(8,128)S(1)}) custom-call(f32[64,320]{1,0:T(8,128)S(1)} %bitcast.29, f32[16,320]{1,0:T(8,128)S(1)} %collective-permute-done.plane, f32[32,320]{1,0:T(8,128)S(1)} %collective-permute-done.1.gy_low, f32[32,320]{1,0:T(8,128)S(1)} %collective-permute-done.2.gy_high, f32[64,320]{1,0:T(8,128)S(1)} %bitcast.33, ...), custom_call_target="tpu_custom_call" | custom-call | flops 1000000000 | bytes 3000000 | tf_op jit(solution)/shard_map/sweep/pallas_call | solution.py:719
  13.0 13.7 %all_to_all.10 = f32[8,8,384]{2,1,0:T(8,128)S(1)} all-to-all(f32[8,8,384]{2,1,0:T(8,128)S(1)} %bitcast.32), channel_id=1, replica_groups={{0,8,16,24,32,40,48,56},{64,72,80,88,96,104,112,120},{128,136,144,152,1..., dimensions={0} | all-to-all | bytes 196608 | tf_op jit(solution)/shard_map/all_to_all | solution.py:745
  26.7 6.7 %maps.1 = (bf16[8,8,80,256]{3,2,1,0:T(8,128)(2,1)S(1)}, bf16[8,8,80,512]{3,2,1,0:T(8,128)(2,1)S(1)}, f32[8,128,128]{2,1,0:T(8,128)S(1)}, f32[8,80,128]{2,1,0:T(8...) custom-call(f32[64,384]{1,0:T(8,128)S(1)} %bitcast.26, ...), custom_call_target="tpu_custom_call" | custom-call | tf_op jit(solution)/shard_map/maps/pallas_call | solution.py:748
  33.3 4.5 %collective-permute-start.6 = (f32[80,256]{1,0:T(8,128)S(1)}, f32[80,256]{1,0:T(8,128)S(1)}, u32[]{:S(2)}, u32[]{:S(2)}) collective-permute-start(f32[80,256]{1,0:T(8,128)S(1)} %get-tuple-element.44.refs_0_), channel_id=1, source_target_pairs={{0,128},{8,136},{16,144},{24,152},{32,160},{40,168},{48,176},{56,1... | collective-permute-start | bytes 245768 | tf_op jit(solution)/shard_map/ppermute | solution.py:653
  37.8 0.4 collective-permute-start.7
  38.3 2.5 %collective-permute-start.5 = (f32[80,128]{1,0:T(8,128)S(1)}, f32[80,128]{1,0:T(8,128)S(1)}, u32[]{:S(2)}, u32[]{:S(2)}) collective-permute-start(f32[80,128]{1,0:T(8,128)S(1)} %get-tuple-element.45), channel_id=1, source_target_pairs={{0,64},{8,72},{16,80},{24,88},{32,96},{40,104},{48,112},{56,120},{... | collective-permute-start | bytes 122888 | tf_op jit(solution)/shard_map/ppermute | solution.py:653
  40.8 4.2 %fuse.1 = (f32[8,88,640]{2,1,0:T(8,128)S(1)}, f32[8,168,640]{2,1,0:T(8,128)S(1)}, f32[64,320]{1,0:T(8,128)S(1)}, bf16[320,256]{1,0:T(8,128)(2,1)S(1)}, bf16[320,256]{1,0:T(8,128)(2,1)S(1)}) custom-call(bf16[8,8,80,256]{3,2,1,0:T(8,128)(2,1)S(1)} %get-tuple-element.46.z_both, bf16[8,8,80,512]{3,2,1,0:T(8,128)(2,1)S(1)} %get-tuple-element.47.v_both, ...), custom_call_target="tpu_custom_call" | custom-call | flops 5000000000 | bytes 12000000 | tf_op jit(solution)/shard_map/fuse/pallas_call | solution.py:775
  45.0 0.0 collective-permute-done.5.refs_1_
  45.0 0.0 collective-permute-done.6.refs_2_
  45.0 1.0 %collective-permute-done.7.refs_3_ = f32[80,256]{1,0:T(8,128)S(1)} collective-permute-done((f32[80,256]{1,0:T(8,128)S(1)}, f32[80,256]{1,0:T(8,128)S(1)}, u32[]{:S(2)}, u32[]{:S(2)}) %collective-permute-start.7) | collective-permute-done | bytes 81952 | tf_op jit(solution)/shard_map/ppermute | solution.py:653
  46.0 1.8 %solve.1 = f32[64,384]{1,0:T(8,128)S(1)} custom-call(f32[80,256]{1,0:T(8,128)S(1)} %get-tuple-element.44.refs_0_, f32[80,128]{1,0:T(8,128)S(1)} %collective-permute-done.5.refs_1_, f32[80,256]{1,0:T(8,128)S(1)} %collective-permute-done.6.refs_2_, f32[80,256]{1,0:T(8,128)S(1)} %collective-permute-done.7.refs_3_, f32[8,88,640]{2,1,0:T(8,128)S(1)} %get-tuple-element.54.refs_4_, ...), custom_call_target="tpu_custom_call" | custom-call | tf_op jit(solution)/shard_map/solve/pallas_call | solution.py:790
  47.8 8.7 %all_to_all.11 = f32[8,8,384]{2,1,0:T(8,128)S(1)} all-to-all(f32[8,8,384]{2,1,0:T(8,128)S(1)} %bitcast.25), channel_id=1, replica_groups={{0,8,16,24,32,40,48,56},{64,72,80,88,96,104,112,120},{128,136,144,152,1..., dimensions={0} | all-to-all | bytes 196608 | tf_op jit(solution)/shard_map/all_to_all | solution.py:745
  56.5 0.7 %finish.1 = f32[64,320]{1,0:T(8,128)} custom-call(f32[64,384]{1,0:T(8,128)S(1)} %bitcast.31, f32[64,320]{1,0:T(8,128)S(1)} %bitcast.30), custom_call_target="tpu_custom_call" | custom-call | tf_op jit(solution)/shard_map/finish/pallas_call | solution.py:798
  (1 shorter events, 0.0 us)
Async XLA Ops:
  0.6 0.9 %copy-start.1 = (f32[4,2,8,320]{3,2,1,0:T(8,128)S(1)}, f32[4,2,8,320]{3,2,1,0:T(8,128)}, u32[]{:S(2)}) copy-start(f32[4,2,8,320]{3,2,1,0:T(8,128)} %param.11) | copy-start | bytes 245764
  1.6 8.8 %collective-permute-start.3 = (f32[8,320]{1,0:T(8,128)S(1)}, f32[8,320]{1,0:T(8,128)S(1)}, u32[]{:S(2)}, u32[]{:S(2)}) collective-permute-start(f32[8,320]{1,0:T(8,128)S(1)} %get-tuple-element.36), channel_id=1, source_target_pairs={{0,8},{8,16},{16,24},{24,32},{32,40},{40,48},{48,56},{56,64},{64,7... | collective-permute-start | bytes 30728 | tf_op jit(solution)/shard_map/halo/ppermute | solution.py:653
  3.1 7.3 %collective-permute-start.4 = (f32[8,320]{1,0:T(8,128)S(1)}, f32[8,320]{1,0:T(8,128)S(1)}, u32[]{:S(2)}, u32[]{:S(2)}) collective-permute-start(f32[8,320]{1,0:T(8,128)S(1)} %get-tuple-element.37), channel_id=1, source_target_pairs={{0,248},{8,0},{16,8},{24,16},{32,24},{40,32},{48,40},{56,48},{64,5... | collective-permute-start | bytes 30728 | tf_op jit(solution)/shard_map/halo/ppermute | solution.py:653
  4.0 7.1 %collective-permute-start.1 = (f32[32,320]{1,0:T(8,128)S(1)}, f32[32,320]{1,0:T(8,128)S(1)}, u32[]{:S(2)}, u32[]{:S(2)}) collective-permute-start(f32[32,320]{1,0:T(8,128)S(1)} %get-tuple-element.32), channel_id=1, source_target_pairs={{0,1},{1,2},{2,3},{3,0},{4,5},{5,6},{6,7},{7,4},{8,9},{9,10},{10,1... | collective-permute-start | bytes 122888 | tf_op jit(solution)/shard_map/halo/ppermute | solution.py:653
  5.2 5.8 %collective-permute-start.2 = (f32[32,320]{1,0:T(8,128)S(1)}, f32[32,320]{1,0:T(8,128)S(1)}, u32[]{:S(2)}, u32[]{:S(2)}) collective-permute-start(f32[32,320]{1,0:T(8,128)S(1)} %get-tuple-element.33), channel_id=1, source_target_pairs={{0,3},{1,0},{2,1},{3,2},{4,7},{5,4},{6,5},{7,6},{8,11},{9,8},{10,9... | collective-permute-start | bytes 122888 | tf_op jit(solution)/shard_map/halo/ppermute | solution.py:653
  7.2 3.8 %collective-permute-start = (f32[16,320]{1,0:T(8,128)S(1)}, f32[16,320]{1,0:T(8,128)S(1)}, u32[]{:S(2)}, u32[]{:S(2)}) collective-permute-start(f32[16,320]{1,0:T(8,128)S(1)} %get-tuple-element.31), channel_id=1, source_target_pairs={{0,4},{4,0},{1,5},{5,1},{2,6},{6,2},{3,7},{7,3},{8,12},{12,8},{9,1... | collective-permute-start | bytes 61448 | tf_op jit(solution)/shard_map/halo/ppermute | solution.py:653
  7.2 3.2 %copy-start = (bf16[3136,320]{1,0:T(8,128)(2,1)S(1)}, bf16[3136,320]{1,0:T(8,128)(2,1)}, u32[]{:S(2)}) copy-start(bf16[3136,320]{1,0:T(8,128)(2,1)} %constant.5.clone.fixed_in.fixed.refs_9_) | copy-start | bytes 6021124
  10.4 0.9 %copy-start.2 = (f32[4,2,8,320]{3,2,1,0:T(8,128)S(1)}, f32[4,2,8,320]{3,2,1,0:T(8,128)}, u32[]{:S(2)}) copy-start(f32[4,2,8,320]{3,2,1,0:T(8,128)} %param.11) | copy-start | bytes 245764
  10.4 0.9 %copy-start.3 = (f32[4,2,8,320]{3,2,1,0:T(8,128)S(1)}, f32[4,2,8,320]{3,2,1,0:T(8,128)}, u32[]{:S(2)}) copy-start(f32[4,2,8,320]{3,2,1,0:T(8,128)} %param.12) | copy-start | bytes 245764
  10.4 1.0 %copy-start.4 = (f32[4,2,8,320]{3,2,1,0:T(8,128)S(1)}, f32[4,2,8,320]{3,2,1,0:T(8,128)}, u32[]{:S(2)}) copy-start(f32[4,2,8,320]{3,2,1,0:T(8,128)} %param.13) | copy-start | bytes 245764
  33.3 11.6 %collective-permute-start.6 = (f32[80,256]{1,0:T(8,128)S(1)}, f32[80,256]{1,0:T(8,128)S(1)}, u32[]{:S(2)}, u32[]{:S(2)}) collective-permute-start(f32[80,256]{1,0:T(8,128)S(1)} %get-tuple-element.44.refs_0_), channel_id=1, source_target_pairs={{0,128},{8,136},{16,144},{24,152},{32,160},{40,168},{48,176},{56,1... | collective-permute-start | bytes 245768 | tf_op jit(solution)/shard_map/ppermute | solution.py:653
  37.8 8.2 %collective-permute-start.7 = (f32[80,256]{1,0:T(8,128)S(1)}, f32[80,256]{1,0:T(8,128)S(1)}, u32[]{:S(2)}, u32[]{:S(2)}) collective-permute-start(f32[80,256]{1,0:T(8,128)S(1)} %get-tuple-element.44.refs_0_), channel_id=1, source_target_pairs={{0,192},{8,200},{16,208},{24,216},{32,224},{40,232},{48,240},{56,2... | collective-permute-start | bytes 245768 | tf_op jit(solution)/shard_map/ppermute | solution.py:653
  38.3 6.7 %collective-permute-start.5 = (f32[80,128]{1,0:T(8,128)S(1)}, f32[80,128]{1,0:T(8,128)S(1)}, u32[]{:S(2)}, u32[]{:S(2)}) collective-permute-start(f32[80,128]{1,0:T(8,128)S(1)} %get-tuple-element.45), channel_id=1, source_target_pairs={{0,64},{8,72},{16,80},{24,88},{32,96},{40,104},{48,112},{56,120},{... | collective-permute-start | bytes 122888 | tf_op jit(solution)/shard_map/ppermute | solution.py:653

commit v9 on v8

--- a/solution.py
+++ b/solution.py
@@ -180,7 +180,10 @@
     return jnp.concatenate([high, low, high], axis=0)
 
 
-def pack_kernel(flow, plane_out, up_out, down_out, last_out, first_out):
+def pack_kernel(flow_in, plane_out, up_out, down_out, last_out, first_out, flow, arrived):
+    copy = pltpu.make_async_copy(flow_in, flow, arrived)
+    copy.start()
+    copy.wait()
     at = pl.multiple_of((1 - lax.axis_index("gx")) * 48, 16)
     plane_out[...] = flow[pl.ds(at, 16)]
     for i in range(4):
@@ -656,10 +659,11 @@
     plane, up, down, last, first = call(
         pack_kernel,
         (shape(16, 320), shape(32, 320), shape(32, 320), shape(8, 320), shape(8, 320)),
-        [VM],
+        [HBM],
+        scratch=[pltpu.VMEM((64, 320), F32), pltpu.SemaphoreType.DMA(())],
         limit=4,
         name="pack",
-    )(flow)
+    )(pltpu.with_memory_space_constraint(flow, pltpu.HBM))
     with jax.named_scope("halo"):
         below, above = ring(last, "span", 1), ring(first, "span", -1)
         gy_low, gy_high = ring(up, "gy", 1), ring(down, "gy", -1)

time: 57.9 us -> 57.9 us (level)
  Pallas kernels: 18.7 us -> 19.6 us
  local copies, waits for them, and re-layouts: 1.18 us -> 0.29 us
    pallas_call x1, Pallas kernels: 0.02 us -> 0.92 us  [on_device(): call(pack_kernel, (shape(16, 320), shape(32, 320), shape(32, 320), shape(...]
    unnamed x10 -> x8, local copies, waits for them, and re-layouts: 1.18 us -> 0.29 us
where the time goes in v9:
time: 57.9 us; the launch traced here: 57.2 us
  blocking collectives  22.4 us (39%)
  Pallas kernels  19.6 us (34%)
  starting transfers between devices  13.1 us (23%)
  waiting for transfers between devices  1.04 us (2%)
  between operations  0.76 us (1%)
    all_to_all x2, blocking collectives, exchange(): lax.all_to_all(value, 'span', 0, 0, axis_index_groups=within, tiled=True)  22.4 us
    ppermute x8, starting transfers between devices, ring(): lax.ppermute(value, axis, [(i, (i + step) % count) for i in range(count)])  13.1 us
    pallas_call x1, Pallas kernels, on_device(): call(maps_kernel, (shape(SEG, SEG, 80, 256, dtype=BF16), shape(SEG, SEG,...  6.66 us
    pallas_call x1, Pallas kernels, on_device(): call(fuse_kernel, (shape(SEG, 88, 640), shape(SEG, 168, 640), shape(64, 3...  4.2 us
    pallas_call x1, Pallas kernels, on_device(): call(prepare_kernel, (shape(320, 320, dtype=BF16), shape(320, 320, dtype=...  3.12 us
    pallas_call x1, Pallas kernels, on_device(): call(solve_kernel, shape(64, 384), [VM] * (groups + 6), scratch=[pltpu.VM...  1.8 us
    pallas_call x1, Pallas kernels, on_device(): call(sweep_kernel, (shape(64, 320), shape(64, 384)), [VM] * 10, scratch=[...  1.6 us
  transfers between devices with their start and end apart: 8, of which 1 were waited for; matrix products, arithmetic and copies ran while one was open for 0% of the time, Pallas kernels for 14%

profile of v9, /device:TPU:2, one launch (start us, length us, event | category | flops | bytes accessed | tf_op | source)
XLA Modules:
  0.0 57.2 jit_solution(11450609798699599225)
XLA Ops:
  0.6 0.9 %pack.1 = (f32[16,320]{1,0:T(8,128)S(1)}, f32[32,320]{1,0:T(8,128)S(1)}, f32[32,320]{1,0:T(8,128)S(1)}, f32[8,320]{1,0:T(8,128)S(1)}, f32[8,320]{1,0:T(8,128)S(1)}) custom-call(f32[64,320]{1,0:T(8,128)} %bitcast.27), custom_call_target="tpu_custom_call" | custom-call | tf_op jit(solution)/shard_map/pack/pallas_call | solution.py:659
  1.6 1.6 %collective-permute-start.3 = (f32[8,320]{1,0:T(8,128)S(1)}, f32[8,320]{1,0:T(8,128)S(1)}, u32[]{:S(2)}, u32[]{:S(2)}) collective-permute-start(f32[8,320]{1,0:T(8,128)S(1)} %get-tuple-element.36), channel_id=1, source_target_pairs={{0,8},{8,16},{16,24},{24,32},{32,40},{40,48},{48,56},{56,64},{64,7... | collective-permute-start | bytes 30728 | tf_op jit(solution)/shard_map/halo/ppermute | solution.py:656
  3.1 0.9 %collective-permute-start.4 = (f32[8,320]{1,0:T(8,128)S(1)}, f32[8,320]{1,0:T(8,128)S(1)}, u32[]{:S(2)}, u32[]{:S(2)}) collective-permute-start(f32[8,320]{1,0:T(8,128)S(1)} %get-tuple-element.37), channel_id=1, source_target_pairs={{0,248},{8,0},{16,8},{24,16},{32,24},{40,32},{48,40},{56,48},{64,5... | collective-permute-start | bytes 30728 | tf_op jit(solution)/shard_map/halo/ppermute | solution.py:656
  4.0 1.2 %collective-permute-start.1 = (f32[32,320]{1,0:T(8,128)S(1)}, f32[32,320]{1,0:T(8,128)S(1)}, u32[]{:S(2)}, u32[]{:S(2)}) collective-permute-start(f32[32,320]{1,0:T(8,128)S(1)} %get-tuple-element.32), channel_id=1, source_target_pairs={{0,1},{1,2},{2,3},{3,0},{4,5},{5,6},{6,7},{7,4},{8,9},{9,10},{10,1... | collective-permute-start | bytes 122888 | tf_op jit(solution)/shard_map/halo/ppermute | solution.py:656
  5.2 2.0 %collective-permute-start.2 = (f32[32,320]{1,0:T(8,128)S(1)}, f32[32,320]{1,0:T(8,128)S(1)}, u32[]{:S(2)}, u32[]{:S(2)}) collective-permute-start(f32[32,320]{1,0:T(8,128)S(1)} %get-tuple-element.33), channel_id=1, source_target_pairs={{0,3},{1,0},{2,1},{3,2},{4,7},{5,4},{6,5},{7,6},{8,11},{9,8},{10,9... | collective-permute-start | bytes 122888 | tf_op jit(solution)/shard_map/halo/ppermute | solution.py:656
  7.2 0.0 collective-permute-start
  7.2 0.0 copy-start
  7.2 3.1 %prepare.1 = (bf16[320,320]{1,0:T(8,128)(2,1)S(1)}, bf16[320,320]{1,0:T(8,128)(2,1)S(1)}, bf16[160,320]{1,0:T(8,128)(2,1)S(1)}, bf16[160,320]{1,0:T(8,128)(2,1)S...) custom-call(f32[8,320,320]{2,1,0:T(8,128)} %bitcast.36, ...), custom_call_target="tpu_custom_call" | custom-call | flops 4000000000 | bytes 8000000 | tf_op jit(solution)/shard_map/prepare/pallas_call | solution.py:680
  10.4 0.0 copy-start.1
  10.4 0.0 copy-start.2
  10.4 0.0 copy-start.3
  10.4 0.0 collective-permute-done.3.below
  10.4 0.0 collective-permute-done.4.above
  10.4 0.0 copy-done
  10.4 0.6 %span.1.operator_in = f32[320,128]{1,0:T(8,128)S(1)} custom-call(f32[8,320]{1,0:T(8,128)S(1)} %collective-permute-done.3.below, f32[8,320]{1,0:T(8,128)S(1)} %collective-permute-done.4.above, f32[248,128]{1,0:T(8,128)S(1)} %get-tuple-element.34.tables, f32[800,128]{1,0:T(8,128)S(1)} %get-tuple-element.35.own_in, f32[320,128]{1,0:T(8,128)S(1)} %get-tuple-element.38.volume_in, ...), custom_call_target="tpu_custom_call" | custom-call | flops 1000000000 | bytes 3000000 | tf_op jit(solution)/shard_map/span/pallas_call | solution.py:713
  11.1 0.0 collective-permute-done.plane
  11.1 0.0 collective-permute-done.1.gy_low
  11.1 0.0 collective-permute-done.2.gy_high
  11.1 0.2 copy-done.1
  11.3 0.0 copy-done.2
  11.3 0.0 copy-done.3
  11.4 1.6 %sweep.1 = (f32[64,320]{1,0:T(8,128)}, f32[64,384]{1,0:T(8,128)S(1)}) custom-call(f32[64,320]{1,0:T(8,128)S(1)} %bitcast.29, f32[16,320]{1,0:T(8,128)S(1)} %collective-permute-done.plane, f32[32,320]{1,0:T(8,128)S(1)} %collective-permute-done.1.gy_low, f32[32,320]{1,0:T(8,128)S(1)} %collective-permute-done.2.gy_high, f32[64,320]{1,0:T(8,128)S(1)} %bitcast.33, ...), custom_call_target="tpu_custom_call" | custom-call | flops 1000000000 | bytes 3000000 | tf_op jit(solution)/shard_map/sweep/pallas_call | solution.py:723
  13.0 13.7 %all_to_all.10 = f32[8,8,384]{2,1,0:T(8,128)S(1)} all-to-all(f32[8,8,384]{2,1,0:T(8,128)S(1)} %bitcast.32), channel_id=1, replica_groups={{0,8,16,24,32,40,48,56},{64,72,80,88,96,104,112,120},{128,136,144,152,1..., dimensions={0} | all-to-all | bytes 196608 | tf_op jit(solution)/shard_map/all_to_all | solution.py:749
  26.7 6.7 %maps.1 = (bf16[8,8,80,256]{3,2,1,0:T(8,128)(2,1)S(1)}, bf16[8,8,80,512]{3,2,1,0:T(8,128)(2,1)S(1)}, f32[8,128,128]{2,1,0:T(8,128)S(1)}, f32[8,80,128]{2,1,0:T(8...) custom-call(f32[64,384]{1,0:T(8,128)S(1)} %bitcast.26, ...), custom_call_target="tpu_custom_call" | custom-call | tf_op jit(solution)/shard_map/maps/pallas_call | solution.py:752
  33.4 4.5 %collective-permute-start.6 = (f32[80,256]{1,0:T(8,128)S(1)}, f32[80,256]{1,0:T(8,128)S(1)}, u32[]{:S(2)}, u32[]{:S(2)}) collective-permute-start(f32[80,256]{1,0:T(8,128)S(1)} %get-tuple-element.44.refs_0_), channel_id=1, source_target_pairs={{0,128},{8,136},{16,144},{24,152},{32,160},{40,168},{48,176},{56,1... | collective-permute-start | bytes 245768 | tf_op jit(solution)/shard_map/ppermute | solution.py:656
  37.8 0.4 collective-permute-start.7
  38.3 2.5 %collective-permute-start.5 = (f32[80,128]{1,0:T(8,128)S(1)}, f32[80,128]{1,0:T(8,128)S(1)}, u32[]{:S(2)}, u32[]{:S(2)}) collective-permute-start(f32[80,128]{1,0:T(8,128)S(1)} %get-tuple-element.45), channel_id=1, source_target_pairs={{0,64},{8,72},{16,80},{24,88},{32,96},{40,104},{48,112},{56,120},{... | collective-permute-start | bytes 122888 | tf_op jit(solution)/shard_map/ppermute | solution.py:656
  40.8 4.2 %fuse.1 = (f32[8,88,640]{2,1,0:T(8,128)S(1)}, f32[8,168,640]{2,1,0:T(8,128)S(1)}, f32[64,320]{1,0:T(8,128)S(1)}, bf16[320,256]{1,0:T(8,128)(2,1)S(1)}, bf16[320,256]{1,0:T(8,128)(2,1)S(1)}) custom-call(bf16[8,8,80,256]{3,2,1,0:T(8,128)(2,1)S(1)} %get-tuple-element.46.z_both, bf16[8,8,80,512]{3,2,1,0:T(8,128)(2,1)S(1)} %get-tuple-element.47.v_both, ...), custom_call_target="tpu_custom_call" | custom-call | flops 5000000000 | bytes 12000000 | tf_op jit(solution)/shard_map/fuse/pallas_call | solution.py:779
  45.0 0.0 collective-permute-done.5.refs_1_
  45.0 0.0 collective-permute-done.6.refs_2_
  45.0 1.0 %collective-permute-done.7.refs_3_ = f32[80,256]{1,0:T(8,128)S(1)} collective-permute-done((f32[80,256]{1,0:T(8,128)S(1)}, f32[80,256]{1,0:T(8,128)S(1)}, u32[]{:S(2)}, u32[]{:S(2)}) %collective-permute-start.7) | collective-permute-done | bytes 81952 | tf_op jit(solution)/shard_map/ppermute | solution.py:656
  46.0 1.8 %solve.1 = f32[64,384]{1,0:T(8,128)S(1)} custom-call(f32[80,256]{1,0:T(8,128)S(1)} %get-tuple-element.44.refs_0_, f32[80,128]{1,0:T(8,128)S(1)} %collective-permute-done.5.refs_1_, f32[80,256]{1,0:T(8,128)S(1)} %collective-permute-done.6.refs_2_, f32[80,256]{1,0:T(8,128)S(1)} %collective-permute-done.7.refs_3_, f32[8,88,640]{2,1,0:T(8,128)S(1)} %get-tuple-element.54.refs_4_, ...), custom_call_target="tpu_custom_call" | custom-call | tf_op jit(solution)/shard_map/solve/pallas_call | solution.py:794
  47.8 8.7 %all_to_all.11 = f32[8,8,384]{2,1,0:T(8,128)S(1)} all-to-all(f32[8,8,384]{2,1,0:T(8,128)S(1)} %bitcast.25), channel_id=1, replica_groups={{0,8,16,24,32,40,48,56},{64,72,80,88,96,104,112,120},{128,136,144,152,1..., dimensions={0} | all-to-all | bytes 196608 | tf_op jit(solution)/shard_map/all_to_all | solution.py:749
  56.5 0.7 %finish.1 = f32[64,320]{1,0:T(8,128)} custom-call(f32[64,384]{1,0:T(8,128)S(1)} %bitcast.31, f32[64,320]{1,0:T(8,128)S(1)} %bitcast.30), custom_call_target="tpu_custom_call" | custom-call | tf_op jit(solution)/shard_map/finish/pallas_call | solution.py:802
Async XLA Ops:
  1.6 8.8 %collective-permute-start.3 = (f32[8,320]{1,0:T(8,128)S(1)}, f32[8,320]{1,0:T(8,128)S(1)}, u32[]{:S(2)}, u32[]{:S(2)}) collective-permute-start(f32[8,320]{1,0:T(8,128)S(1)} %get-tuple-element.36), channel_id=1, source_target_pairs={{0,8},{8,16},{16,24},{24,32},{32,40},{40,48},{48,56},{56,64},{64,7... | collective-permute-start | bytes 30728 | tf_op jit(solution)/shard_map/halo/ppermute | solution.py:656
  3.1 7.3 %collective-permute-start.4 = (f32[8,320]{1,0:T(8,128)S(1)}, f32[8,320]{1,0:T(8,128)S(1)}, u32[]{:S(2)}, u32[]{:S(2)}) collective-permute-start(f32[8,320]{1,0:T(8,128)S(1)} %get-tuple-element.37), channel_id=1, source_target_pairs={{0,248},{8,0},{16,8},{24,16},{32,24},{40,32},{48,40},{56,48},{64,5... | collective-permute-start | bytes 30728 | tf_op jit(solution)/shard_map/halo/ppermute | solution.py:656
  4.0 7.1 %collective-permute-start.1 = (f32[32,320]{1,0:T(8,128)S(1)}, f32[32,320]{1,0:T(8,128)S(1)}, u32[]{:S(2)}, u32[]{:S(2)}) collective-permute-start(f32[32,320]{1,0:T(8,128)S(1)} %get-tuple-element.32), channel_id=1, source_target_pairs={{0,1},{1,2},{2,3},{3,0},{4,5},{5,6},{6,7},{7,4},{8,9},{9,10},{10,1... | collective-permute-start | bytes 122888 | tf_op jit(solution)/shard_map/halo/ppermute | solution.py:656
  5.2 5.8 %collective-permute-start.2 = (f32[32,320]{1,0:T(8,128)S(1)}, f32[32,320]{1,0:T(8,128)S(1)}, u32[]{:S(2)}, u32[]{:S(2)}) collective-permute-start(f32[32,320]{1,0:T(8,128)S(1)} %get-tuple-element.33), channel_id=1, source_target_pairs={{0,3},{1,0},{2,1},{3,2},{4,7},{5,4},{6,5},{7,6},{8,11},{9,8},{10,9... | collective-permute-start | bytes 122888 | tf_op jit(solution)/shard_map/halo/ppermute | solution.py:656
  7.2 3.8 %collective-permute-start = (f32[16,320]{1,0:T(8,128)S(1)}, f32[16,320]{1,0:T(8,128)S(1)}, u32[]{:S(2)}, u32[]{:S(2)}) collective-permute-start(f32[16,320]{1,0:T(8,128)S(1)} %get-tuple-element.31), channel_id=1, source_target_pairs={{0,4},{4,0},{1,5},{5,1},{2,6},{6,2},{3,7},{7,3},{8,12},{12,8},{9,1... | collective-permute-start | bytes 61448 | tf_op jit(solution)/shard_map/halo/ppermute | solution.py:656
  7.2 3.2 %copy-start = (bf16[3136,320]{1,0:T(8,128)(2,1)S(1)}, bf16[3136,320]{1,0:T(8,128)(2,1)}, u32[]{:S(2)}) copy-start(bf16[3136,320]{1,0:T(8,128)(2,1)} %constant.5.clone.fixed_in.fixed.refs_9_) | copy-start | bytes 6021124
  10.4 0.9 %copy-start.1 = (f32[4,2,8,320]{3,2,1,0:T(8,128)S(1)}, f32[4,2,8,320]{3,2,1,0:T(8,128)}, u32[]{:S(2)}) copy-start(f32[4,2,8,320]{3,2,1,0:T(8,128)} %param.11) | copy-start | bytes 245764
  10.4 0.9 %copy-start.2 = (f32[4,2,8,320]{3,2,1,0:T(8,128)S(1)}, f32[4,2,8,320]{3,2,1,0:T(8,128)}, u32[]{:S(2)}) copy-start(f32[4,2,8,320]{3,2,1,0:T(8,128)} %param.12) | copy-start | bytes 245764
  10.4 1.0 %copy-start.3 = (f32[4,2,8,320]{3,2,1,0:T(8,128)S(1)}, f32[4,2,8,320]{3,2,1,0:T(8,128)}, u32[]{:S(2)}) copy-start(f32[4,2,8,320]{3,2,1,0:T(8,128)} %param.13) | copy-start | bytes 245764
  33.4 11.6 %collective-permute-start.6 = (f32[80,256]{1,0:T(8,128)S(1)}, f32[80,256]{1,0:T(8,128)S(1)}, u32[]{:S(2)}, u32[]{:S(2)}) collective-permute-start(f32[80,256]{1,0:T(8,128)S(1)} %get-tuple-element.44.refs_0_), channel_id=1, source_target_pairs={{0,128},{8,136},{16,144},{24,152},{32,160},{40,168},{48,176},{56,1... | collective-permute-start | bytes 245768 | tf_op jit(solution)/shard_map/ppermute | solution.py:656
  37.8 8.2 %collective-permute-start.7 = (f32[80,256]{1,0:T(8,128)S(1)}, f32[80,256]{1,0:T(8,128)S(1)}, u32[]{:S(2)}, u32[]{:S(2)}) collective-permute-start(f32[80,256]{1,0:T(8,128)S(1)} %get-tuple-element.44.refs_0_), channel_id=1, source_target_pairs={{0,192},{8,200},{16,208},{24,216},{32,224},{40,232},{48,240},{56,2... | collective-permute-start | bytes 245768 | tf_op jit(solution)/shard_map/ppermute | solution.py:656
  38.3 6.7 %collective-permute-start.5 = (f32[80,128]{1,0:T(8,128)S(1)}, f32[80,128]{1,0:T(8,128)S(1)}, u32[]{:S(2)}, u32[]{:S(2)}) collective-permute-start(f32[80,128]{1,0:T(8,128)S(1)} %get-tuple-element.45), channel_id=1, source_target_pairs={{0,64},{8,72},{16,80},{24,88},{32,96},{40,104},{48,112},{56,120},{... | collective-permute-start | bytes 122888 | tf_op jit(solution)/shard_map/ppermute | solution.py:656
